TPU v7x, 32 devices: a whole 2x2x4 slice. The times are simulated.
32 devices in a mesh: row: 4 (over y, x), col: 8 (over z, core).
Axes of the slice: x: 2, y: 2, z: 4, core: 2. Of those that a mesh axis runs over, the one named last changes fastest.
Arguments:
- points: bfloat16 [2048, 768], P(('row', 'col')), may hold values from -8 to 8
- assign: int32 [2048], P(('row', 'col')), may hold values from 0 to 1023, as said below
Outputs:
- distance: float32 [2048, 1024], P('row', 'col')
Inputs may be any that keep to these rules, and one draw needn't show every extreme that they name: Cluster group of a point is assign // 128. Among the 64 points of one device (aligned blocks of 64) at most 16 fall in one cluster group, and in every such block some group has exactly 16.
All inputs are finite; a program needn't handle non-finite values.
Results may differ from a plain program's by a relative error of at most 0.0003.
Values may be sent and summed in bfloat16 or wider, within the bound.
No kernel may reach another device: no remote copies, remote signals or barrier semaphores. Data moves between devices by JAX's collectives and lax.ppermute only.
A program may use at most 64 MiB of HBM per device.

v0:
```python
import jax
import jax.numpy as jnp
from jax import lax
from jax.sharding import PartitionSpec as P

D = 768
CL_DEV = 128


def squares(values):
    return jnp.sum(jnp.square(values.astype(jnp.float32)), axis=1)


def kernel_tile(left_rows, left_norms, right_rows, right_norms):
    inner_prod = lax.dot_general(
        left_rows, right_rows, (((1,), (1,)), ((), ())), preferred_element_type=jnp.float32
    )
    squared = left_norms[:, None] + right_norms[None, :] - 2.0 * inner_prod
    return jnp.exp(-squared / D).astype(jnp.bfloat16)


def onehot(slot_ids, cluster_cols):
    return (slot_ids[:, None] == jnp.arange(cluster_cols, dtype=jnp.int32)[None, :]).astype(
        jnp.bfloat16
    )


def per_device(points, assign):
    own_count = points.shape[0]
    group_count = lax.axis_size("col")
    slot_cap = max(2, 2 * own_count // group_count)
    group_of = assign // CL_DEV
    local_ids = assign - group_of * CL_DEV
    member = (group_of[:, None] == jnp.arange(group_count, dtype=jnp.int32)[None, :]).astype(
        jnp.int32
    )
    before = jnp.cumsum(member, axis=0) - member
    position = jnp.sum(before * member, axis=1)
    target = group_of * slot_cap + position
    matches = target[None, :] == jnp.arange(group_count * slot_cap, dtype=jnp.int32)[:, None]
    dispatch = matches.astype(jnp.bfloat16)
    buckets = jnp.dot(dispatch, points, preferred_element_type=jnp.float32).astype(jnp.bfloat16)
    buckets = buckets.reshape(group_count, slot_cap, D)
    slot_ids = jnp.max(jnp.where(matches, local_ids[None, :], -1), axis=1).reshape(
        group_count, slot_cap
    )
    arrived, arrived_ids = (
        lax.all_to_all(buckets, "col", split_axis=0, concat_axis=0, tiled=True),
        lax.all_to_all(slot_ids, "col", split_axis=0, concat_axis=0, tiled=True),
    )
    slice_pts = arrived.reshape(-1, D)
    slice_ids = arrived_ids.reshape(-1)
    row_block = lax.all_gather(points, "col", axis=0, tiled=True)
    block_rows = row_block.shape[0]
    left_rows = jnp.concatenate([row_block, slice_pts], axis=0)
    left_norms = squares(left_rows)
    part_pts = lax.all_gather(slice_pts, "row", axis=0, tiled=True)
    part_ids = lax.all_gather(slice_ids, "row", axis=0, tiled=True)
    tile_vals = kernel_tile(left_rows, left_norms, part_pts, squares(part_pts))
    indicator = onehot(part_ids, CL_DEV)
    all_sums = jnp.dot(tile_vals, indicator, preferred_element_type=jnp.float32)
    counts = jnp.sum(indicator.astype(jnp.float32), axis=0)
    row_sums = all_sums[:block_rows]
    self_rows = all_sums[block_rows:]
    partial_self = jnp.sum(onehot(slice_ids, CL_DEV).astype(jnp.float32) * self_rows, axis=0)
    self_total = lax.psum(partial_self, "row")
    sizes_floor = jnp.maximum(counts, 1.0)
    return (
        1.0
        - 2.0 * row_sums / sizes_floor[None, :]
        + self_total[None, :] / (sizes_floor * sizes_floor)[None, :]
    )


def solution(mesh):
    return jax.shard_map(
        per_device,
        mesh=mesh,
        in_specs=(P(("row", "col"), None), P(("row", "col"))),
        out_specs=P("row", "col"),
        check_vma=False,
    )
```

profile of v0, /device:TPU:0, one launch (start us, length us, event | category | flops | bytes accessed | tf_op | source)
XLA Modules:
  0.0 68.8 jit_solution(6959925299847743621)
XLA Ops:
  0.0 0.0 copy-start
  0.0 0.7 %multiply_subtract_fusion = (s32[64]{0:T(128)S(1)}, s32[64]{0:T(128)S(1)}) fusion(s32[64]{0:T(128)} %param.3), kind=kLoop, calls=%fused_computation.38 | loop fusion | flops 1088 | bytes 768 | tf_op jit(solution)/shard_map/sub | solution.py:33
  0.7 0.1 fusion.17
  0.8 0.1 reduce_window_sum.11
  0.9 0.2 select_reduce_fusion.1
  1.1 0.1 select_reduce_fusion
  1.2 0.7 all_to_all.10
  1.9 6.3 %all-to-all-start.1 = ((s32[8,1,16]{2,1,0:T(1,128)}), s32[8,1,16]{2,1,0:T(1,128)S(1)}, u32[]{:S(2)}, u32[]{:S(2)}) async-start(s32[8,1,16]{2,1,0:T(1,128)} %bitcast.2), calls=%async_computation.1 | async-start | bytes 8192 | tf_op jit(solution)/shard_map/all_to_all | solution.py:49
  8.2 1.9 %convolution_convert_fusion = bf16[128,768]{1,0:T(8,128)(2,1)} fusion(bf16[64,768]{1,0:T(8,128)(2,1)} %param.2, s32[64]{0:T(128)S(1)} %multiply_add_fusion), kind=kOutput, calls=%fused_computation.9 | convolution fusion | flops 12689408 | bytes 295168 | tf_op jit(solution)/shard_map/dot_general | solution.py:42
  10.1 3.7 %all-to-all-done.1 = s32[8,1,16]{2,1,0:T(1,128)S(1)} async-done(((s32[8,1,16]{2,1,0:T(1,128)}), s32[8,1,16]{2,1,0:T(1,128)S(1)}, u32[]{:S(2)}, u32[]{:S(2)}) %all-to-all-start.1) | async-done | bytes 544 | tf_op jit(solution)/shard_map/all_to_all | solution.py:49
  13.7 3.4 %all-to-all-start = ((bf16[8,16,768]{2,1,0:T(8,128)(2,1)}), bf16[8,16,768]{2,1,0:T(8,128)(2,1)S(1)}, u32[]{:S(2)}, u32[]{:S(2)}) async-start(bf16[8,16,768]{2,1,0:T(8,128)(2,1)} %bitcast), calls=%async_computation | async-start | bytes 393216 | tf_op jit(solution)/shard_map/all_to_all | solution.py:48
  17.1 0.0 copy-done
  17.1 18.8 %all_gather.9 = bf16[512,768]{1,0:T(8,128)(2,1)S(1)} all-gather(bf16[64,768]{1,0:T(8,128)(2,1)S(1)} %copy-done), channel_id=1, replica_groups=mesh['row'=4,'col'=8] {'col'}, dimensions={0}, use_global_device_ids=true | all-gather | bytes 884736 | tf_op jit(solution)/shard_map/all_gather | solution.py:53
  35.9 0.1 reshape.29
  36.0 0.6 broadcast.31
  36.6 0.7 %reduce.5 = s32[8,16]{1,0:T(8,128)S(1)} reduce(s32[8,1,16]{2,1,0:T(1,128)S(1)} %all-to-all-done.1, s32[]{:T(128)} %broadcast.31), dimensions={1}, to_apply=%all_to_all.11.reduce_sub_computation.5 | reduce | bytes 1028 | tf_op jit(solution)/shard_map/all_to_all | solution.py:49
  37.3 0.1 reshape.30
  37.4 7.9 %all-gather = s32[4,1,128]{2,1,0:T(1,128)S(1)} all-gather(s32[1,1,128]{2,1,0:T(1,128)S(1)} %reshape.30), channel_id=1, replica_groups=mesh['row'=4,'col'=8] {'row'}, dimensions={0}, use_global_device_ids=true | all-gather | bytes 2560 | tf_op jit(solution)/shard_map/all_gather | solution.py:58
  45.3 0.1 convert_reduce_fusion
  45.5 0.0 all-to-all-done
  45.5 12.0 %all_gather.10 = bf16[512,768]{1,0:T(8,128)(2,1)S(1)} all-gather(bf16[128,768]{1,0:T(8,128)(2,1)S(1)} %bitcast.7), channel_id=1, replica_groups=mesh['row'=4,'col'=8] {'row'}, dimensions={0}, use_global_device_ids=true | all-gather | bytes 983040 | tf_op jit(solution)/shard_map/all_gather | solution.py:57
  57.5 0.2 multiply_reduce_fusion.1
  57.7 0.3 multiply_reduce_fusion
  58.0 1.0 %fusion.5 = f32[640,128]{1,0:T(8,128)S(1)} fusion(bf16[512,768]{1,0:T(8,128)(2,1)S(1)} %all_gather.10, f32[512]{0:T(512)S(1)} %multiply_reduce_fusion.1, f32[640]{0:T(1024)S(1)} %multiply_reduce_fusion, bf16[128,768]{1,0:T(8,128)(2,1)S(1)} %bitcast.9, bf16[512,768]{1,0:T(8,128)(2,1)S(1)} %all_gather.9, s32[512]{0:T(512)S(1)} %bitcast.12), kind=kOutput, calls=%fused_computation.8 | convolution fusion | flops 591200256 | bytes 2103808 | tf_op jit(solution)/shard_map/dot_general | solution.py:61
  59.0 0.1 fusion.15
  59.1 8.9 %psum.7 = f32[128]{0:T(128)S(1)} all-reduce(f32[128]{0:T(128)S(1)} %fusion.15), channel_id=1, replica_groups=mesh['row'=4,'col'=8] {'row'}, use_global_device_ids=true, to_apply=%region_7.8 | all-reduce | flops 128 | bytes 1024 | tf_op jit(solution)/shard_map/psum | solution.py:66
  68.1 0.7 %fusion.12 = f32[512,128]{1,0:T(8,128)} fusion(f32[640,128]{1,0:T(8,128)S(1)} %fusion.5, f32[128]{0:T(128)S(1)} %get-tuple-element.8, f32[128]{0:T(128)S(1)} %get-tuple-element.7), kind=kLoop, calls=%fused_computation.18 | loop fusion | flops 262144 | bytes 525312 | tf_op jit(solution)/shard_map/add | solution.py:69
  (2 shorter events, 0.0 us)
Async XLA Ops:
  0.0 17.1 %copy-start = (bf16[64,768]{1,0:T(8,128)(2,1)S(1)}, bf16[64,768]{1,0:T(8,128)(2,1)}, u32[]{:S(2)}) copy-start(bf16[64,768]{1,0:T(8,128)(2,1)} %param.2) | copy-start | bytes 294916
  1.9 11.9 %all-to-all-start.1 = ((s32[8,1,16]{2,1,0:T(1,128)}), s32[8,1,16]{2,1,0:T(1,128)S(1)}, u32[]{:S(2)}, u32[]{:S(2)}) async-start(s32[8,1,16]{2,1,0:T(1,128)} %bitcast.2), calls=%async_computation.1 | async-start | bytes 8192 | tf_op jit(solution)/shard_map/all_to_all | solution.py:49
  13.7 31.7 %all-to-all-start = ((bf16[8,16,768]{2,1,0:T(8,128)(2,1)}), bf16[8,16,768]{2,1,0:T(8,128)(2,1)S(1)}, u32[]{:S(2)}, u32[]{:S(2)}) async-start(bf16[8,16,768]{2,1,0:T(8,128)(2,1)} %bitcast), calls=%async_computation | async-start | bytes 393216 | tf_op jit(solution)/shard_map/all_to_all | solution.py:48
where the time goes:
time: 69.2 us; the launch traced here: 68.8 us
  blocking collectives  47.7 us (69%)
  starting transfers between devices  9.72 us (14%)
  waiting for transfers between devices  3.66 us (5%)
  other arithmetic  3.36 us (5%)
  matrix products  2.91 us (4%)
  local copies, waits for them, and re-layouts  1.43 us (2%)
    all_gather x1, blocking collectives, per_device(): row_block = lax.all_gather(points, 'col', axis=0, tiled=True)  18.8 us
    all_gather x1, blocking collectives, per_device(): part_pts = lax.all_gather(slice_pts, 'row', axis=0, tiled=True)  12 us
    psum x1, blocking collectives, per_device(): self_total = lax.psum(partial_self, 'row')  8.92 us
    all_gather x1, blocking collectives, per_device(): part_ids = lax.all_gather(slice_ids, 'row', axis=0, tiled=True)  7.92 us
    all_to_all x1, starting transfers between devices, per_device(): lax.all_to_all(slot_ids, 'col', split_axis=0, concat_axis=0, tiled=True)  6.33 us
    all_to_all x1, waiting for transfers between devices, per_device(): lax.all_to_all(slot_ids, 'col', split_axis=0, concat_axis=0, tiled=True)  3.66 us
    all_to_all x1, starting transfers between devices, per_device(): lax.all_to_all(buckets, 'col', split_axis=0, concat_axis=0, tiled=True)  3.39 us
    dot_general x1, matrix products, per_device(): jnp.dot(dispatch, points, preferred_element_type=jnp.float32)  1.9 us
  transfers between devices with their start and end apart: 2, of which 1 were waited for; matrix products, arithmetic and copies ran while one was open for 5% of the time, Pallas kernels for 0%

commit v1 on v0

v1 whole, which is shorter than its diff:
```python
import functools

import jax
import jax.numpy as jnp
from jax import lax
from jax.experimental import pallas as pl
from jax.experimental.pallas import tpu as pltpu
from jax.sharding import PartitionSpec as P

CL_DEV = 128
ID_ROWS = 8
NT = (((1,), (1,)), ((), ()))
NN = (((1,), (0,)), ((), ()))


def dot(left, right, dims):
    return lax.dot_general(left, right, dims, preferred_element_type=jnp.float32)


def bucket_kernel(chips, slots, me_ref, assign_ref, points_ref, *payload_refs):
    own_count, width = points_ref.shape
    groups = 2 * chips
    total = groups * slots
    assign = assign_ref[...]
    group_of = assign // CL_DEV
    local_ids = assign - group_of * CL_DEV
    relative = group_of ^ me_ref[0]
    member = (
        lax.broadcasted_iota(jnp.int32, (groups, own_count), 0) == relative
    ).astype(jnp.float32)
    earlier = (
        lax.broadcasted_iota(jnp.int32, (own_count, own_count), 0)
        < lax.broadcasted_iota(jnp.int32, (own_count, own_count), 1)
    ).astype(jnp.bfloat16)
    rank = dot(member.astype(jnp.bfloat16), earlier, NN)
    position = jnp.sum(rank * member, axis=0, keepdims=True).astype(jnp.int32)
    half = chips * slots
    target = (relative & 1) * half + (relative >> 1) * slots + position
    dispatch = (
        lax.broadcasted_iota(jnp.int32, (total, own_count), 0) == target
    ).astype(jnp.bfloat16)
    rows = dot(dispatch, points_ref[...], NN).astype(jnp.bfloat16)
    ids = dot(
        jnp.broadcast_to(local_ids + 1, (ID_ROWS, own_count)).astype(jnp.bfloat16), dispatch, NT
    )
    lane = lax.broadcasted_iota(jnp.int32, (ID_ROWS, total), 1)
    owner = (lane % half) // slots
    for q, payload_ref in enumerate(payload_refs):
        for h in range(2):
            start = h * half + q * slots
            payload_ref[h * slots : (h + 1) * slots, :] = rows[start : start + slots]
        payload_ref[2 * slots :, :] = jnp.zeros((ID_ROWS, width), jnp.bfloat16)
        payload_ref[2 * slots :, :total] = jnp.where(owner == q, ids, 0.0).astype(jnp.bfloat16)


def merge_kernel(slots, *refs):
    *payload_refs, out_ref = refs
    half = len(payload_refs) * slots
    ids = jnp.zeros((ID_ROWS, out_ref.shape[1]), jnp.float32)
    for q, payload_ref in enumerate(payload_refs):
        for h in range(2):
            start = h * half + q * slots
            out_ref[start : start + slots, :] = payload_ref[h * slots : (h + 1) * slots, :]
        ids += payload_ref[2 * slots :, :].astype(jnp.float32)
    out_ref[2 * half :, :] = ids.astype(jnp.bfloat16)


def column_norms(rows):
    values = rows.astype(jnp.float32)
    return jnp.sum(values * values, axis=1, keepdims=True)


def row_of(column):
    return jnp.transpose(jnp.broadcast_to(column, (column.shape[0], 128)))[:1]


def distance_kernel(half, blocks, sets, chunk, me_ref, *refs):
    block_refs, set_refs = refs[:blocks], refs[blocks : blocks + sets]
    out_ref, rows_ref, slots_ref, norms_ref, hot_ref = refs[blocks + sets :]
    me = me_ref[0]
    own_count, width = block_refs[0].shape
    scale = 1.0 / width
    total = sets * half
    for s, set_ref in enumerate(set_refs):
        start = 0 if s < sets // 2 else half
        slot_rows = set_ref[start : start + half, :]
        slots_ref[s * half : (s + 1) * half, :] = slot_rows
        norms_ref[:, s * half : (s + 1) * half] = jnp.broadcast_to(
            row_of(column_norms(slot_rows)), (norms_ref.shape[0], half)
        )
        ids = set_ref[2 * half :, start : start + half].astype(jnp.float32)[:1]
        hot_ref[:, s * half : (s + 1) * half] = (
            lax.broadcasted_iota(jnp.int32, (CL_DEV, half), 0) + 1 == ids.astype(jnp.int32)
        ).astype(jnp.bfloat16)
    for b, block_ref in enumerate(block_refs):
        place = (me ^ (2 * b)) if b < blocks // 2 else (me ^ (2 * (b - blocks // 2)) ^ 1)
        rows_ref[pl.ds(pl.multiple_of(place * own_count, own_count), own_count), :] = block_ref[...]
    hot = hot_ref[...]
    slot_norms = norms_ref[:1, :]

    def kern(rows):
        inner = dot(rows, slots_ref[...], NT)
        squared = column_norms(rows) + slot_norms - 2.0 * inner
        return jnp.exp(squared * -scale).astype(jnp.bfloat16)

    ones = jnp.ones((8, total), jnp.bfloat16)
    sizes = jnp.maximum(dot(ones, hot, NT)[:1], 1.0)
    self_column = jnp.zeros((CL_DEV, 1), jnp.float32)
    for start in range(0, total, chunk):
        part = kern(slots_ref[start : start + chunk, :])
        weights = hot_ref[:, start : start + chunk]
        sums = dot(weights, part, NN)
        self_column += jnp.sum(sums * hot.astype(jnp.float32), axis=1, keepdims=True)
    self_total = row_of(self_column)
    offset = 1.0 + self_total / (sizes * sizes)
    factor = 2.0 / sizes
    for start in range(0, rows_ref.shape[0], chunk):
        row_sums = dot(kern(rows_ref[start : start + chunk, :]), hot, NT)
        out_ref[start : start + chunk, :] = offset - row_sums * factor


VMEM = pl.BlockSpec(memory_space=pltpu.VMEM)
SMEM = pl.BlockSpec(memory_space=pltpu.SMEM)


def per_device(points, assign):
    own_count, width = points.shape
    group_count, row_count = lax.axis_size("col"), lax.axis_size("row")
    chips = group_count // 2
    slots = max(2, 2 * own_count // group_count)
    half = chips * slots
    me = lax.axis_index("col").astype(jnp.int32).reshape(1)

    def over_col(values, bits):
        return lax.ppermute(values, "col", [(i, i ^ bits) for i in range(group_count)])

    def over_row(values, step):
        bit_count = row_count.bit_length() - 1
        pairs = []
        for r in range(row_count):
            for c in range(group_count):
                bit = step if c % 2 == 0 else bit_count - 1 - step
                pairs.append((r * group_count + c, (r ^ (1 << bit)) * group_count + c))
        return lax.ppermute(values, ("row", "col"), pairs)

    payloads = pl.pallas_call(
        functools.partial(bucket_kernel, chips, slots),
        out_shape=[jax.ShapeDtypeStruct((2 * slots + ID_ROWS, width), jnp.bfloat16)] * chips,
        in_specs=[SMEM, VMEM, VMEM],
        out_specs=[VMEM] * chips,
    )(me, assign.reshape(1, own_count), points)
    arrived = [payloads[0]] + [over_col(payloads[q], 2 * q) for q in range(1, chips)]
    blocks = [points] + [over_col(points, 2 * q) for q in range(1, chips)]
    sets = [
        pl.pallas_call(
            functools.partial(merge_kernel, slots),
            out_shape=jax.ShapeDtypeStruct((2 * half + ID_ROWS, width), jnp.bfloat16),
            in_specs=[VMEM] * chips,
            out_specs=VMEM,
        )(*arrived)
    ]
    step = 0
    while len(sets) < row_count:
        sets += [over_row(one, step) for one in sets]
        step += 1
    blocks += [over_col(one, 1) for one in blocks]
    sets += [over_col(one, 1) for one in sets]
    rows, total = len(blocks) * own_count, len(sets) * half
    chunk = min(256, rows)
    return pl.pallas_call(
        functools.partial(distance_kernel, half, len(blocks), len(sets), chunk),
        out_shape=jax.ShapeDtypeStruct((rows, CL_DEV), jnp.float32),
        in_specs=[SMEM] + [VMEM] * (len(blocks) + len(sets)),
        out_specs=VMEM,
        scratch_shapes=[
            pltpu.VMEM((rows, width), jnp.bfloat16),
            pltpu.VMEM((total, width), jnp.bfloat16),
            pltpu.VMEM((8, total), jnp.float32),
            pltpu.VMEM((CL_DEV, total), jnp.bfloat16),
        ],
        compiler_params=pltpu.CompilerParams(vmem_limit_bytes=32 * 1024 * 1024),
    )(me, *blocks, *sets)


def solution(mesh):
    return jax.shard_map(
        per_device,
        mesh=mesh,
        in_specs=(P(("row", "col"), None), P(("row", "col"))),
        out_specs=P("row", "col"),
        check_vma=False,
    )
```

time: 69.2 us -> 43 us (0.62)
  blocking collectives: 47.7 us -> 0 us
  waiting for transfers between devices: 3.66 us -> 20.5 us
  Pallas kernels: 0 us -> 6.36 us
  starting transfers between devices: 9.72 us -> 14.4 us
  other arithmetic: 3.36 us -> 0 us
  matrix products: 2.91 us -> 0 us
    all_gather x3 -> x0, blocking collectives: 38.7 us -> none  [the longest x1 18.8 us: per_device(): row_block = lax.all_gather(points, 'col', axis=0, tiled=True)]
    ppermute x0 -> x17, waiting for transfers between devices: none -> 20.5 us  [the longest x14 15.7 us: over_col(): lax.ppermute(values, 'col', [(i, i ^ bits) for i in range(group_count)])]
    ppermute x0 -> x17, starting transfers between devices: none -> 14.4 us  [the longest x14 11.4 us: over_col(): lax.ppermute(values, 'col', [(i, i ^ bits) for i in range(group_count)])]
    all_to_all x2 -> x0, starting transfers between devices: 9.72 us -> none  [the longest x1 6.33 us: per_device(): lax.all_to_all(slot_ids, 'col', split_axis=0, concat_axis=0, tiled=True)]
    psum x1 -> x0, blocking collectives: 8.92 us -> none  [per_device(): self_total = lax.psum(partial_self, 'row')]
    pallas_call x0 -> x3, Pallas kernels: none -> 6.36 us  [the longest x1 2.8 us: per_device(): pl.pallas_call(functools.partial(distance_kernel, half, len(blocks), len(...]
    all_to_all x2 -> x0, waiting for transfers between devices: 3.66 us -> none  [the longest x1 3.66 us: per_device(): lax.all_to_all(slot_ids, 'col', split_axis=0, concat_axis=0, tiled=True)]
    dot_general x2 -> x0, matrix products: 2.91 us -> none  [the longest x1 1.9 us: per_device(): jnp.dot(dispatch, points, preferred_element_type=jnp.float32)]
  transfers between devices with their start and end apart: 2 -> 17, of which waited for: 1 -> 7; matrix products, arithmetic and copies ran while one was open for 5% -> 0% of each run, Pallas kernels for 0% -> 0%
where the time goes in v1:
time: 43 us; the launch traced here: 42.8 us
  waiting for transfers between devices  20.5 us (48%)
  starting transfers between devices  14.4 us (33%)
  Pallas kernels  6.36 us (15%)
  local copies, waits for them, and re-layouts  1.55 us (4%)
    ppermute x14, waiting for transfers between devices, over_col(): lax.ppermute(values, 'col', [(i, i ^ bits) for i in range(group_count)])  15.7 us
    ppermute x14, starting transfers between devices, over_col(): lax.ppermute(values, 'col', [(i, i ^ bits) for i in range(group_count)])  11.4 us
    ppermute x3, waiting for transfers between devices, over_row(): return lax.ppermute(values, ('row', 'col'), pairs)  4.74 us
    ppermute x3, starting transfers between devices, over_row(): return lax.ppermute(values, ('row', 'col'), pairs)  3.04 us
    pallas_call x1, Pallas kernels, per_device(): pl.pallas_call(functools.partial(distance_kernel, half, len(blocks), len(...  2.8 us
    pallas_call x1, Pallas kernels, per_device(): pl.pallas_call(functools.partial(bucket_kernel, chips, slots), out_shape=...  1.91 us
    pallas_call x1, Pallas kernels, per_device(): pl.pallas_call(functools.partial(merge_kernel, slots), out_shape=jax.Shap...  1.65 us
    unnamed x10, local copies, waits for them, and re-layouts  1.55 us
  transfers between devices with their start and end apart: 17, of which 7 were waited for; matrix products, arithmetic and copies ran while one was open for 0% of the time, Pallas kernels for 0%

profile of v1, /device:TPU:0, one launch (start us, length us, event | category | flops | bytes accessed | tf_op | source)
XLA Modules:
  0.0 42.8 jit_solution(10909342417716732102)
XLA Ops:
  0.0 1.9 %shard_map.28 = (bf16[40,768]{1,0:T(8,128)(2,1)}, bf16[40,768]{1,0:T(8,128)(2,1)}, bf16[40,768]{1,0:T(8,128)(2,1)}, bf16[40,768]{1,0:T(8,128)(2,1)}) custom-call(s32[1]{0:T(128)} %bitcast.me_ref, s32[1,64]{1,0:T(1,128)} %bitcast.2, bf16[64,768]{1,0:T(8,128)(2,1)} %refs_0_.1), custom_call_target="tpu_custom_call" | custom-call | tf_op jit(solution)/shard_map/pallas_call | solution.py:146
  1.9 3.0 %collective-permute-start.7 = (bf16[40,768]{1,0:T(8,128)(2,1)}, bf16[40,768]{1,0:T(8,128)(2,1)S(1)}, u32[]{:S(2)}, u32[]{:S(2)}) collective-permute-start(bf16[40,768]{1,0:T(8,128)(2,1)} %get-tuple-element.10), channel_id=1, source_target_pairs={{0,2},{1,3},{2,0},{3,1},{4,6},{5,7},{6,4},{7,5},{8,10},{9,11},{10,... | collective-permute-start | bytes 184328 | tf_op jit(solution)/shard_map/ppermute | solution.py:135
  4.9 2.6 %collective-permute-start.8 = (bf16[40,768]{1,0:T(8,128)(2,1)}, bf16[40,768]{1,0:T(8,128)(2,1)S(1)}, u32[]{:S(2)}, u32[]{:S(2)}) collective-permute-start(bf16[40,768]{1,0:T(8,128)(2,1)} %get-tuple-element.11), channel_id=1, source_target_pairs={{0,4},{1,5},{2,6},{3,7},{4,0},{5,1},{6,2},{7,3},{8,12},{9,13},{10,... | collective-permute-start | bytes 184328 | tf_op jit(solution)/shard_map/ppermute | solution.py:135
  7.5 0.0 collective-permute-start.9
  7.5 0.0 collective-permute-done.7.refs_1_
  7.5 0.0 copy-start.2
  7.5 4.0 %collective-permute-done.8.refs_2_ = bf16[40,768]{1,0:T(8,128)(2,1)S(1)} collective-permute-done((bf16[40,768]{1,0:T(8,128)(2,1)}, bf16[40,768]{1,0:T(8,128)(2,1)S(1)}, u32[]{:S(2)}, u32[]{:S(2)}) %collective-permute-start.8) | collective-permute-done | bytes 61472 | tf_op jit(solution)/shard_map/ppermute | solution.py:135
  11.5 0.0 copy-start.3
  11.5 2.3 %collective-permute-done.9.refs_3_ = bf16[40,768]{1,0:T(8,128)(2,1)S(1)} collective-permute-done((bf16[40,768]{1,0:T(8,128)(2,1)}, bf16[40,768]{1,0:T(8,128)(2,1)S(1)}, u32[]{:S(2)}, u32[]{:S(2)}) %collective-permute-start.9) | collective-permute-done | bytes 61472 | tf_op jit(solution)/shard_map/ppermute | solution.py:135
  13.8 0.0 copy-start.4
  13.8 0.0 copy-done.2
  13.8 0.0 copy-done.3
  13.8 0.6 %copy-done.4 = bf16[40,768]{1,0:T(8,128)(2,1)} copy-done((bf16[40,768]{1,0:T(8,128)(2,1)}, bf16[40,768]{1,0:T(8,128)(2,1)S(1)}, u32[]{:S(2)}) %copy-start.4) | copy-done | bytes 61464
  14.4 0.0 copy-start.1
  14.4 1.7 %shard_map.29.refs_8_ = bf16[136,768]{1,0:T(8,128)(2,1)} custom-call(bf16[40,768]{1,0:T(8,128)(2,1)} %get-tuple-element.9.refs_0_, bf16[40,768]{1,0:T(8,128)(2,1)} %copy-done.2, bf16[40,768]{1,0:T(8,128)(2,1)} %copy-done.3, bf16[40,768]{1,0:T(8,128)(2,1)} %copy-done.4), custom_call_target="tpu_custom_call" | custom-call | tf_op jit(solution)/shard_map/pallas_call | solution.py:155
  16.0 1.5 %collective-permute-start.10 = (bf16[136,768]{1,0:T(8,128)(2,1)}, bf16[136,768]{1,0:T(8,128)(2,1)S(1)}, u32[]{:S(2)}, u32[]{:S(2)}) collective-permute-start(bf16[136,768]{1,0:T(8,128)(2,1)} %shard_map.29.refs_8_), channel_id=1, source_target_pairs={{0,8},{1,17},{2,10},{3,19},{4,12},{5,21},{6,14},{7,23},{8,0},{9,25... | collective-permute-start | bytes 626696 | tf_op jit(solution)/shard_map/ppermute | solution.py:144
  17.5 1.5 %collective-permute-start.11 = (bf16[136,768]{1,0:T(8,128)(2,1)}, bf16[136,768]{1,0:T(8,128)(2,1)S(1)}, u32[]{:S(2)}, u32[]{:S(2)}) collective-permute-start(bf16[136,768]{1,0:T(8,128)(2,1)} %shard_map.29.refs_8_), channel_id=1, source_target_pairs={{0,16},{1,9},{2,18},{3,11},{4,20},{5,13},{6,22},{7,15},{8,24},{9,1... | collective-permute-start | bytes 626696 | tf_op jit(solution)/shard_map/ppermute | solution.py:144
  19.0 4.7 %collective-permute-done.10.refs_9_ = bf16[136,768]{1,0:T(8,128)(2,1)S(1)} collective-permute-done((bf16[136,768]{1,0:T(8,128)(2,1)}, bf16[136,768]{1,0:T(8,128)(2,1)S(1)}, u32[]{:S(2)}, u32[]{:S(2)}) %collective-permute-start.10) | collective-permute-done | bytes 208928 | tf_op jit(solution)/shard_map/ppermute | solution.py:144
  23.8 0.0 collective-permute-start.12
  23.8 0.0 copy-done.1
  23.8 0.0 collective-permute-start.3
  23.8 2.2 %collective-permute-start.2 = (bf16[64,768]{1,0:T(8,128)(2,1)S(1)}, bf16[64,768]{1,0:T(8,128)(2,1)S(1)}, u32[]{:S(2)}, u32[]{:S(2)}) collective-permute-start(bf16[64,768]{1,0:T(8,128)(2,1)S(1)} %copy-done.1), channel_id=1, source_target_pairs={{0,6},{1,7},{2,4},{3,5},{4,2},{5,3},{6,0},{7,1},{8,14},{9,15},{10,... | collective-permute-start | bytes 294920 | tf_op jit(solution)/shard_map/ppermute | solution.py:135
  26.0 0.0 collective-permute-start.1
  26.0 0.0 collective-permute-done.3.refs_4_
  26.0 2.2 %collective-permute-start = (bf16[64,768]{1,0:T(8,128)(2,1)S(1)}, bf16[64,768]{1,0:T(8,128)(2,1)S(1)}, u32[]{:S(2)}, u32[]{:S(2)}) collective-permute-start(bf16[64,768]{1,0:T(8,128)(2,1)S(1)} %copy-done.1), channel_id=1, source_target_pairs={{0,2},{1,3},{2,0},{3,1},{4,6},{5,7},{6,4},{7,5},{8,10},{9,11},{10,... | collective-permute-start | bytes 294920 | tf_op jit(solution)/shard_map/ppermute | solution.py:135
  28.3 3.1 %collective-permute-done.2.refs_3_ = bf16[64,768]{1,0:T(8,128)(2,1)S(1)} collective-permute-done((bf16[64,768]{1,0:T(8,128)(2,1)S(1)}, bf16[64,768]{1,0:T(8,128)(2,1)S(1)}, u32[]{:S(2)}, u32[]{:S(2)}) %collective-permute-start.2) | collective-permute-done | bytes 98336 | tf_op jit(solution)/shard_map/ppermute | solution.py:135
  31.4 0.0 collective-permute-start.6
  31.4 3.9 %collective-permute-done.1.refs_2_ = bf16[64,768]{1,0:T(8,128)(2,1)S(1)} collective-permute-done((bf16[64,768]{1,0:T(8,128)(2,1)S(1)}, bf16[64,768]{1,0:T(8,128)(2,1)S(1)}, u32[]{:S(2)}, u32[]{:S(2)}) %collective-permute-start.1) | collective-permute-done | bytes 98336 | tf_op jit(solution)/shard_map/ppermute | solution.py:135
  35.3 0.0 collective-permute-start.13
  35.3 0.0 collective-permute-done.refs_1_
  35.3 0.5 %collective-permute-start.14 = (bf16[136,768]{1,0:T(8,128)(2,1)S(1)}, bf16[136,768]{1,0:T(8,128)(2,1)S(1)}, u32[]{:S(2)}, u32[]{:S(2)}) collective-permute-start(bf16[136,768]{1,0:T(8,128)(2,1)S(1)} %collective-permute-done.10.refs_9_), channel_id=1, source_target_pairs={{0,1},{1,0},{2,3},{3,2},{4,5},{5,4},{6,7},{7,6},{8,9},{9,8},{10,11... | collective-permute-start | bytes 626696 | tf_op jit(solution)/shard_map/ppermute | solution.py:135
  35.8 0.0 collective-permute-done.11.refs_10_
  35.8 0.1 collective-permute-start.15
  35.9 0.0 collective-permute-done.12.refs_11_
  35.9 0.4 %collective-permute-start.16 = (bf16[136,768]{1,0:T(8,128)(2,1)S(1)}, bf16[136,768]{1,0:T(8,128)(2,1)S(1)}, u32[]{:S(2)}, u32[]{:S(2)}) collective-permute-start(bf16[136,768]{1,0:T(8,128)(2,1)S(1)} %collective-permute-done.12.refs_11_), channel_id=1, source_target_pairs={{0,1},{1,0},{2,3},{3,2},{4,5},{5,4},{6,7},{7,6},{8,9},{9,8},{10,11... | collective-permute-start | bytes 626696 | tf_op jit(solution)/shard_map/ppermute | solution.py:135
  36.3 0.0 collective-permute-done.6.refs_7_
  36.3 0.1 collective-permute-start.5
  36.4 1.4 %collective-permute-done.5.refs_6_ = bf16[64,768]{1,0:T(8,128)(2,1)S(1)} collective-permute-done((bf16[64,768]{1,0:T(8,128)(2,1)S(1)}, bf16[64,768]{1,0:T(8,128)(2,1)S(1)}, u32[]{:S(2)}, u32[]{:S(2)}) %collective-permute-start.5) | collective-permute-done | bytes 98336 | tf_op jit(solution)/shard_map/ppermute | solution.py:135
  37.8 0.2 collective-permute-start.4
  38.0 1.1 %collective-permute-done.4.refs_5_ = bf16[64,768]{1,0:T(8,128)(2,1)S(1)} collective-permute-done((bf16[64,768]{1,0:T(8,128)(2,1)S(1)}, bf16[64,768]{1,0:T(8,128)(2,1)S(1)}, u32[]{:S(2)}, u32[]{:S(2)}) %collective-permute-start.4) | collective-permute-done | bytes 98336 | tf_op jit(solution)/shard_map/ppermute | solution.py:135
  39.1 0.0 collective-permute-done.13.refs_12_
  39.1 0.0 collective-permute-done.15.refs_14_
  39.1 0.0 collective-permute-done.14.refs_13_
  39.1 0.0 collective-permute-done.16.refs_15_
  39.1 0.0 copy-start
  39.1 0.9 %copy-done = bf16[136,768]{1,0:T(8,128)(2,1)S(1)} copy-done((bf16[136,768]{1,0:T(8,128)(2,1)S(1)}, bf16[136,768]{1,0:T(8,128)(2,1)}, u32[]{:S(2)}) %copy-start) | copy-done | bytes 208920
  40.0 2.8 %shard_map.30 = f32[512,128]{1,0:T(8,128)} custom-call(s32[1]{0:T(128)} %bitcast.me_ref, bf16[64,768]{1,0:T(8,128)(2,1)S(1)} %copy-done.1, bf16[64,768]{1,0:T(8,128)(2,1)S(1)} %collective-permute-done.refs_1_, bf16[64,768]{1,0:T(8,128)(2,1)S(1)} %collective-permute-done.1.refs_2_, bf16[64,768]{1,0:T(8,128)(2,1)S(1)} %collective-permute-done.2.refs_3_, ...), custom_call_target="tpu_custom_call" | custom-call | tf_op jit(solution)/shard_map/pallas_call | solution.py:170
Async XLA Ops:
  1.9 5.6 %collective-permute-start.7 = (bf16[40,768]{1,0:T(8,128)(2,1)}, bf16[40,768]{1,0:T(8,128)(2,1)S(1)}, u32[]{:S(2)}, u32[]{:S(2)}) collective-permute-start(bf16[40,768]{1,0:T(8,128)(2,1)} %get-tuple-element.10), channel_id=1, source_target_pairs={{0,2},{1,3},{2,0},{3,1},{4,6},{5,7},{6,4},{7,5},{8,10},{9,11},{10,... | collective-permute-start | bytes 184328 | tf_op jit(solution)/shard_map/ppermute | solution.py:135
  4.9 6.6 %collective-permute-start.8 = (bf16[40,768]{1,0:T(8,128)(2,1)}, bf16[40,768]{1,0:T(8,128)(2,1)S(1)}, u32[]{:S(2)}, u32[]{:S(2)}) collective-permute-start(bf16[40,768]{1,0:T(8,128)(2,1)} %get-tuple-element.11), channel_id=1, source_target_pairs={{0,4},{1,5},{2,6},{3,7},{4,0},{5,1},{6,2},{7,3},{8,12},{9,13},{10,... | collective-permute-start | bytes 184328 | tf_op jit(solution)/shard_map/ppermute | solution.py:135
  7.5 6.2 %collective-permute-start.9 = (bf16[40,768]{1,0:T(8,128)(2,1)}, bf16[40,768]{1,0:T(8,128)(2,1)S(1)}, u32[]{:S(2)}, u32[]{:S(2)}) collective-permute-start(bf16[40,768]{1,0:T(8,128)(2,1)} %get-tuple-element.12), channel_id=1, source_target_pairs={{0,6},{1,7},{2,4},{3,5},{4,2},{5,3},{6,0},{7,1},{8,14},{9,15},{10,... | collective-permute-start | bytes 184328 | tf_op jit(solution)/shard_map/ppermute | solution.py:135
  7.5 6.2 %copy-start.2 = (bf16[40,768]{1,0:T(8,128)(2,1)}, bf16[40,768]{1,0:T(8,128)(2,1)S(1)}, u32[]{:S(2)}) copy-start(bf16[40,768]{1,0:T(8,128)(2,1)S(1)} %collective-permute-done.7.refs_1_) | copy-start | bytes 184324
  11.5 2.3 %copy-start.3 = (bf16[40,768]{1,0:T(8,128)(2,1)}, bf16[40,768]{1,0:T(8,128)(2,1)S(1)}, u32[]{:S(2)}) copy-start(bf16[40,768]{1,0:T(8,128)(2,1)S(1)} %collective-permute-done.8.refs_2_) | copy-start | bytes 184324
  13.8 0.6 %copy-start.4 = (bf16[40,768]{1,0:T(8,128)(2,1)}, bf16[40,768]{1,0:T(8,128)(2,1)S(1)}, u32[]{:S(2)}) copy-start(bf16[40,768]{1,0:T(8,128)(2,1)S(1)} %collective-permute-done.9.refs_3_) | copy-start | bytes 184324
  14.4 9.4 %copy-start.1 = (bf16[64,768]{1,0:T(8,128)(2,1)S(1)}, bf16[64,768]{1,0:T(8,128)(2,1)}, u32[]{:S(2)}) copy-start(bf16[64,768]{1,0:T(8,128)(2,1)} %refs_0_.1) | copy-start | bytes 294916
  16.0 7.7 %collective-permute-start.10 = (bf16[136,768]{1,0:T(8,128)(2,1)}, bf16[136,768]{1,0:T(8,128)(2,1)S(1)}, u32[]{:S(2)}, u32[]{:S(2)}) collective-permute-start(bf16[136,768]{1,0:T(8,128)(2,1)} %shard_map.29.refs_8_), channel_id=1, source_target_pairs={{0,8},{1,17},{2,10},{3,19},{4,12},{5,21},{6,14},{7,23},{8,0},{9,25... | collective-permute-start | bytes 626696 | tf_op jit(solution)/shard_map/ppermute | solution.py:144
  17.5 18.3 %collective-permute-start.11 = (bf16[136,768]{1,0:T(8,128)(2,1)}, bf16[136,768]{1,0:T(8,128)(2,1)S(1)}, u32[]{:S(2)}, u32[]{:S(2)}) collective-permute-start(bf16[136,768]{1,0:T(8,128)(2,1)} %shard_map.29.refs_8_), channel_id=1, source_target_pairs={{0,16},{1,9},{2,18},{3,11},{4,20},{5,13},{6,22},{7,15},{8,24},{9,1... | collective-permute-start | bytes 626696 | tf_op jit(solution)/shard_map/ppermute | solution.py:144
  23.8 12.1 %collective-permute-start.12 = (bf16[136,768]{1,0:T(8,128)(2,1)S(1)}, bf16[136,768]{1,0:T(8,128)(2,1)S(1)}, u32[]{:S(2)}, u32[]{:S(2)}) collective-permute-start(bf16[136,768]{1,0:T(8,128)(2,1)S(1)} %collective-permute-done.10.refs_9_), channel_id=1, source_target_pairs={{0,16},{1,9},{2,18},{3,11},{4,20},{5,13},{6,22},{7,15},{8,24},{9,1... | collective-permute-start | bytes 626696 | tf_op jit(solution)/shard_map/ppermute | solution.py:144
  23.8 2.2 %collective-permute-start.3 = (bf16[64,768]{1,0:T(8,128)(2,1)S(1)}, bf16[64,768]{1,0:T(8,128)(2,1)S(1)}, u32[]{:S(2)}, u32[]{:S(2)}) collective-permute-start(bf16[64,768]{1,0:T(8,128)(2,1)S(1)} %copy-done.1), channel_id=1, source_target_pairs={{0,1},{1,0},{2,3},{3,2},{4,5},{5,4},{6,7},{7,6},{8,9},{9,8},{10,11... | collective-permute-start | bytes 294920 | tf_op jit(solution)/shard_map/ppermute | solution.py:135
  23.8 7.5 %collective-permute-start.2 = (bf16[64,768]{1,0:T(8,128)(2,1)S(1)}, bf16[64,768]{1,0:T(8,128)(2,1)S(1)}, u32[]{:S(2)}, u32[]{:S(2)}) collective-permute-start(bf16[64,768]{1,0:T(8,128)(2,1)S(1)} %copy-done.1), channel_id=1, source_target_pairs={{0,6},{1,7},{2,4},{3,5},{4,2},{5,3},{6,0},{7,1},{8,14},{9,15},{10,... | collective-permute-start | bytes 294920 | tf_op jit(solution)/shard_map/ppermute | solution.py:135
  26.0 9.2 %collective-permute-start.1 = (bf16[64,768]{1,0:T(8,128)(2,1)S(1)}, bf16[64,768]{1,0:T(8,128)(2,1)S(1)}, u32[]{:S(2)}, u32[]{:S(2)}) collective-permute-start(bf16[64,768]{1,0:T(8,128)(2,1)S(1)} %copy-done.1), channel_id=1, source_target_pairs={{0,4},{1,5},{2,6},{3,7},{4,0},{5,1},{6,2},{7,3},{8,12},{9,13},{10,... | collective-permute-start | bytes 294920 | tf_op jit(solution)/shard_map/ppermute | solution.py:135
  26.0 9.3 %collective-permute-start = (bf16[64,768]{1,0:T(8,128)(2,1)S(1)}, bf16[64,768]{1,0:T(8,128)(2,1)S(1)}, u32[]{:S(2)}, u32[]{:S(2)}) collective-permute-start(bf16[64,768]{1,0:T(8,128)(2,1)S(1)} %copy-done.1), channel_id=1, source_target_pairs={{0,2},{1,3},{2,0},{3,1},{4,6},{5,7},{6,4},{7,5},{8,10},{9,11},{10,... | collective-permute-start | bytes 294920 | tf_op jit(solution)/shard_map/ppermute | solution.py:135
  31.4 5.0 %collective-permute-start.6 = (bf16[64,768]{1,0:T(8,128)(2,1)S(1)}, bf16[64,768]{1,0:T(8,128)(2,1)S(1)}, u32[]{:S(2)}, u32[]{:S(2)}) collective-permute-start(bf16[64,768]{1,0:T(8,128)(2,1)S(1)} %collective-permute-done.2.refs_3_), channel_id=1, source_target_pairs={{0,1},{1,0},{2,3},{3,2},{4,5},{5,4},{6,7},{7,6},{8,9},{9,8},{10,11... | collective-permute-start | bytes 294920 | tf_op jit(solution)/shard_map/ppermute | solution.py:135
  35.3 3.8 %collective-permute-start.13 = (bf16[136,768]{1,0:T(8,128)(2,1)}, bf16[136,768]{1,0:T(8,128)(2,1)S(1)}, u32[]{:S(2)}, u32[]{:S(2)}) collective-permute-start(bf16[136,768]{1,0:T(8,128)(2,1)} %shard_map.29.refs_8_), channel_id=1, source_target_pairs={{0,1},{1,0},{2,3},{3,2},{4,5},{5,4},{6,7},{7,6},{8,9},{9,8},{10,11... | collective-permute-start | bytes 626696 | tf_op jit(solution)/shard_map/ppermute | solution.py:135
  35.3 3.8 %collective-permute-start.14 = (bf16[136,768]{1,0:T(8,128)(2,1)S(1)}, bf16[136,768]{1,0:T(8,128)(2,1)S(1)}, u32[]{:S(2)}, u32[]{:S(2)}) collective-permute-start(bf16[136,768]{1,0:T(8,128)(2,1)S(1)} %collective-permute-done.10.refs_9_), channel_id=1, source_target_pairs={{0,1},{1,0},{2,3},{3,2},{4,5},{5,4},{6,7},{7,6},{8,9},{9,8},{10,11... | collective-permute-start | bytes 626696 | tf_op jit(solution)/shard_map/ppermute | solution.py:135
  35.8 3.3 %collective-permute-start.15 = (bf16[136,768]{1,0:T(8,128)(2,1)S(1)}, bf16[136,768]{1,0:T(8,128)(2,1)S(1)}, u32[]{:S(2)}, u32[]{:S(2)}) collective-permute-start(bf16[136,768]{1,0:T(8,128)(2,1)S(1)} %collective-permute-done.11.refs_10_), channel_id=1, source_target_pairs={{0,1},{1,0},{2,3},{3,2},{4,5},{5,4},{6,7},{7,6},{8,9},{9,8},{10,11... | collective-permute-start | bytes 626696 | tf_op jit(solution)/shard_map/ppermute | solution.py:135
  35.9 3.2 %collective-permute-start.16 = (bf16[136,768]{1,0:T(8,128)(2,1)S(1)}, bf16[136,768]{1,0:T(8,128)(2,1)S(1)}, u32[]{:S(2)}, u32[]{:S(2)}) collective-permute-start(bf16[136,768]{1,0:T(8,128)(2,1)S(1)} %collective-permute-done.12.refs_11_), channel_id=1, source_target_pairs={{0,1},{1,0},{2,3},{3,2},{4,5},{5,4},{6,7},{7,6},{8,9},{9,8},{10,11... | collective-permute-start | bytes 626696 | tf_op jit(solution)/shard_map/ppermute | solution.py:135
  36.3 1.5 %collective-permute-start.5 = (bf16[64,768]{1,0:T(8,128)(2,1)S(1)}, bf16[64,768]{1,0:T(8,128)(2,1)S(1)}, u32[]{:S(2)}, u32[]{:S(2)}) collective-permute-start(bf16[64,768]{1,0:T(8,128)(2,1)S(1)} %collective-permute-done.1.refs_2_), channel_id=1, source_target_pairs={{0,1},{1,0},{2,3},{3,2},{4,5},{5,4},{6,7},{7,6},{8,9},{9,8},{10,11... | collective-permute-start | bytes 294920 | tf_op jit(solution)/shard_map/ppermute | solution.py:135
  37.8 1.3 %collective-permute-start.4 = (bf16[64,768]{1,0:T(8,128)(2,1)S(1)}, bf16[64,768]{1,0:T(8,128)(2,1)S(1)}, u32[]{:S(2)}, u32[]{:S(2)}) collective-permute-start(bf16[64,768]{1,0:T(8,128)(2,1)S(1)} %collective-permute-done.refs_1_), channel_id=1, source_target_pairs={{0,1},{1,0},{2,3},{3,2},{4,5},{5,4},{6,7},{7,6},{8,9},{9,8},{10,11... | collective-permute-start | bytes 294920 | tf_op jit(solution)/shard_map/ppermute | solution.py:135
  39.1 0.9 %copy-start = (bf16[136,768]{1,0:T(8,128)(2,1)S(1)}, bf16[136,768]{1,0:T(8,128)(2,1)}, u32[]{:S(2)}) copy-start(bf16[136,768]{1,0:T(8,128)(2,1)} %shard_map.29.refs_8_) | copy-start | bytes 626692

commit v2 on v0

v2 whole, which is shorter than its diff:
```python
import functools

import jax
import jax.numpy as jnp
from jax import lax
from jax.experimental import pallas as pl
from jax.experimental.pallas import tpu as pltpu
from jax.sharding import PartitionSpec as P

CL_DEV = 128
ID_ROWS = 8
NT = (((1,), (1,)), ((), ()))
NN = (((1,), (0,)), ((), ()))
VMEM = pl.BlockSpec(memory_space=pltpu.VMEM)
MIB = 1024 * 1024


def dot(left, right, dims):
    return lax.dot_general(left, right, dims, preferred_element_type=jnp.float32)


def bf16(*shape):
    return jax.ShapeDtypeStruct(shape, jnp.bfloat16)


def call(kernel, out_shape, args, scratch=(), mib=8, after=(), cost=None):
    count = len(args)

    def body(*refs):
        kernel(*refs[:count], *refs[count + len(after) :])

    return pl.pallas_call(
        body,
        out_shape=out_shape,
        in_specs=[VMEM] * count + [pl.BlockSpec(memory_space=pl.ANY)] * len(after),
        out_specs=[VMEM] * len(out_shape),
        scratch_shapes=scratch,
        compiler_params=pltpu.CompilerParams(vmem_limit_bytes=mib * MIB),
        cost_estimate=cost,
    )(*args, *after)


def label_kernel(points_ref, labels_ref, out_ref):
    own_count, width = points_ref.shape
    out_ref[:own_count, :] = points_ref[...]
    out_ref[own_count:, :] = jnp.zeros((ID_ROWS, width), jnp.bfloat16)
    for n in range(2):
        out_ref[own_count:, n * CL_DEV : n * CL_DEV + own_count] = jnp.broadcast_to(
            labels_ref[n : n + 1, :].astype(jnp.float32), (ID_ROWS, own_count)
        ).astype(jnp.bfloat16)


def select_kernel(slots, *refs):
    *block_refs, local_ref, set_ref = refs
    count = len(block_refs)
    own_count = block_refs[0].shape[0] - ID_ROWS
    points = count * own_count
    half = count * slots
    me = lax.axis_index("col")
    earlier = (
        lax.broadcasted_iota(jnp.int32, (own_count, own_count), 0)
        < lax.broadcasted_iota(jnp.int32, (own_count, own_count), 1)
    ).astype(jnp.bfloat16)
    slot = lax.broadcasted_iota(jnp.int32, (2 * half, own_count), 0)
    ids = jnp.zeros((ID_ROWS, 2 * half), jnp.float32)
    dispatch = []
    for n, block_ref in enumerate(block_refs):
        local_ref[n * own_count : (n + 1) * own_count, :] = block_ref[:own_count, :]
        group_of = block_ref[own_count:, :own_count].astype(jnp.float32).astype(jnp.int32)
        labels = block_ref[own_count:, CL_DEV : CL_DEV + own_count].astype(jnp.float32) + 1.0
        relative = group_of ^ me
        member = lax.broadcasted_iota(jnp.int32, (ID_ROWS, own_count), 0) == relative
        rank = dot(member.astype(jnp.bfloat16), earlier, NN)
        position = jnp.sum(jnp.where(member, rank, 0.0), axis=0, keepdims=True)
        target = jnp.where(
            relative < 2, relative * half + n * slots + position.astype(jnp.int32), -1
        )
        chosen = (slot == target[:1]).astype(jnp.bfloat16)
        ids += dot(labels.astype(jnp.bfloat16), chosen, NT)
        dispatch.append(chosen)
    rows = dot(jnp.concatenate(dispatch, axis=1), local_ref[:points, :], NN).astype(jnp.bfloat16)
    for ref, start in ((local_ref, points), (set_ref, 0)):
        end = start + 2 * half
        ref[start:end, :] = rows
        ref[end:, :] = jnp.zeros((ID_ROWS, ref.shape[1]), jnp.bfloat16)
        ref[end:, : 2 * half] = ids.astype(jnp.bfloat16)


def column_norms(rows):
    values = rows.astype(jnp.float32)
    return jnp.sum(values * values, axis=1, keepdims=True)


def row_of(column):
    return jnp.transpose(jnp.broadcast_to(column, (column.shape[0], 128)))[:1]


class Half:
    def __init__(self, ref, base, count, second):
        self.ref, self.base, self.count = ref, base, count
        self.start = count if second else 0

    def rows(self):
        start = self.base + self.start
        return self.ref[start : start + self.count, :]

    def indicator(self):
        base = self.base + 2 * self.count
        ids = self.ref[base : base + ID_ROWS, self.start : self.start + self.count]
        ids = ids.astype(jnp.float32).astype(jnp.int32)[:1]
        clusters = lax.broadcasted_iota(jnp.int32, (CL_DEV, self.count), 0)
        return (clusters + 1 == ids).astype(jnp.bfloat16)


def stack_kernel(*refs):
    *in_refs, out_ref = refs
    place = 0
    for in_ref in in_refs:
        out_ref[place : place + in_ref.shape[0], :] = in_ref[...]
        place += in_ref.shape[0]


def stack(*arrays, after=()):
    rows = sum(one.shape[0] for one in arrays)
    return call(stack_kernel, [bf16(rows, arrays[0].shape[1])], arrays, after=after)[0]


def kern(rows, slots, slot_norms):
    inner = dot(rows, slots, NT)
    squared = column_norms(rows) + slot_norms - 2.0 * inner
    return jnp.exp(squared * (-1.0 / rows.shape[1])).astype(jnp.bfloat16)


def row_norms(slots_ref):
    pieces = [
        row_of(column_norms(slots_ref[start : start + CL_DEV, :]))
        for start in range(0, slots_ref.shape[0], CL_DEV)
    ]
    return jnp.concatenate(pieces, axis=1)


def chunks(begin, end, step):
    return [(start, min(start + step, end)) for start in range(begin, end, step)]


def sums_kernel(counts, parts, *refs):
    *array_refs, left_ref, hot_ref, sums_ref, totals_ref = refs
    rows, total = sums_ref.shape[0], left_ref.shape[0]
    place = 0
    for array_ref, count in zip(array_refs, counts):
        left_ref[place : place + count, :] = array_ref[:count, :]
        place += count
    for n, *rest in parts:
        part = Half(array_refs[n], *rest)
        end = place + part.count
        left_ref[place:end, :] = part.rows()
        hot_ref[:, place - rows : end - rows] = part.indicator()
        place = end
    slots, hot = left_ref[rows:, :], hot_ref[...]
    norms = row_norms(left_ref.at[rows:])
    for start, end in chunks(0, rows, 256):
        sums_ref[start:end, :] = dot(kern(left_ref[start:end, :], slots, norms), hot, NT)
    shares = jnp.zeros(hot.shape, jnp.float32)
    for start, end in chunks(rows, total, 256):
        tile = kern(left_ref[start:end, :], slots, norms)
        shares += dot(hot_ref[:, start - rows : end - rows], tile, NN)
    column = jnp.sum(shares * hot.astype(jnp.float32), axis=1, keepdims=True)
    ones = jnp.ones((8, total - rows), jnp.bfloat16)
    totals_ref[:8, :] = jnp.broadcast_to(row_of(column), (8, CL_DEV))
    totals_ref[8:, :] = dot(ones, hot, NT)


def distance_kernel(parts, order, *refs):
    left_ref, old_hot_ref, sums_ref, totals_ref, *refs = refs
    *array_refs, out_ref, slots_ref, hot_ref = refs
    rows, total = sums_ref.shape[0], left_ref.shape[0]
    place = 0
    for n, *rest in parts:
        part = Half(array_refs[n], *rest)
        end = place + part.count
        slots_ref[place:end, :] = part.rows()
        hot_ref[:, place:end] = part.indicator()
        place = end
    slots, hot = slots_ref[...], hot_ref[...]
    norms = row_norms(slots_ref)
    shares = dot(hot, kern(slots, slots, norms), NN)
    for start, end in chunks(rows, total, 512):
        tile = kern(left_ref[start:end, :], slots, norms)
        shares += 2.0 * dot(old_hot_ref[:, start - rows : end - rows], tile, NN)
    column = jnp.sum(shares * hot.astype(jnp.float32), axis=1, keepdims=True)
    totals = totals_ref[:1, :] + row_of(column)
    counts = totals_ref[8:9, :] + dot(jnp.ones((8, place), jnp.bfloat16), hot, NT)[:1]
    sizes = jnp.maximum(counts, 1.0)
    offset = 1.0 + totals / (sizes * sizes)
    factor = 2.0 / sizes
    me = lax.axis_index("col")
    own_count = rows // len(order)
    for start, end in chunks(0, rows, 512):
        part = sums_ref[start:end, :] + dot(kern(left_ref[start:end, :], slots, norms), hot, NT)
        part = offset - part * factor
        for b in range((end - start) // own_count):
            row = pl.multiple_of((me ^ order[start // own_count + b]) * own_count, own_count)
            out_ref[pl.ds(row, own_count), :] = part[b * own_count : (b + 1) * own_count]


def parts_of(sets, arrays):
    parts = []
    for one, base, count, second in sets:
        n = [array is one for array in arrays].index(True)
        for start in range(base, one.shape[0], 2 * count + ID_ROWS):
            parts.append((n, start, count, second))
    return parts


def cost_of(rows, slots, width):
    return pl.CostEstimate(
        flops=2 * rows * slots * (width + CL_DEV),
        bytes_accessed=2 * rows * width,
        transcendentals=rows * slots,
    )


def sum_slots(sets):
    arrays = [one for one, *_ in sets]
    counts = [base for _, base, *_ in sets if base]
    parts = parts_of(sets, arrays)
    width, rows, slots = arrays[0].shape[1], sum(counts), sum(part[2] for part in parts)
    return call(
        functools.partial(sums_kernel, counts, parts),
        [
            bf16(rows + slots, width),
            bf16(CL_DEV, slots),
            jax.ShapeDtypeStruct((rows, CL_DEV), jnp.float32),
            jax.ShapeDtypeStruct((16, CL_DEV), jnp.float32),
        ],
        arrays,
        mib=32,
        cost=cost_of(3 * (rows + slots), slots, width),
    )


def finish(order, sums, sets):
    arrays = [one for one, *_ in sets]
    parts = parts_of(sets, arrays)
    width, slots = arrays[0].shape[1], sum(part[2] for part in parts)
    return call(
        functools.partial(distance_kernel, parts, order),
        [jax.ShapeDtypeStruct(sums[2].shape, jnp.float32)],
        [*sums, *arrays],
        [pltpu.VMEM((slots, width), jnp.bfloat16), pltpu.VMEM((CL_DEV, slots), jnp.bfloat16)],
        mib=32,
        cost=cost_of(sums[0].shape[0] + slots, slots, width),
    )[0]


def per_device(points, assign):
    own_count, width = points.shape
    group_count, row_count = lax.axis_size("col"), lax.axis_size("row")
    chips = group_count // 2
    slots = max(2, 2 * own_count // group_count)

    def over_col(values, bits):
        return lax.ppermute(values, "col", [(i, i ^ bits) for i in range(group_count)])

    def over_row(values, bits_of):
        pairs = [
            (r * group_count + c, (r ^ bits_of(c)) * group_count + c)
            for r in range(row_count)
            for c in range(group_count)
        ]
        return lax.ppermute(values, ("row", "col"), pairs)

    def in_steps(sets, here):
        steps = row_count.bit_length() - 1
        for step in range(steps):
            got = over_row(sets, lambda c: 1 << (step if c % 2 == 0 else steps - 1 - step))
            if step < steps - 1:
                sets, here = stack(sets, got), stack(here, got)
        return here, got

    def at_once(sets, here):
        got = [over_row(sets, lambda c: bits) for bits in range(row_count - 1, 0, -1)]
        return here, stack(*got)

    group_of = assign // CL_DEV
    labels = jnp.stack([group_of, assign - group_of * CL_DEV])
    [labelled] = call(label_kernel, [bf16(own_count + ID_ROWS, width)], [points, labels])
    blocks = {0: labelled}
    bit = chips // 2
    while bit:
        blocks |= {q + bit: over_col(one, 2 * bit) for q, one in blocks.items()}
        bit //= 2
    places, near, last = [], [], []
    for batch, share in ((range(2), in_steps), (range(2, chips), at_once)):
        base, half = len(batch) * own_count, len(batch) * slots
        here, sets = call(
            functools.partial(select_kernel, slots),
            [bf16(base + 2 * half + ID_ROWS, width), bf16(2 * half + ID_ROWS, width)],
            [blocks[q] for q in batch],
            after=[one[0] for one in near],
        )
        here, got = share(sets, here)
        places.append([2 * q for q in batch])
        near.append((here, base, half))
        last.append((got, 0, half))

    def both_cores(one, base, half):
        return [(one, base, half, False), (over_col(one, 1), base, half, True)]

    pairs = [both_cores(*one) for one in near]
    old = [pair[0] for pair in pairs] + [pair[1] for pair in pairs] + both_cores(*last[0])
    order = [q for side in range(2) for batch in places for q in (one ^ side for one in batch)]
    sums = sum_slots(old)
    return finish(order, sums, both_cores(*last[1]))


def solution(mesh):
    return jax.shard_map(
        per_device,
        mesh=mesh,
        in_specs=(P(("row", "col"), None), P(("row", "col"))),
        out_specs=P("row", "col"),
        check_vma=False,
    )
```

time: 69.2 us -> 29.8 us (0.43)
  blocking collectives: 47.7 us -> 0 us
  starting transfers between devices: 9.72 us -> 15.2 us
  waiting for transfers between devices: 3.66 us -> 8.32 us
  Pallas kernels: 0 us -> 4.44 us
  matrix products: 2.91 us -> 0 us
  other arithmetic: 3.36 us -> 0.68 us
    all_gather x3 -> x0, blocking collectives: 38.7 us -> none  [the longest x1 18.8 us: per_device(): row_block = lax.all_gather(points, 'col', axis=0, tiled=True)]
    ppermute x0 -> x12, starting transfers between devices: none -> 15.2 us  [the longest x5 8.51 us: over_row(): return lax.ppermute(values, ('row', 'col'), pairs)]
    all_to_all x2 -> x0, starting transfers between devices: 9.72 us -> none  [the longest x1 6.33 us: per_device(): lax.all_to_all(slot_ids, 'col', split_axis=0, concat_axis=0, tiled=True)]
    psum x1 -> x0, blocking collectives: 8.92 us -> none  [per_device(): self_total = lax.psum(partial_self, 'row')]
    ppermute x0 -> x12, waiting for transfers between devices: none -> 8.32 us  [the longest x5 4.87 us: over_row(): return lax.ppermute(values, ('row', 'col'), pairs)]
    pallas_call x0 -> x8, Pallas kernels: none -> 4.44 us  [call(): pl.pallas_call(body, out_shape=out_shape, in_specs=[VMEM] * count + [pl.B...]
    all_to_all x2 -> x0, waiting for transfers between devices: 3.66 us -> none  [the longest x1 3.66 us: per_device(): lax.all_to_all(slot_ids, 'col', split_axis=0, concat_axis=0, tiled=True)]
    dot_general x2 -> x0, matrix products: 2.91 us -> none  [the longest x1 1.9 us: per_device(): jnp.dot(dispatch, points, preferred_element_type=jnp.float32)]
  transfers between devices with their start and end apart: 2 -> 12, of which waited for: 1 -> 7; matrix products, arithmetic and copies ran while one was open for 5% -> 0% of each run, Pallas kernels for 0% -> 9%
where the time goes in v2:
time: 29.8 us; the launch traced here: 29.6 us
  starting transfers between devices  15.2 us (51%)
  waiting for transfers between devices  8.32 us (28%)
  Pallas kernels  4.44 us (15%)
  local copies, waits for them, and re-layouts  0.89 us (3%)
  other arithmetic  0.68 us (2%)
    ppermute x5, starting transfers between devices, over_row(): return lax.ppermute(values, ('row', 'col'), pairs)  8.51 us
    ppermute x7, starting transfers between devices, over_col(): lax.ppermute(values, 'col', [(i, i ^ bits) for i in range(group_count)])  6.71 us
    ppermute x5, waiting for transfers between devices, over_row(): return lax.ppermute(values, ('row', 'col'), pairs)  4.87 us
    pallas_call x8, Pallas kernels, call(): pl.pallas_call(body, out_shape=out_shape, in_specs=[VMEM] * count + [pl.B...  4.44 us
    ppermute x7, waiting for transfers between devices, over_col(): lax.ppermute(values, 'col', [(i, i ^ bits) for i in range(group_count)])  3.45 us
    unnamed x2, local copies, waits for them, and re-layouts  0.89 us
    another operation x2, other arithmetic, per_device(): labels = jnp.stack([group_of, assign - group_of * CL_DEV])  0.68 us
  transfers between devices with their start and end apart: 12, of which 7 were waited for; matrix products, arithmetic and copies ran while one was open for 0% of the time, Pallas kernels for 9%

profile of v2, /device:TPU:0, one launch (start us, length us, event | category | flops | bytes accessed | tf_op | source)
XLA Modules:
  0.0 29.6 jit_solution(13449336366639481869)
XLA Ops:
  0.0 0.7 %subtract_bitcast_fusion = (s32[1,64]{1,0:T(1,128)S(1)}, s32[64]{0:T(128)S(1)}) fusion(s32[64]{0:T(128)} %param.3), kind=kLoop, calls=%fused_computation.5 | loop fusion | flops 1088 | bytes 768 | tf_op jit(solution)/shard_map/stack | solution.py:286
  0.7 0.0 copy-start
  0.7 0.9 %copy-done = bf16[64,768]{1,0:T(8,128)(2,1)S(1)} copy-done((bf16[64,768]{1,0:T(8,128)(2,1)S(1)}, bf16[64,768]{1,0:T(8,128)(2,1)}, u32[]{:S(2)}) %copy-start) | copy-done | bytes 98328
  1.6 3.1 %collective-permute-start = (bf16[72,768]{1,0:T(8,128)(2,1)S(1)}, bf16[72,768]{1,0:T(8,128)(2,1)S(1)}, u32[]{:S(2)}, u32[]{:S(2)}) collective-permute-start(bf16[72,768]{1,0:T(8,128)(2,1)S(1)} %shard_map.28.refs_0_), channel_id=1, source_target_pairs={{0,2},{1,3},{2,0},{3,1},{4,6},{5,7},{6,4},{7,5},{8,10},{9,11},{10,... | collective-permute-start | bytes 331784 | tf_op jit(solution)/shard_map/ppermute | solution.py:263
  4.7 2.6 %collective-permute-start.2 = (bf16[72,768]{1,0:T(8,128)(2,1)S(1)}, bf16[72,768]{1,0:T(8,128)(2,1)S(1)}, u32[]{:S(2)}, u32[]{:S(2)}) collective-permute-start(bf16[72,768]{1,0:T(8,128)(2,1)S(1)} %shard_map.28.refs_0_), channel_id=1, source_target_pairs={{0,4},{1,5},{2,6},{3,7},{4,0},{5,1},{6,2},{7,3},{8,12},{9,13},{10,... | collective-permute-start | bytes 331784 | tf_op jit(solution)/shard_map/ppermute | solution.py:263
  7.3 0.5 %collective-permute-done.refs_1_ = bf16[72,768]{1,0:T(8,128)(2,1)S(1)} collective-permute-done((bf16[72,768]{1,0:T(8,128)(2,1)S(1)}, bf16[72,768]{1,0:T(8,128)(2,1)S(1)}, u32[]{:S(2)}, u32[]{:S(2)}) %collective-permute-start) | collective-permute-done | bytes 110624 | tf_op jit(solution)/shard_map/ppermute | solution.py:263
  7.7 0.4 %shard_map.29 = (bf16[200,768]{1,0:T(8,128)(2,1)S(1)}, bf16[72,768]{1,0:T(8,128)(2,1)S(1)}) custom-call(bf16[72,768]{1,0:T(8,128)(2,1)S(1)} %shard_map.28.refs_0_, bf16[72,768]{1,0:T(8,128)(2,1)S(1)} %collective-permute-done.refs_1_), custom_call_target="tpu_custom_call" | custom-call | tf_op jit(solution)/shard_map/pallas_call | solution.py:32
  8.1 2.8 %collective-permute-start.1 = (bf16[72,768]{1,0:T(8,128)(2,1)S(1)}, bf16[72,768]{1,0:T(8,128)(2,1)S(1)}, u32[]{:S(2)}, u32[]{:S(2)}) collective-permute-start(bf16[72,768]{1,0:T(8,128)(2,1)S(1)} %get-tuple-element.14.refs_0_), channel_id=1, source_target_pairs={{0,8},{1,17},{2,10},{3,19},{4,12},{5,21},{6,14},{7,23},{8,0},{9,25... | collective-permute-start | bytes 331784 | tf_op jit(solution)/shard_map/ppermute | solution.py:271
  11.0 1.6 %collective-permute-done.2.refs_0_ = bf16[72,768]{1,0:T(8,128)(2,1)S(1)} collective-permute-done((bf16[72,768]{1,0:T(8,128)(2,1)S(1)}, bf16[72,768]{1,0:T(8,128)(2,1)S(1)}, u32[]{:S(2)}, u32[]{:S(2)}) %collective-permute-start.2) | collective-permute-done | bytes 110624 | tf_op jit(solution)/shard_map/ppermute | solution.py:263
  12.5 0.4 %collective-permute-start.3 = (bf16[72,768]{1,0:T(8,128)(2,1)S(1)}, bf16[72,768]{1,0:T(8,128)(2,1)S(1)}, u32[]{:S(2)}, u32[]{:S(2)}) collective-permute-start(bf16[72,768]{1,0:T(8,128)(2,1)S(1)} %collective-permute-done.2.refs_0_), channel_id=1, source_target_pairs={{0,2},{1,3},{2,0},{3,1},{4,6},{5,7},{6,4},{7,5},{8,10},{9,11},{10,... | collective-permute-start | bytes 331784 | tf_op jit(solution)/shard_map/ppermute | solution.py:263
  13.0 0.7 %collective-permute-done.1.refs_1_ = bf16[72,768]{1,0:T(8,128)(2,1)S(1)} collective-permute-done((bf16[72,768]{1,0:T(8,128)(2,1)S(1)}, bf16[72,768]{1,0:T(8,128)(2,1)S(1)}, u32[]{:S(2)}, u32[]{:S(2)}) %collective-permute-start.1) | collective-permute-done | bytes 110624 | tf_op jit(solution)/shard_map/ppermute | solution.py:271
  13.7 2.1 %collective-permute-start.6 = (bf16[144,768]{1,0:T(8,128)(2,1)S(1)}, bf16[144,768]{1,0:T(8,128)(2,1)S(1)}, u32[]{:S(2)}, u32[]{:S(2)}) collective-permute-start(bf16[144,768]{1,0:T(8,128)(2,1)S(1)} %shard_map.32), channel_id=1, source_target_pairs={{0,16},{1,9},{2,18},{3,11},{4,20},{5,13},{6,22},{7,15},{8,24},{9,1... | collective-permute-start | bytes 663560 | tf_op jit(solution)/shard_map/ppermute | solution.py:271
  15.8 1.4 %collective-permute-done.3.refs_1_ = bf16[72,768]{1,0:T(8,128)(2,1)S(1)} collective-permute-done((bf16[72,768]{1,0:T(8,128)(2,1)S(1)}, bf16[72,768]{1,0:T(8,128)(2,1)S(1)}, u32[]{:S(2)}, u32[]{:S(2)}) %collective-permute-start.3) | collective-permute-done | bytes 110624 | tf_op jit(solution)/shard_map/ppermute | solution.py:263
  17.3 0.4 %shard_map.31 = (bf16[200,768]{1,0:T(8,128)(2,1)S(1)}, bf16[72,768]{1,0:T(8,128)(2,1)S(1)}) custom-call(bf16[72,768]{1,0:T(8,128)(2,1)S(1)} %collective-permute-done.2.refs_0_, bf16[72,768]{1,0:T(8,128)(2,1)S(1)} %collective-permute-done.3.refs_1_, bf16[272,768]{1,0:T(8,128)(2,1)S(1)} %shard_map.30.refs_2_.refs_0_), custom_call_target="tpu_custom_call" | custom-call | tf_op jit(solution)/shard_map/pallas_call | solution.py:32
  17.6 2.5 %collective-permute-start.8 = (bf16[72,768]{1,0:T(8,128)(2,1)S(1)}, bf16[72,768]{1,0:T(8,128)(2,1)S(1)}, u32[]{:S(2)}, u32[]{:S(2)}) collective-permute-start(bf16[72,768]{1,0:T(8,128)(2,1)S(1)} %get-tuple-element.20), channel_id=1, source_target_pairs={{0,24},{1,25},{2,26},{3,27},{4,28},{5,29},{6,30},{7,31},{8,16},{9,... | collective-permute-start | bytes 331784 | tf_op jit(solution)/shard_map/ppermute | solution.py:271
  20.1 0.0 collective-permute-start.4
  20.1 0.5 %collective-permute-start.9 = (bf16[72,768]{1,0:T(8,128)(2,1)S(1)}, bf16[72,768]{1,0:T(8,128)(2,1)S(1)}, u32[]{:S(2)}, u32[]{:S(2)}) collective-permute-start(bf16[72,768]{1,0:T(8,128)(2,1)S(1)} %get-tuple-element.20), channel_id=1, source_target_pairs={{0,16},{1,17},{2,18},{3,19},{4,20},{5,21},{6,22},{7,23},{8,24},{9,... | collective-permute-start | bytes 331784 | tf_op jit(solution)/shard_map/ppermute | solution.py:271
  20.7 0.5 %collective-permute-start.10 = (bf16[72,768]{1,0:T(8,128)(2,1)S(1)}, bf16[72,768]{1,0:T(8,128)(2,1)S(1)}, u32[]{:S(2)}, u32[]{:S(2)}) collective-permute-start(bf16[72,768]{1,0:T(8,128)(2,1)S(1)} %get-tuple-element.20), channel_id=1, source_target_pairs={{0,8},{1,9},{2,10},{3,11},{4,12},{5,13},{6,14},{7,15},{8,0},{9,1},... | collective-permute-start | bytes 331784 | tf_op jit(solution)/shard_map/ppermute | solution.py:271
  21.2 2.2 %collective-permute-done.8.refs_0_ = bf16[72,768]{1,0:T(8,128)(2,1)S(1)} collective-permute-done((bf16[72,768]{1,0:T(8,128)(2,1)S(1)}, bf16[72,768]{1,0:T(8,128)(2,1)S(1)}, u32[]{:S(2)}, u32[]{:S(2)}) %collective-permute-start.8) | collective-permute-done | bytes 110624 | tf_op jit(solution)/shard_map/ppermute | solution.py:271
  23.4 0.0 collective-permute-start.5
  23.4 0.0 collective-permute-done.6.refs_4_
  23.4 0.5 %collective-permute-start.7 = (bf16[144,768]{1,0:T(8,128)(2,1)S(1)}, bf16[144,768]{1,0:T(8,128)(2,1)S(1)}, u32[]{:S(2)}, u32[]{:S(2)}) collective-permute-start(bf16[144,768]{1,0:T(8,128)(2,1)S(1)} %collective-permute-done.6.refs_4_), channel_id=1, source_target_pairs={{0,1},{1,0},{2,3},{3,2},{4,5},{5,4},{6,7},{7,6},{8,9},{9,8},{10,11... | collective-permute-start | bytes 663560 | tf_op jit(solution)/shard_map/ppermute | solution.py:263
  23.9 1.8 %collective-permute-done.9.refs_1_ = bf16[72,768]{1,0:T(8,128)(2,1)S(1)} collective-permute-done((bf16[72,768]{1,0:T(8,128)(2,1)S(1)}, bf16[72,768]{1,0:T(8,128)(2,1)S(1)}, u32[]{:S(2)}, u32[]{:S(2)}) %collective-permute-start.9) | collective-permute-done | bytes 110624 | tf_op jit(solution)/shard_map/ppermute | solution.py:271
  25.7 0.1 collective-permute-done.10.refs_2_
  25.9 0.1 collective-permute-start.11
  26.0 0.0 collective-permute-done.5.refs_3_
  26.0 0.0 collective-permute-done.4.refs_2_
  26.0 0.0 collective-permute-done.7.refs_5_
  26.0 1.8 %shard_map.33 = (bf16[832,768]{1,0:T(8,128)(2,1)S(1)}, bf16[128,320]{1,0:T(8,128)(2,1)S(1)}, f32[512,128]{1,0:T(8,128)S(1)}, f32[16,128]{1,0:T(8,128)S(1)}) custom-call(bf16[272,768]{1,0:T(8,128)(2,1)S(1)} %shard_map.30.refs_2_.refs_0_, bf16[200,768]{1,0:T(8,128)(2,1)S(1)} %get-tuple-element.15.refs_1_, bf16[272,768]{1,0:T(8,128)(2,1)S(1)} %collective-permute-done.4.refs_2_, ...), custom_call_target="tpu_custom_call" | custom-call | flops 1431306240 | bytes 3833856 | tf_op jit(solution)/shard_map/pallas_call | solution.py:32
  27.8 0.0 collective-permute-done.11.refs_5_
  27.8 1.8 %shard_map.35 = f32[512,128]{1,0:T(8,128)} custom-call(bf16[832,768]{1,0:T(8,128)(2,1)S(1)} %get-tuple-element.16.refs_0_, bf16[128,320]{1,0:T(8,128)(2,1)S(1)} %get-tuple-element.17.refs_1_, f32[512,128]{1,0:T(8,128)S(1)} %get-tuple-element.18.refs_2_, f32[16,128]{1,0:T(8,128)S(1)} %get-tuple-element.19.refs_3_, bf16[216,768]{1,0:T(8,128)(2,1)S(1)} %shard_map.34.refs_4_, ...), custom_call_target="tpu_custom_call" | custom-call | flops 352321536 | bytes 1572864 | tf_op jit(solution)/shard_map/pallas_call | solution.py:32
  (5 shorter events, 0.1 us)
Async XLA Ops:
  0.7 0.9 %copy-start = (bf16[64,768]{1,0:T(8,128)(2,1)S(1)}, bf16[64,768]{1,0:T(8,128)(2,1)}, u32[]{:S(2)}) copy-start(bf16[64,768]{1,0:T(8,128)(2,1)} %refs_0_.1) | copy-start | bytes 294916
  1.6 6.2 %collective-permute-start = (bf16[72,768]{1,0:T(8,128)(2,1)S(1)}, bf16[72,768]{1,0:T(8,128)(2,1)S(1)}, u32[]{:S(2)}, u32[]{:S(2)}) collective-permute-start(bf16[72,768]{1,0:T(8,128)(2,1)S(1)} %shard_map.28.refs_0_), channel_id=1, source_target_pairs={{0,2},{1,3},{2,0},{3,1},{4,6},{5,7},{6,4},{7,5},{8,10},{9,11},{10,... | collective-permute-start | bytes 331784 | tf_op jit(solution)/shard_map/ppermute | solution.py:263
  4.7 7.8 %collective-permute-start.2 = (bf16[72,768]{1,0:T(8,128)(2,1)S(1)}, bf16[72,768]{1,0:T(8,128)(2,1)S(1)}, u32[]{:S(2)}, u32[]{:S(2)}) collective-permute-start(bf16[72,768]{1,0:T(8,128)(2,1)S(1)} %shard_map.28.refs_0_), channel_id=1, source_target_pairs={{0,4},{1,5},{2,6},{3,7},{4,0},{5,1},{6,2},{7,3},{8,12},{9,13},{10,... | collective-permute-start | bytes 331784 | tf_op jit(solution)/shard_map/ppermute | solution.py:263
  8.1 5.6 %collective-permute-start.1 = (bf16[72,768]{1,0:T(8,128)(2,1)S(1)}, bf16[72,768]{1,0:T(8,128)(2,1)S(1)}, u32[]{:S(2)}, u32[]{:S(2)}) collective-permute-start(bf16[72,768]{1,0:T(8,128)(2,1)S(1)} %get-tuple-element.14.refs_0_), channel_id=1, source_target_pairs={{0,8},{1,17},{2,10},{3,19},{4,12},{5,21},{6,14},{7,23},{8,0},{9,25... | collective-permute-start | bytes 331784 | tf_op jit(solution)/shard_map/ppermute | solution.py:271
  12.5 4.7 %collective-permute-start.3 = (bf16[72,768]{1,0:T(8,128)(2,1)S(1)}, bf16[72,768]{1,0:T(8,128)(2,1)S(1)}, u32[]{:S(2)}, u32[]{:S(2)}) collective-permute-start(bf16[72,768]{1,0:T(8,128)(2,1)S(1)} %collective-permute-done.2.refs_0_), channel_id=1, source_target_pairs={{0,2},{1,3},{2,0},{3,1},{4,6},{5,7},{6,4},{7,5},{8,10},{9,11},{10,... | collective-permute-start | bytes 331784 | tf_op jit(solution)/shard_map/ppermute | solution.py:263
  13.7 9.7 %collective-permute-start.6 = (bf16[144,768]{1,0:T(8,128)(2,1)S(1)}, bf16[144,768]{1,0:T(8,128)(2,1)S(1)}, u32[]{:S(2)}, u32[]{:S(2)}) collective-permute-start(bf16[144,768]{1,0:T(8,128)(2,1)S(1)} %shard_map.32), channel_id=1, source_target_pairs={{0,16},{1,9},{2,18},{3,11},{4,20},{5,13},{6,22},{7,15},{8,24},{9,1... | collective-permute-start | bytes 663560 | tf_op jit(solution)/shard_map/ppermute | solution.py:271
  17.6 5.7 %collective-permute-start.8 = (bf16[72,768]{1,0:T(8,128)(2,1)S(1)}, bf16[72,768]{1,0:T(8,128)(2,1)S(1)}, u32[]{:S(2)}, u32[]{:S(2)}) collective-permute-start(bf16[72,768]{1,0:T(8,128)(2,1)S(1)} %get-tuple-element.20), channel_id=1, source_target_pairs={{0,24},{1,25},{2,26},{3,27},{4,28},{5,29},{6,30},{7,31},{8,16},{9,... | collective-permute-start | bytes 331784 | tf_op jit(solution)/shard_map/ppermute | solution.py:271
  20.1 5.8 %collective-permute-start.4 = (bf16[272,768]{1,0:T(8,128)(2,1)S(1)}, bf16[272,768]{1,0:T(8,128)(2,1)S(1)}, u32[]{:S(2)}, u32[]{:S(2)}) collective-permute-start(bf16[272,768]{1,0:T(8,128)(2,1)S(1)} %shard_map.30.refs_2_.refs_0_), channel_id=1, source_target_pairs={{0,1},{1,0},{2,3},{3,2},{4,5},{5,4},{6,7},{7,6},{8,9},{9,8},{10,11... | collective-permute-start | bytes 1253384 | tf_op jit(solution)/shard_map/ppermute | solution.py:263
  20.1 5.6 %collective-permute-start.9 = (bf16[72,768]{1,0:T(8,128)(2,1)S(1)}, bf16[72,768]{1,0:T(8,128)(2,1)S(1)}, u32[]{:S(2)}, u32[]{:S(2)}) collective-permute-start(bf16[72,768]{1,0:T(8,128)(2,1)S(1)} %get-tuple-element.20), channel_id=1, source_target_pairs={{0,16},{1,17},{2,18},{3,19},{4,20},{5,21},{6,22},{7,23},{8,24},{9,... | collective-permute-start | bytes 331784 | tf_op jit(solution)/shard_map/ppermute | solution.py:271
  20.7 5.2 %collective-permute-start.10 = (bf16[72,768]{1,0:T(8,128)(2,1)S(1)}, bf16[72,768]{1,0:T(8,128)(2,1)S(1)}, u32[]{:S(2)}, u32[]{:S(2)}) collective-permute-start(bf16[72,768]{1,0:T(8,128)(2,1)S(1)} %get-tuple-element.20), channel_id=1, source_target_pairs={{0,8},{1,9},{2,10},{3,11},{4,12},{5,13},{6,14},{7,15},{8,0},{9,1},... | collective-permute-start | bytes 331784 | tf_op jit(solution)/shard_map/ppermute | solution.py:271
  23.4 2.6 %collective-permute-start.5 = (bf16[200,768]{1,0:T(8,128)(2,1)S(1)}, bf16[200,768]{1,0:T(8,128)(2,1)S(1)}, u32[]{:S(2)}, u32[]{:S(2)}) collective-permute-start(bf16[200,768]{1,0:T(8,128)(2,1)S(1)} %get-tuple-element.15.refs_1_), channel_id=1, source_target_pairs={{0,1},{1,0},{2,3},{3,2},{4,5},{5,4},{6,7},{7,6},{8,9},{9,8},{10,11... | collective-permute-start | bytes 921608 | tf_op jit(solution)/shard_map/ppermute | solution.py:263
  23.4 2.6 %collective-permute-start.7 = (bf16[144,768]{1,0:T(8,128)(2,1)S(1)}, bf16[144,768]{1,0:T(8,128)(2,1)S(1)}, u32[]{:S(2)}, u32[]{:S(2)}) collective-permute-start(bf16[144,768]{1,0:T(8,128)(2,1)S(1)} %collective-permute-done.6.refs_4_), channel_id=1, source_target_pairs={{0,1},{1,0},{2,3},{3,2},{4,5},{5,4},{6,7},{7,6},{8,9},{9,8},{10,11... | collective-permute-start | bytes 663560 | tf_op jit(solution)/shard_map/ppermute | solution.py:263
  25.9 1.9 %collective-permute-start.11 = (bf16[216,768]{1,0:T(8,128)(2,1)S(1)}, bf16[216,768]{1,0:T(8,128)(2,1)S(1)}, u32[]{:S(2)}, u32[]{:S(2)}) collective-permute-start(bf16[216,768]{1,0:T(8,128)(2,1)S(1)} %shard_map.34.refs_4_), channel_id=1, source_target_pairs={{0,1},{1,0},{2,3},{3,2},{4,5},{5,4},{6,7},{7,6},{8,9},{9,8},{10,11... | collective-permute-start | bytes 995336 | tf_op jit(solution)/shard_map/ppermute | solution.py:263

commit v3 on v2

--- a/solution.py
+++ b/solution.py
@@ -40,13 +40,15 @@
     )(*args, *after)
 
 
-def label_kernel(points_ref, labels_ref, out_ref):
+def label_kernel(points_ref, assign_ref, out_ref):
     own_count, width = points_ref.shape
+    assign = assign_ref[...]
+    group_of = assign // CL_DEV
     out_ref[:own_count, :] = points_ref[...]
     out_ref[own_count:, :] = jnp.zeros((ID_ROWS, width), jnp.bfloat16)
-    for n in range(2):
-        out_ref[own_count:, n * CL_DEV : n * CL_DEV + own_count] = jnp.broadcast_to(
-            labels_ref[n : n + 1, :].astype(jnp.float32), (ID_ROWS, own_count)
+    for start, labels in ((0, group_of), (CL_DEV, assign - group_of * CL_DEV)):
+        out_ref[own_count:, start : start + own_count] = jnp.broadcast_to(
+            labels.astype(jnp.float32), (ID_ROWS, own_count)
         ).astype(jnp.bfloat16)
 
 
@@ -120,9 +122,9 @@
         place += in_ref.shape[0]
 
 
-def stack(*arrays, after=()):
+def stack(*arrays, after=(), cost=None):
     rows = sum(one.shape[0] for one in arrays)
-    return call(stack_kernel, [bf16(rows, arrays[0].shape[1])], arrays, after=after)[0]
+    return call(stack_kernel, [bf16(rows, arrays[0].shape[1])], arrays, after=after, cost=cost)[0]
 
 
 def kern(rows, slots, slot_norms):
@@ -235,7 +237,7 @@
         ],
         arrays,
         mib=32,
-        cost=cost_of(3 * (rows + slots), slots, width),
+        cost=cost_of(1 * (rows + slots), slots, width),
     )
 
 
@@ -262,44 +264,36 @@
     def over_col(values, bits):
         return lax.ppermute(values, "col", [(i, i ^ bits) for i in range(group_count)])
 
-    def over_row(values, bits_of):
-        pairs = [
-            (r * group_count + c, (r ^ bits_of(c)) * group_count + c)
-            for r in range(row_count)
-            for c in range(group_count)
-        ]
-        return lax.ppermute(values, ("row", "col"), pairs)
-
-    def in_steps(sets, here):
-        steps = row_count.bit_length() - 1
-        for step in range(steps):
-            got = over_row(sets, lambda c: 1 << (step if c % 2 == 0 else steps - 1 - step))
-            if step < steps - 1:
-                sets, here = stack(sets, got), stack(here, got)
-        return here, got
-
-    def at_once(sets, here):
-        got = [over_row(sets, lambda c: bits) for bits in range(row_count - 1, 0, -1)]
-        return here, stack(*got)
-
-    group_of = assign // CL_DEV
-    labels = jnp.stack([group_of, assign - group_of * CL_DEV])
-    [labelled] = call(label_kernel, [bf16(own_count + ID_ROWS, width)], [points, labels])
-    blocks = {0: labelled}
-    bit = chips // 2
+    def over_row(values, bits):
+        return lax.ppermute(values, "row", [(i, i ^ bits) for i in range(row_count)])
+
+    def pending(one, flops):
+        return stack(one, cost=pl.CostEstimate(flops=int(flops), bytes_accessed=0, transcendentals=0))
+
+    def label(values, ids):
+        return call(label_kernel, [bf16(own_count + ID_ROWS, width)], [values, ids])[0]
+
+    assign = assign.reshape(1, own_count)
+    far = chips // 2
+    blocks = {0: label(points, assign)}
+    for q in sorted({far, 1}, reverse=True):
+        blocks[q] = label(pending(over_col(points, 2 * q), 1e8 if q > 1 else 4e9), over_col(assign, 2 * q))
+    bit = far // 2
     while bit:
-        blocks |= {q + bit: over_col(one, 2 * bit) for q, one in blocks.items()}
+        for q in range(0, chips, 2 * bit):
+            if q + bit not in blocks:
+                blocks[q + bit] = pending(over_col(blocks[q], 2 * bit), 1e9)
         bit //= 2
     places, near, last = [], [], []
-    for batch, share in ((range(2), in_steps), (range(2, chips), at_once)):
+    for batch in (range(2), range(2, chips)):
         base, half = len(batch) * own_count, len(batch) * slots
         here, sets = call(
             functools.partial(select_kernel, slots),
             [bf16(base + 2 * half + ID_ROWS, width), bf16(2 * half + ID_ROWS, width)],
             [blocks[q] for q in batch],
-            after=[one[0] for one in near],
+            after=[] if last else [blocks[far]],
         )
-        here, got = share(sets, here)
+        got = [over_row(sets, bits) for bits in range(row_count - 1, 0, -1)]
         places.append([2 * q for q in batch])
         near.append((here, base, half))
         last.append((got, 0, half))
@@ -308,10 +302,13 @@
         return [(one, base, half, False), (over_col(one, 1), base, half, True)]
 
     pairs = [both_cores(*one) for one in near]
-    old = [pair[0] for pair in pairs] + [pair[1] for pair in pairs] + both_cores(*last[0])
+    got, base, half = last[0]
+    first = both_cores(stack(*got), base, half)
+    old = [pair[0] for pair in pairs] + [pair[1] for pair in pairs] + first
     order = [q for side in range(2) for batch in places for q in (one ^ side for one in batch)]
     sums = sum_slots(old)
-    return finish(order, sums, both_cores(*last[1]))
+    got, base, half = last[1]
+    return finish(order, sums, both_cores(stack(*got), base, half))
 
 
 def solution(mesh):

time: 29.8 us -> 28.4 us (0.953)
  waiting for transfers between devices: 8.32 us -> 6.99 us
  other arithmetic: 0.68 us -> 0 us
  local copies, waits for them, and re-layouts: 0.89 us -> 1.55 us
    ppermute x5 -> x6, waiting for transfers between devices: 4.87 us -> 3.48 us  [over_row(): lax.ppermute(values, 'row', [(i, i ^ bits) for i in range(row_count)])]
    ppermute x5 -> x6, starting transfers between devices: 8.51 us -> 7.79 us  [over_row(): lax.ppermute(values, 'row', [(i, i ^ bits) for i in range(row_count)])]
    ppermute x7 -> x9, starting transfers between devices: 6.71 us -> 7.39 us  [over_col(): lax.ppermute(values, 'col', [(i, i ^ bits) for i in range(group_count)])]
    another operation x2 -> x0, other arithmetic: 0.68 us -> none  [per_device(): labels = jnp.stack([group_of, assign - group_of * CL_DEV])]
    unnamed x2 -> x4, local copies, waits for them, and re-layouts: 0.89 us -> 1.55 us
    ppermute x7 -> x9, waiting for transfers between devices: 3.45 us -> 3.51 us  [over_col(): lax.ppermute(values, 'col', [(i, i ^ bits) for i in range(group_count)])]
    pallas_call x8 -> x12, Pallas kernels: 4.44 us -> 4.48 us  [call(): pl.pallas_call(body, out_shape=out_shape, in_specs=[VMEM] * count + [pl.B...]
  transfers between devices with their start and end apart: 12 -> 15, of which waited for: 7 -> 7; matrix products, arithmetic and copies ran while one was open for 0% -> 0% of each run, Pallas kernels for 9% -> 9%
where the time goes in v3:
time: 28.4 us; the launch traced here: 28.3 us
  starting transfers between devices  15.2 us (54%)
  waiting for transfers between devices  6.99 us (25%)
  Pallas kernels  4.48 us (16%)
  local copies, waits for them, and re-layouts  1.55 us (5%)
    ppermute x6, starting transfers between devices, over_row(): lax.ppermute(values, 'row', [(i, i ^ bits) for i in range(row_count)])  7.79 us
    ppermute x9, starting transfers between devices, over_col(): lax.ppermute(values, 'col', [(i, i ^ bits) for i in range(group_count)])  7.39 us
    pallas_call x12, Pallas kernels, call(): pl.pallas_call(body, out_shape=out_shape, in_specs=[VMEM] * count + [pl.B...  4.48 us
    ppermute x9, waiting for transfers between devices, over_col(): lax.ppermute(values, 'col', [(i, i ^ bits) for i in range(group_count)])  3.51 us
    ppermute x6, waiting for transfers between devices, over_row(): lax.ppermute(values, 'row', [(i, i ^ bits) for i in range(row_count)])  3.48 us
    unnamed x4, local copies, waits for them, and re-layouts  1.55 us
  transfers between devices with their start and end apart: 15, of which 7 were waited for; matrix products, arithmetic and copies ran while one was open for 0% of the time, Pallas kernels for 9%

profile of v3, /device:TPU:0, one launch (start us, length us, event | category | flops | bytes accessed | tf_op | source)
XLA Modules:
  0.0 28.3 jit_solution(10186437675779470540)
XLA Ops:
  0.0 4.0 %collective-permute-start.2 = (bf16[64,768]{1,0:T(8,128)(2,1)}, bf16[64,768]{1,0:T(8,128)(2,1)S(1)}, u32[]{:S(2)}, u32[]{:S(2)}) collective-permute-start(bf16[64,768]{1,0:T(8,128)(2,1)} %refs_0_.1), channel_id=1, source_target_pairs={{0,4},{1,5},{2,6},{3,7},{4,0},{5,1},{6,2},{7,3},{8,12},{9,13},{10,... | collective-permute-start | bytes 294920 | tf_op jit(solution)/shard_map/ppermute | solution.py:265
  4.0 1.6 %collective-permute-start = (bf16[64,768]{1,0:T(8,128)(2,1)}, bf16[64,768]{1,0:T(8,128)(2,1)S(1)}, u32[]{:S(2)}, u32[]{:S(2)}) collective-permute-start(bf16[64,768]{1,0:T(8,128)(2,1)} %refs_0_.1), channel_id=1, source_target_pairs={{0,2},{1,3},{2,0},{3,1},{4,6},{5,7},{6,4},{7,5},{8,10},{9,11},{10,... | collective-permute-start | bytes 294920 | tf_op jit(solution)/shard_map/ppermute | solution.py:265
  5.6 0.3 %collective-permute-start.3 = (s32[1,64]{1,0:T(1,128)}, s32[1,64]{1,0:T(1,128)S(1)}, u32[]{:S(2)}, u32[]{:S(2)}) collective-permute-start(s32[1,64]{1,0:T(1,128)} %bitcast.1), channel_id=1, source_target_pairs={{0,4},{1,5},{2,6},{3,7},{4,0},{5,1},{6,2},{7,3},{8,12},{9,13},{10,... | collective-permute-start | bytes 776 | tf_op jit(solution)/shard_map/ppermute | solution.py:265
  6.0 0.1 collective-permute-start.1
  6.1 0.0 copy-start
  6.1 0.9 %copy-done = bf16[64,768]{1,0:T(8,128)(2,1)S(1)} copy-done((bf16[64,768]{1,0:T(8,128)(2,1)S(1)}, bf16[64,768]{1,0:T(8,128)(2,1)}, u32[]{:S(2)}) %copy-start) | copy-done | bytes 98328
  7.0 0.0 copy-start.1
  7.0 0.7 %copy-done.1 = s32[64]{0:T(128)S(1)} copy-done((s32[64]{0:T(128)S(1)}, s32[64]{0:T(128)}, u32[]{:S(2)}) %copy-start.1) | copy-done | bytes 280
  7.6 1.4 %collective-permute-done.2.refs_0_ = bf16[64,768]{1,0:T(8,128)(2,1)S(1)} collective-permute-done((bf16[64,768]{1,0:T(8,128)(2,1)}, bf16[64,768]{1,0:T(8,128)(2,1)S(1)}, u32[]{:S(2)}, u32[]{:S(2)}) %collective-permute-start.2) | collective-permute-done | bytes 98336 | tf_op jit(solution)/shard_map/ppermute | solution.py:265
  9.1 1.1 %collective-permute-done.3.refs_1_ = s32[1,64]{1,0:T(1,128)S(1)} collective-permute-done((s32[1,64]{1,0:T(1,128)}, s32[1,64]{1,0:T(1,128)S(1)}, u32[]{:S(2)}, u32[]{:S(2)}) %collective-permute-start.3) | collective-permute-done | bytes 288 | tf_op jit(solution)/shard_map/ppermute | solution.py:265
  10.2 0.7 %collective-permute-start.4 = (bf16[72,768]{1,0:T(8,128)(2,1)S(1)}, bf16[72,768]{1,0:T(8,128)(2,1)S(1)}, u32[]{:S(2)}, u32[]{:S(2)}) collective-permute-start(bf16[72,768]{1,0:T(8,128)(2,1)S(1)} %shard_map.32.refs_2_.refs_0_), channel_id=1, source_target_pairs={{0,2},{1,3},{2,0},{3,1},{4,6},{5,7},{6,4},{7,5},{8,10},{9,11},{10,... | collective-permute-start | bytes 331784 | tf_op jit(solution)/shard_map/ppermute | solution.py:265
  10.9 0.0 collective-permute-done.refs_0_
  10.9 0.0 collective-permute-done.1.refs_1_
  10.9 0.4 %shard_map.33 = (bf16[200,768]{1,0:T(8,128)(2,1)S(1)}, bf16[72,768]{1,0:T(8,128)(2,1)S(1)}) custom-call(bf16[72,768]{1,0:T(8,128)(2,1)S(1)} %shard_map.28.refs_0_, bf16[72,768]{1,0:T(8,128)(2,1)S(1)} %shard_map.30.refs_1_, bf16[72,768]{1,0:T(8,128)(2,1)S(1)} %shard_map.32.refs_2_.refs_0_), custom_call_target="tpu_custom_call" | custom-call | tf_op jit(solution)/shard_map/pallas_call | solution.py:32
  11.3 2.5 %collective-permute-start.7 = (bf16[72,768]{1,0:T(8,128)(2,1)S(1)}, bf16[72,768]{1,0:T(8,128)(2,1)S(1)}, u32[]{:S(2)}, u32[]{:S(2)}) collective-permute-start(bf16[72,768]{1,0:T(8,128)(2,1)S(1)} %get-tuple-element.15), channel_id=1, source_target_pairs={{0,24},{8,16},{16,8},{24,0},{1,25},{9,17},{17,9},{25,1},{2,26},{10... | collective-permute-start | bytes 331784 | tf_op jit(solution)/shard_map/ppermute | solution.py:268
  13.8 0.5 %collective-permute-start.8 = (bf16[72,768]{1,0:T(8,128)(2,1)S(1)}, bf16[72,768]{1,0:T(8,128)(2,1)S(1)}, u32[]{:S(2)}, u32[]{:S(2)}) collective-permute-start(bf16[72,768]{1,0:T(8,128)(2,1)S(1)} %get-tuple-element.15), channel_id=1, source_target_pairs={{0,16},{8,24},{16,0},{24,8},{1,17},{9,25},{17,1},{25,9},{2,18},{10... | collective-permute-start | bytes 331784 | tf_op jit(solution)/shard_map/ppermute | solution.py:268
  14.3 0.6 %collective-permute-start.9 = (bf16[72,768]{1,0:T(8,128)(2,1)S(1)}, bf16[72,768]{1,0:T(8,128)(2,1)S(1)}, u32[]{:S(2)}, u32[]{:S(2)}) collective-permute-start(bf16[72,768]{1,0:T(8,128)(2,1)S(1)} %get-tuple-element.15), channel_id=1, source_target_pairs={{0,8},{8,0},{16,24},{24,16},{1,9},{9,1},{17,25},{25,17},{2,10},{10... | collective-permute-start | bytes 331784 | tf_op jit(solution)/shard_map/ppermute | solution.py:268
  14.9 0.1 collective-permute-done.4.refs_0_
  15.0 0.4 %shard_map.35 = (bf16[200,768]{1,0:T(8,128)(2,1)S(1)}, bf16[72,768]{1,0:T(8,128)(2,1)S(1)}) custom-call(bf16[72,768]{1,0:T(8,128)(2,1)S(1)} %shard_map.32.refs_2_.refs_0_, bf16[72,768]{1,0:T(8,128)(2,1)S(1)} %shard_map.34.refs_1_), custom_call_target="tpu_custom_call" | custom-call | tf_op jit(solution)/shard_map/pallas_call | solution.py:32
  15.4 2.5 %collective-permute-start.11 = (bf16[72,768]{1,0:T(8,128)(2,1)S(1)}, bf16[72,768]{1,0:T(8,128)(2,1)S(1)}, u32[]{:S(2)}, u32[]{:S(2)}) collective-permute-start(bf16[72,768]{1,0:T(8,128)(2,1)S(1)} %get-tuple-element.20), channel_id=1, source_target_pairs={{0,24},{8,16},{16,8},{24,0},{1,25},{9,17},{17,9},{25,1},{2,26},{10... | collective-permute-start | bytes 331784 | tf_op jit(solution)/shard_map/ppermute | solution.py:268
  17.9 0.5 %collective-permute-start.12 = (bf16[72,768]{1,0:T(8,128)(2,1)S(1)}, bf16[72,768]{1,0:T(8,128)(2,1)S(1)}, u32[]{:S(2)}, u32[]{:S(2)}) collective-permute-start(bf16[72,768]{1,0:T(8,128)(2,1)S(1)} %get-tuple-element.20), channel_id=1, source_target_pairs={{0,16},{8,24},{16,0},{24,8},{1,17},{9,25},{17,1},{25,9},{2,18},{10... | collective-permute-start | bytes 331784 | tf_op jit(solution)/shard_map/ppermute | solution.py:268
  18.4 0.0 collective-permute-done.7.refs_0_
  18.4 1.2 %collective-permute-start.13 = (bf16[72,768]{1,0:T(8,128)(2,1)S(1)}, bf16[72,768]{1,0:T(8,128)(2,1)S(1)}, u32[]{:S(2)}, u32[]{:S(2)}) collective-permute-start(bf16[72,768]{1,0:T(8,128)(2,1)S(1)} %get-tuple-element.20), channel_id=1, source_target_pairs={{0,8},{8,0},{16,24},{24,16},{1,9},{9,1},{17,25},{25,17},{2,10},{10... | collective-permute-start | bytes 331784 | tf_op jit(solution)/shard_map/ppermute | solution.py:268
  19.7 1.2 %collective-permute-done.8.refs_1_ = bf16[72,768]{1,0:T(8,128)(2,1)S(1)} collective-permute-done((bf16[72,768]{1,0:T(8,128)(2,1)S(1)}, bf16[72,768]{1,0:T(8,128)(2,1)S(1)}, u32[]{:S(2)}, u32[]{:S(2)}) %collective-permute-start.8) | collective-permute-done | bytes 110624 | tf_op jit(solution)/shard_map/ppermute | solution.py:268
  20.9 0.0 collective-permute-done.9.refs_2_
  20.9 0.1 collective-permute-start.10
  21.0 0.5 %collective-permute-start.5 = (bf16[200,768]{1,0:T(8,128)(2,1)S(1)}, bf16[200,768]{1,0:T(8,128)(2,1)S(1)}, u32[]{:S(2)}, u32[]{:S(2)}) collective-permute-start(bf16[200,768]{1,0:T(8,128)(2,1)S(1)} %get-tuple-element.13.refs_0_), channel_id=1, source_target_pairs={{0,1},{1,0},{2,3},{3,2},{4,5},{5,4},{6,7},{7,6},{8,9},{9,8},{10,11... | collective-permute-start | bytes 921608 | tf_op jit(solution)/shard_map/ppermute | solution.py:265
  21.5 1.6 %collective-permute-done.11.refs_0_ = bf16[72,768]{1,0:T(8,128)(2,1)S(1)} collective-permute-done((bf16[72,768]{1,0:T(8,128)(2,1)S(1)}, bf16[72,768]{1,0:T(8,128)(2,1)S(1)}, u32[]{:S(2)}, u32[]{:S(2)}) %collective-permute-start.11) | collective-permute-done | bytes 110624 | tf_op jit(solution)/shard_map/ppermute | solution.py:268
  23.1 0.0 collective-permute-start.6
  23.1 0.7 %collective-permute-done.12.refs_1_ = bf16[72,768]{1,0:T(8,128)(2,1)S(1)} collective-permute-done((bf16[72,768]{1,0:T(8,128)(2,1)S(1)}, bf16[72,768]{1,0:T(8,128)(2,1)S(1)}, u32[]{:S(2)}, u32[]{:S(2)}) %collective-permute-start.12) | collective-permute-done | bytes 110624 | tf_op jit(solution)/shard_map/ppermute | solution.py:268
  23.7 0.0 collective-permute-done.13.refs_2_
  23.8 0.1 collective-permute-start.14
  23.8 0.0 collective-permute-done.5.refs_2_
  23.9 0.8 %collective-permute-done.6.refs_3_ = bf16[200,768]{1,0:T(8,128)(2,1)S(1)} collective-permute-done((bf16[200,768]{1,0:T(8,128)(2,1)S(1)}, bf16[200,768]{1,0:T(8,128)(2,1)S(1)}, u32[]{:S(2)}, u32[]{:S(2)}) %collective-permute-start.6) | collective-permute-done | bytes 307232 | tf_op jit(solution)/shard_map/ppermute | solution.py:265
  24.7 0.0 collective-permute-done.10.refs_5_
  24.7 1.8 %shard_map.37 = (bf16[832,768]{1,0:T(8,128)(2,1)S(1)}, bf16[128,320]{1,0:T(8,128)(2,1)S(1)}, f32[512,128]{1,0:T(8,128)S(1)}, f32[16,128]{1,0:T(8,128)S(1)}) custom-call(bf16[200,768]{1,0:T(8,128)(2,1)S(1)} %get-tuple-element.13.refs_0_, bf16[200,768]{1,0:T(8,128)(2,1)S(1)} %get-tuple-element.14.refs_1_, bf16[200,768]{1,0:T(8,128)(2,1)S(1)} %collective-permute-done.5.refs_2_, ...), custom_call_target="tpu_custom_call" | custom-call | flops 477102080 | bytes 1277952 | tf_op jit(solution)/shard_map/pallas_call | solution.py:32
  26.5 0.0 collective-permute-done.14.refs_5_
  26.5 1.8 %shard_map.39 = f32[512,128]{1,0:T(8,128)} custom-call(bf16[832,768]{1,0:T(8,128)(2,1)S(1)} %get-tuple-element.16.refs_0_, bf16[128,320]{1,0:T(8,128)(2,1)S(1)} %get-tuple-element.17.refs_1_, f32[512,128]{1,0:T(8,128)S(1)} %get-tuple-element.18.refs_2_, f32[16,128]{1,0:T(8,128)S(1)} %get-tuple-element.19.refs_3_, bf16[216,768]{1,0:T(8,128)(2,1)S(1)} %shard_map.38.refs_4_, ...), custom_call_target="tpu_custom_call" | custom-call | flops 352321536 | bytes 1572864 | tf_op jit(solution)/shard_map/pallas_call | solution.py:32
  (8 shorter events, 0.1 us)
Async XLA Ops:
  0.0 9.0 %collective-permute-start.2 = (bf16[64,768]{1,0:T(8,128)(2,1)}, bf16[64,768]{1,0:T(8,128)(2,1)S(1)}, u32[]{:S(2)}, u32[]{:S(2)}) collective-permute-start(bf16[64,768]{1,0:T(8,128)(2,1)} %refs_0_.1), channel_id=1, source_target_pairs={{0,4},{1,5},{2,6},{3,7},{4,0},{5,1},{6,2},{7,3},{8,12},{9,13},{10,... | collective-permute-start | bytes 294920 | tf_op jit(solution)/shard_map/ppermute | solution.py:265
  4.0 6.9 %collective-permute-start = (bf16[64,768]{1,0:T(8,128)(2,1)}, bf16[64,768]{1,0:T(8,128)(2,1)S(1)}, u32[]{:S(2)}, u32[]{:S(2)}) collective-permute-start(bf16[64,768]{1,0:T(8,128)(2,1)} %refs_0_.1), channel_id=1, source_target_pairs={{0,2},{1,3},{2,0},{3,1},{4,6},{5,7},{6,4},{7,5},{8,10},{9,11},{10,... | collective-permute-start | bytes 294920 | tf_op jit(solution)/shard_map/ppermute | solution.py:265
  5.6 4.6 %collective-permute-start.3 = (s32[1,64]{1,0:T(1,128)}, s32[1,64]{1,0:T(1,128)S(1)}, u32[]{:S(2)}, u32[]{:S(2)}) collective-permute-start(s32[1,64]{1,0:T(1,128)} %bitcast.1), channel_id=1, source_target_pairs={{0,4},{1,5},{2,6},{3,7},{4,0},{5,1},{6,2},{7,3},{8,12},{9,13},{10,... | collective-permute-start | bytes 776 | tf_op jit(solution)/shard_map/ppermute | solution.py:265
  6.0 5.0 %collective-permute-start.1 = (s32[1,64]{1,0:T(1,128)}, s32[1,64]{1,0:T(1,128)S(1)}, u32[]{:S(2)}, u32[]{:S(2)}) collective-permute-start(s32[1,64]{1,0:T(1,128)} %bitcast.2), channel_id=1, source_target_pairs={{0,2},{1,3},{2,0},{3,1},{4,6},{5,7},{6,4},{7,5},{8,10},{9,11},{10,... | collective-permute-start | bytes 776 | tf_op jit(solution)/shard_map/ppermute | solution.py:265
  6.1 0.9 %copy-start = (bf16[64,768]{1,0:T(8,128)(2,1)S(1)}, bf16[64,768]{1,0:T(8,128)(2,1)}, u32[]{:S(2)}) copy-start(bf16[64,768]{1,0:T(8,128)(2,1)} %refs_0_.1) | copy-start | bytes 294916
  7.0 0.7 %copy-start.1 = (s32[64]{0:T(128)S(1)}, s32[64]{0:T(128)}, u32[]{:S(2)}) copy-start(s32[64]{0:T(128)} %param.3) | copy-start | bytes 772
  10.2 4.8 %collective-permute-start.4 = (bf16[72,768]{1,0:T(8,128)(2,1)S(1)}, bf16[72,768]{1,0:T(8,128)(2,1)S(1)}, u32[]{:S(2)}, u32[]{:S(2)}) collective-permute-start(bf16[72,768]{1,0:T(8,128)(2,1)S(1)} %shard_map.32.refs_2_.refs_0_), channel_id=1, source_target_pairs={{0,2},{1,3},{2,0},{3,1},{4,6},{5,7},{6,4},{7,5},{8,10},{9,11},{10,... | collective-permute-start | bytes 331784 | tf_op jit(solution)/shard_map/ppermute | solution.py:265
  11.3 7.1 %collective-permute-start.7 = (bf16[72,768]{1,0:T(8,128)(2,1)S(1)}, bf16[72,768]{1,0:T(8,128)(2,1)S(1)}, u32[]{:S(2)}, u32[]{:S(2)}) collective-permute-start(bf16[72,768]{1,0:T(8,128)(2,1)S(1)} %get-tuple-element.15), channel_id=1, source_target_pairs={{0,24},{8,16},{16,8},{24,0},{1,25},{9,17},{17,9},{25,1},{2,26},{10... | collective-permute-start | bytes 331784 | tf_op jit(solution)/shard_map/ppermute | solution.py:268
  13.8 7.1 %collective-permute-start.8 = (bf16[72,768]{1,0:T(8,128)(2,1)S(1)}, bf16[72,768]{1,0:T(8,128)(2,1)S(1)}, u32[]{:S(2)}, u32[]{:S(2)}) collective-permute-start(bf16[72,768]{1,0:T(8,128)(2,1)S(1)} %get-tuple-element.15), channel_id=1, source_target_pairs={{0,16},{8,24},{16,0},{24,8},{1,17},{9,25},{17,1},{25,9},{2,18},{10... | collective-permute-start | bytes 331784 | tf_op jit(solution)/shard_map/ppermute | solution.py:268
  14.3 6.6 %collective-permute-start.9 = (bf16[72,768]{1,0:T(8,128)(2,1)S(1)}, bf16[72,768]{1,0:T(8,128)(2,1)S(1)}, u32[]{:S(2)}, u32[]{:S(2)}) collective-permute-start(bf16[72,768]{1,0:T(8,128)(2,1)S(1)} %get-tuple-element.15), channel_id=1, source_target_pairs={{0,8},{8,0},{16,24},{24,16},{1,9},{9,1},{17,25},{25,17},{2,10},{10... | collective-permute-start | bytes 331784 | tf_op jit(solution)/shard_map/ppermute | solution.py:268
  15.4 7.7 %collective-permute-start.11 = (bf16[72,768]{1,0:T(8,128)(2,1)S(1)}, bf16[72,768]{1,0:T(8,128)(2,1)S(1)}, u32[]{:S(2)}, u32[]{:S(2)}) collective-permute-start(bf16[72,768]{1,0:T(8,128)(2,1)S(1)} %get-tuple-element.20), channel_id=1, source_target_pairs={{0,24},{8,16},{16,8},{24,0},{1,25},{9,17},{17,9},{25,1},{2,26},{10... | collective-permute-start | bytes 331784 | tf_op jit(solution)/shard_map/ppermute | solution.py:268
  17.9 5.8 %collective-permute-start.12 = (bf16[72,768]{1,0:T(8,128)(2,1)S(1)}, bf16[72,768]{1,0:T(8,128)(2,1)S(1)}, u32[]{:S(2)}, u32[]{:S(2)}) collective-permute-start(bf16[72,768]{1,0:T(8,128)(2,1)S(1)} %get-tuple-element.20), channel_id=1, source_target_pairs={{0,16},{8,24},{16,0},{24,8},{1,17},{9,25},{17,1},{25,9},{2,18},{10... | collective-permute-start | bytes 331784 | tf_op jit(solution)/shard_map/ppermute | solution.py:268
  18.4 5.3 %collective-permute-start.13 = (bf16[72,768]{1,0:T(8,128)(2,1)S(1)}, bf16[72,768]{1,0:T(8,128)(2,1)S(1)}, u32[]{:S(2)}, u32[]{:S(2)}) collective-permute-start(bf16[72,768]{1,0:T(8,128)(2,1)S(1)} %get-tuple-element.20), channel_id=1, source_target_pairs={{0,8},{8,0},{16,24},{24,16},{1,9},{9,1},{17,25},{25,17},{2,10},{10... | collective-permute-start | bytes 331784 | tf_op jit(solution)/shard_map/ppermute | solution.py:268
  20.9 3.8 %collective-permute-start.10 = (bf16[216,768]{1,0:T(8,128)(2,1)S(1)}, bf16[216,768]{1,0:T(8,128)(2,1)S(1)}, u32[]{:S(2)}, u32[]{:S(2)}) collective-permute-start(bf16[216,768]{1,0:T(8,128)(2,1)S(1)} %shard_map.36.refs_4_), channel_id=1, source_target_pairs={{0,1},{1,0},{2,3},{3,2},{4,5},{5,4},{6,7},{7,6},{8,9},{9,8},{10,11... | collective-permute-start | bytes 995336 | tf_op jit(solution)/shard_map/ppermute | solution.py:265
  21.0 2.9 %collective-permute-start.5 = (bf16[200,768]{1,0:T(8,128)(2,1)S(1)}, bf16[200,768]{1,0:T(8,128)(2,1)S(1)}, u32[]{:S(2)}, u32[]{:S(2)}) collective-permute-start(bf16[200,768]{1,0:T(8,128)(2,1)S(1)} %get-tuple-element.13.refs_0_), channel_id=1, source_target_pairs={{0,1},{1,0},{2,3},{3,2},{4,5},{5,4},{6,7},{7,6},{8,9},{9,8},{10,11... | collective-permute-start | bytes 921608 | tf_op jit(solution)/shard_map/ppermute | solution.py:265
  23.1 1.6 %collective-permute-start.6 = (bf16[200,768]{1,0:T(8,128)(2,1)S(1)}, bf16[200,768]{1,0:T(8,128)(2,1)S(1)}, u32[]{:S(2)}, u32[]{:S(2)}) collective-permute-start(bf16[200,768]{1,0:T(8,128)(2,1)S(1)} %get-tuple-element.14.refs_1_), channel_id=1, source_target_pairs={{0,1},{1,0},{2,3},{3,2},{4,5},{5,4},{6,7},{7,6},{8,9},{9,8},{10,11... | collective-permute-start | bytes 921608 | tf_op jit(solution)/shard_map/ppermute | solution.py:265
  23.8 2.7 %collective-permute-start.14 = (bf16[216,768]{1,0:T(8,128)(2,1)S(1)}, bf16[216,768]{1,0:T(8,128)(2,1)S(1)}, u32[]{:S(2)}, u32[]{:S(2)}) collective-permute-start(bf16[216,768]{1,0:T(8,128)(2,1)S(1)} %shard_map.38.refs_4_), channel_id=1, source_target_pairs={{0,1},{1,0},{2,3},{3,2},{4,5},{5,4},{6,7},{7,6},{8,9},{9,8},{10,11... | collective-permute-start | bytes 995336 | tf_op jit(solution)/shard_map/ppermute | solution.py:265

commit v4 on v3

--- a/solution.py
+++ b/solution.py
@@ -9,6 +9,7 @@
 
 CL_DEV = 128
 ID_ROWS = 8
+LANES = 128
 NT = (((1,), (1,)), ((), ()))
 NN = (((1,), (0,)), ((), ()))
 VMEM = pl.BlockSpec(memory_space=pltpu.VMEM)
@@ -40,23 +41,34 @@
     )(*args, *after)
 
 
+def tall(rows):
+    return [rows[:, start : start + LANES] for start in range(0, rows.shape[1], LANES)]
+
+
+def put_tall(ref, base, rows):
+    count = rows.shape[0]
+    for t, piece in enumerate(tall(rows)):
+        ref[base + t * count : base + (t + 1) * count, :] = piece
+
+
 def label_kernel(points_ref, assign_ref, out_ref):
-    own_count, width = points_ref.shape
+    own_count = points_ref.shape[0]
     assign = assign_ref[...]
     group_of = assign // CL_DEV
-    out_ref[:own_count, :] = points_ref[...]
-    out_ref[own_count:, :] = jnp.zeros((ID_ROWS, width), jnp.bfloat16)
-    for start, labels in ((0, group_of), (CL_DEV, assign - group_of * CL_DEV)):
-        out_ref[own_count:, start : start + own_count] = jnp.broadcast_to(
+    put_tall(out_ref, 0, points_ref[...])
+    end = out_ref.shape[0] - ID_ROWS
+    out_ref[end:, :] = jnp.zeros((ID_ROWS, LANES), jnp.bfloat16)
+    for n, labels in enumerate((group_of, assign - group_of * CL_DEV)):
+        out_ref[end:, n * own_count : (n + 1) * own_count] = jnp.broadcast_to(
             labels.astype(jnp.float32), (ID_ROWS, own_count)
         ).astype(jnp.bfloat16)
 
 
 def select_kernel(slots, *refs):
-    *block_refs, local_ref, set_ref = refs
+    *block_refs, local_ref, set_ref, points_ref = refs
     count = len(block_refs)
-    own_count = block_refs[0].shape[0] - ID_ROWS
-    points = count * own_count
+    points, width = points_ref.shape
+    own_count = points // count
     half = count * slots
     me = lax.axis_index("col")
     earlier = (
@@ -67,9 +79,13 @@
     ids = jnp.zeros((ID_ROWS, 2 * half), jnp.float32)
     dispatch = []
     for n, block_ref in enumerate(block_refs):
-        local_ref[n * own_count : (n + 1) * own_count, :] = block_ref[:own_count, :]
-        group_of = block_ref[own_count:, :own_count].astype(jnp.float32).astype(jnp.int32)
-        labels = block_ref[own_count:, CL_DEV : CL_DEV + own_count].astype(jnp.float32) + 1.0
+        for t in range(width // LANES):
+            points_ref[n * own_count : (n + 1) * own_count, t * LANES : (t + 1) * LANES] = block_ref[
+                t * own_count : (t + 1) * own_count, :
+            ]
+        end = block_ref.shape[0] - ID_ROWS
+        group_of = block_ref[end:, :own_count].astype(jnp.float32).astype(jnp.int32)
+        labels = block_ref[end:, own_count : 2 * own_count].astype(jnp.float32) + 1.0
         relative = group_of ^ me
         member = lax.broadcasted_iota(jnp.int32, (ID_ROWS, own_count), 0) == relative
         rank = dot(member.astype(jnp.bfloat16), earlier, NN)
@@ -80,11 +96,12 @@
         chosen = (slot == target[:1]).astype(jnp.bfloat16)
         ids += dot(labels.astype(jnp.bfloat16), chosen, NT)
         dispatch.append(chosen)
-    rows = dot(jnp.concatenate(dispatch, axis=1), local_ref[:points, :], NN).astype(jnp.bfloat16)
-    for ref, start in ((local_ref, points), (set_ref, 0)):
-        end = start + 2 * half
-        ref[start:end, :] = rows
-        ref[end:, :] = jnp.zeros((ID_ROWS, ref.shape[1]), jnp.bfloat16)
+    rows = dot(jnp.concatenate(dispatch, axis=1), points_ref[...], NN).astype(jnp.bfloat16)
+    put_tall(local_ref, 0, points_ref[...])
+    for ref, start in ((local_ref, points * width // LANES), (set_ref, 0)):
+        end = ref.shape[0] - ID_ROWS
+        put_tall(ref, start, rows)
+        ref[end:, :] = jnp.zeros((ID_ROWS, LANES), jnp.bfloat16)
         ref[end:, : 2 * half] = ids.astype(jnp.bfloat16)
 
 
@@ -102,12 +119,15 @@
         self.ref, self.base, self.count = ref, base, count
         self.start = count if second else 0
 
-    def rows(self):
-        start = self.base + self.start
-        return self.ref[start : start + self.count, :]
-
-    def indicator(self):
-        base = self.base + 2 * self.count
+    def put(self, out_ref, place):
+        for t in range(out_ref.shape[1] // LANES):
+            start = self.base + 2 * t * self.count + self.start
+            out_ref[place : place + self.count, t * LANES : (t + 1) * LANES] = self.ref[
+                start : start + self.count, :
+            ]
+
+    def indicator(self, width):
+        base = self.base + 2 * self.count * width // LANES
         ids = self.ref[base : base + ID_ROWS, self.start : self.start + self.count]
         ids = ids.astype(jnp.float32).astype(jnp.int32)[:1]
         clusters = lax.broadcasted_iota(jnp.int32, (CL_DEV, self.count), 0)
@@ -147,16 +167,19 @@
 
 def sums_kernel(counts, parts, *refs):
     *array_refs, left_ref, hot_ref, sums_ref, totals_ref = refs
-    rows, total = sums_ref.shape[0], left_ref.shape[0]
+    rows, (total, width) = sums_ref.shape[0], left_ref.shape
     place = 0
     for array_ref, count in zip(array_refs, counts):
-        left_ref[place : place + count, :] = array_ref[:count, :]
+        for t in range(width // LANES):
+            left_ref[place : place + count, t * LANES : (t + 1) * LANES] = array_ref[
+                t * count : (t + 1) * count, :
+            ]
         place += count
     for n, *rest in parts:
         part = Half(array_refs[n], *rest)
         end = place + part.count
-        left_ref[place:end, :] = part.rows()
-        hot_ref[:, place - rows : end - rows] = part.indicator()
+        part.put(left_ref, place)
+        hot_ref[:, place - rows : end - rows] = part.indicator(width)
         place = end
     slots, hot = left_ref[rows:, :], hot_ref[...]
     norms = row_norms(left_ref.at[rows:])
@@ -180,8 +203,8 @@
     for n, *rest in parts:
         part = Half(array_refs[n], *rest)
         end = place + part.count
-        slots_ref[place:end, :] = part.rows()
-        hot_ref[:, place:end] = part.indicator()
+        part.put(slots_ref, place)
+        hot_ref[:, place:end] = part.indicator(slots_ref.shape[1])
         place = end
     slots, hot = slots_ref[...], hot_ref[...]
     norms = row_norms(slots_ref)
@@ -205,11 +228,11 @@
             out_ref[pl.ds(row, own_count), :] = part[b * own_count : (b + 1) * own_count]
 
 
-def parts_of(sets, arrays):
+def parts_of(sets, arrays, width):
     parts = []
     for one, base, count, second in sets:
         n = [array is one for array in arrays].index(True)
-        for start in range(base, one.shape[0], 2 * count + ID_ROWS):
+        for start in range(base, one.shape[0], 2 * count * width // LANES + ID_ROWS):
             parts.append((n, start, count, second))
     return parts
 
@@ -222,11 +245,11 @@
     )
 
 
-def sum_slots(sets):
+def sum_slots(sets, width):
     arrays = [one for one, *_ in sets]
-    counts = [base for _, base, *_ in sets if base]
-    parts = parts_of(sets, arrays)
-    width, rows, slots = arrays[0].shape[1], sum(counts), sum(part[2] for part in parts)
+    counts = [base * LANES // width for _, base, *_ in sets if base]
+    parts = parts_of(sets, arrays, width)
+    rows, slots = sum(counts), sum(part[2] for part in parts)
     return call(
         functools.partial(sums_kernel, counts, parts),
         [
@@ -241,10 +264,10 @@
     )
 
 
-def finish(order, sums, sets):
+def finish(order, sums, sets, width):
     arrays = [one for one, *_ in sets]
-    parts = parts_of(sets, arrays)
-    width, slots = arrays[0].shape[1], sum(part[2] for part in parts)
+    parts = parts_of(sets, arrays, width)
+    slots = sum(part[2] for part in parts)
     return call(
         functools.partial(distance_kernel, parts, order),
         [jax.ShapeDtypeStruct(sums[2].shape, jnp.float32)],
@@ -258,7 +281,7 @@
 def per_device(points, assign):
     own_count, width = points.shape
     group_count, row_count = lax.axis_size("col"), lax.axis_size("row")
-    chips = group_count // 2
+    chips, tiles = group_count // 2, width // LANES
     slots = max(2, 2 * own_count // group_count)
 
     def over_col(values, bits):
@@ -271,7 +294,7 @@
         return stack(one, cost=pl.CostEstimate(flops=int(flops), bytes_accessed=0, transcendentals=0))
 
     def label(values, ids):
-        return call(label_kernel, [bf16(own_count + ID_ROWS, width)], [values, ids])[0]
+        return call(label_kernel, [bf16(own_count * tiles + ID_ROWS, LANES)], [values, ids])[0]
 
     assign = assign.reshape(1, own_count)
     far = chips // 2
@@ -286,11 +309,13 @@
         bit //= 2
     places, near, last = [], [], []
     for batch in (range(2), range(2, chips)):
-        base, half = len(batch) * own_count, len(batch) * slots
+        base, half = len(batch) * own_count * tiles, len(batch) * slots
+        set_rows = 2 * half * tiles + ID_ROWS
         here, sets = call(
             functools.partial(select_kernel, slots),
-            [bf16(base + 2 * half + ID_ROWS, width), bf16(2 * half + ID_ROWS, width)],
+            [bf16(base + set_rows, LANES), bf16(set_rows, LANES)],
             [blocks[q] for q in batch],
+            [pltpu.VMEM((len(batch) * own_count, width), jnp.bfloat16)],
             after=[] if last else [blocks[far]],
         )
         got = [over_row(sets, bits) for bits in range(row_count - 1, 0, -1)]
@@ -306,9 +331,9 @@
     first = both_cores(stack(*got), base, half)
     old = [pair[0] for pair in pairs] + [pair[1] for pair in pairs] + first
     order = [q for side in range(2) for batch in places for q in (one ^ side for one in batch)]
-    sums = sum_slots(old)
+    sums = sum_slots(old, width)
     got, base, half = last[1]
-    return finish(order, sums, both_cores(stack(*got), base, half))
+    return finish(order, sums, both_cores(stack(*got), base, half), width)
 
 
 def solution(mesh):

time: 28.4 us -> 28 us (0.986)
  waiting for transfers between devices: 6.99 us -> 6.37 us
  Pallas kernels: 4.48 us -> 4.81 us
    ppermute x9, waiting for transfers between devices: 3.51 us -> 3.04 us  [over_col(): lax.ppermute(values, 'col', [(i, i ^ bits) for i in range(group_count)])]
    pallas_call x12, Pallas kernels: 4.48 us -> 4.81 us  [call(): pl.pallas_call(body, out_shape=out_shape, in_specs=[VMEM] * count + [pl.B...]
  transfers between devices with their start and end apart: 15 -> 15, of which waited for: 7 -> 6; matrix products, arithmetic and copies ran while one was open for 0% -> 0% of each run, Pallas kernels for 9% -> 11%
where the time goes in v4:
time: 28 us; the launch traced here: 27.8 us
  starting transfers between devices  15 us (54%)
  waiting for transfers between devices  6.37 us (23%)
  Pallas kernels  4.81 us (17%)
  local copies, waits for them, and re-layouts  1.55 us (6%)
    ppermute x6, starting transfers between devices, over_row(): lax.ppermute(values, 'row', [(i, i ^ bits) for i in range(row_count)])  7.67 us
    ppermute x9, starting transfers between devices, over_col(): lax.ppermute(values, 'col', [(i, i ^ bits) for i in range(group_count)])  7.33 us
    pallas_call x12, Pallas kernels, call(): pl.pallas_call(body, out_shape=out_shape, in_specs=[VMEM] * count + [pl.B...  4.81 us
    ppermute x6, waiting for transfers between devices, over_row(): lax.ppermute(values, 'row', [(i, i ^ bits) for i in range(row_count)])  3.33 us
    ppermute x9, waiting for transfers between devices, over_col(): lax.ppermute(values, 'col', [(i, i ^ bits) for i in range(group_count)])  3.04 us
    unnamed x4, local copies, waits for them, and re-layouts  1.55 us
  transfers between devices with their start and end apart: 15, of which 6 were waited for; matrix products, arithmetic and copies ran while one was open for 0% of the time, Pallas kernels for 11%

profile of v4, /device:TPU:0, one launch (start us, length us, event | category | flops | bytes accessed | tf_op | source)
XLA Modules:
  0.0 27.8 jit_solution(1744306675322255372)
XLA Ops:
  0.0 4.0 %collective-permute-start.2 = (bf16[64,768]{1,0:T(8,128)(2,1)}, bf16[64,768]{1,0:T(8,128)(2,1)S(1)}, u32[]{:S(2)}, u32[]{:S(2)}) collective-permute-start(bf16[64,768]{1,0:T(8,128)(2,1)} %refs_0_.1), channel_id=1, source_target_pairs={{0,4},{1,5},{2,6},{3,7},{4,0},{5,1},{6,2},{7,3},{8,12},{9,13},{10,... | collective-permute-start | bytes 294920 | tf_op jit(solution)/shard_map/ppermute | solution.py:288
  4.0 1.6 %collective-permute-start = (bf16[64,768]{1,0:T(8,128)(2,1)}, bf16[64,768]{1,0:T(8,128)(2,1)S(1)}, u32[]{:S(2)}, u32[]{:S(2)}) collective-permute-start(bf16[64,768]{1,0:T(8,128)(2,1)} %refs_0_.1), channel_id=1, source_target_pairs={{0,2},{1,3},{2,0},{3,1},{4,6},{5,7},{6,4},{7,5},{8,10},{9,11},{10,... | collective-permute-start | bytes 294920 | tf_op jit(solution)/shard_map/ppermute | solution.py:288
  5.6 0.3 %collective-permute-start.3 = (s32[1,64]{1,0:T(1,128)}, s32[1,64]{1,0:T(1,128)S(1)}, u32[]{:S(2)}, u32[]{:S(2)}) collective-permute-start(s32[1,64]{1,0:T(1,128)} %bitcast.1), channel_id=1, source_target_pairs={{0,4},{1,5},{2,6},{3,7},{4,0},{5,1},{6,2},{7,3},{8,12},{9,13},{10,... | collective-permute-start | bytes 776 | tf_op jit(solution)/shard_map/ppermute | solution.py:288
  6.0 0.1 collective-permute-start.1
  6.1 0.0 copy-start
  6.1 0.9 %copy-done = bf16[64,768]{1,0:T(8,128)(2,1)S(1)} copy-done((bf16[64,768]{1,0:T(8,128)(2,1)S(1)}, bf16[64,768]{1,0:T(8,128)(2,1)}, u32[]{:S(2)}) %copy-start) | copy-done | bytes 98328
  7.0 0.0 copy-start.1
  7.0 0.7 %copy-done.1 = s32[64]{0:T(128)S(1)} copy-done((s32[64]{0:T(128)S(1)}, s32[64]{0:T(128)}, u32[]{:S(2)}) %copy-start.1) | copy-done | bytes 280
  7.6 0.1 shard_map.28.refs_0_
  7.7 1.3 %collective-permute-done.2.refs_0_ = bf16[64,768]{1,0:T(8,128)(2,1)S(1)} collective-permute-done((bf16[64,768]{1,0:T(8,128)(2,1)}, bf16[64,768]{1,0:T(8,128)(2,1)S(1)}, u32[]{:S(2)}, u32[]{:S(2)}) %collective-permute-start.2) | collective-permute-done | bytes 98336 | tf_op jit(solution)/shard_map/ppermute | solution.py:288
  9.1 1.1 %collective-permute-done.3.refs_1_ = s32[1,64]{1,0:T(1,128)S(1)} collective-permute-done((s32[1,64]{1,0:T(1,128)}, s32[1,64]{1,0:T(1,128)S(1)}, u32[]{:S(2)}, u32[]{:S(2)}) %collective-permute-start.3) | collective-permute-done | bytes 288 | tf_op jit(solution)/shard_map/ppermute | solution.py:288
  10.2 0.1 shard_map.32.refs_2_.refs_0_
  10.3 0.6 %collective-permute-start.4 = (bf16[392,128]{1,0:T(8,128)(2,1)S(1)}, bf16[392,128]{1,0:T(8,128)(2,1)S(1)}, u32[]{:S(2)}, u32[]{:S(2)}) collective-permute-start(bf16[392,128]{1,0:T(8,128)(2,1)S(1)} %shard_map.32.refs_2_.refs_0_), channel_id=1, source_target_pairs={{0,2},{1,3},{2,0},{3,1},{4,6},{5,7},{6,4},{7,5},{8,10},{9,11},{10,... | collective-permute-start | bytes 301064 | tf_op jit(solution)/shard_map/ppermute | solution.py:288
  10.9 0.0 collective-permute-done.refs_0_
  10.9 0.0 collective-permute-done.1.refs_1_
  10.9 0.1 shard_map.30.refs_1_
  11.0 0.4 %shard_map.33 = (bf16[1160,128]{1,0:T(8,128)(2,1)S(1)}, bf16[392,128]{1,0:T(8,128)(2,1)S(1)}) custom-call(bf16[392,128]{1,0:T(8,128)(2,1)S(1)} %shard_map.28.refs_0_, bf16[392,128]{1,0:T(8,128)(2,1)S(1)} %shard_map.30.refs_1_, bf16[392,128]{1,0:T(8,128)(2,1)S(1)} %shard_map.32.refs_2_.refs_0_), custom_call_target="tpu_custom_call" | custom-call | tf_op jit(solution)/shard_map/pallas_call | solution.py:33
  11.4 2.5 %collective-permute-start.7 = (bf16[392,128]{1,0:T(8,128)(2,1)S(1)}, bf16[392,128]{1,0:T(8,128)(2,1)S(1)}, u32[]{:S(2)}, u32[]{:S(2)}) collective-permute-start(bf16[392,128]{1,0:T(8,128)(2,1)S(1)} %get-tuple-element.15), channel_id=1, source_target_pairs={{0,24},{8,16},{16,8},{24,0},{1,25},{9,17},{17,9},{25,1},{2,26},{10... | collective-permute-start | bytes 301064 | tf_op jit(solution)/shard_map/ppermute | solution.py:291
  13.9 0.5 %collective-permute-start.8 = (bf16[392,128]{1,0:T(8,128)(2,1)S(1)}, bf16[392,128]{1,0:T(8,128)(2,1)S(1)}, u32[]{:S(2)}, u32[]{:S(2)}) collective-permute-start(bf16[392,128]{1,0:T(8,128)(2,1)S(1)} %get-tuple-element.15), channel_id=1, source_target_pairs={{0,16},{8,24},{16,0},{24,8},{1,17},{9,25},{17,1},{25,9},{2,18},{10... | collective-permute-start | bytes 301064 | tf_op jit(solution)/shard_map/ppermute | solution.py:291
  14.4 0.6 %collective-permute-start.9 = (bf16[392,128]{1,0:T(8,128)(2,1)S(1)}, bf16[392,128]{1,0:T(8,128)(2,1)S(1)}, u32[]{:S(2)}, u32[]{:S(2)}) collective-permute-start(bf16[392,128]{1,0:T(8,128)(2,1)S(1)} %get-tuple-element.15), channel_id=1, source_target_pairs={{0,8},{8,0},{16,24},{24,16},{1,9},{9,1},{17,25},{25,17},{2,10},{10... | collective-permute-start | bytes 301064 | tf_op jit(solution)/shard_map/ppermute | solution.py:291
  14.9 0.0 collective-permute-done.4.refs_0_
  15.0 0.4 %shard_map.35 = (bf16[1160,128]{1,0:T(8,128)(2,1)S(1)}, bf16[392,128]{1,0:T(8,128)(2,1)S(1)}) custom-call(bf16[392,128]{1,0:T(8,128)(2,1)S(1)} %shard_map.32.refs_2_.refs_0_, bf16[392,128]{1,0:T(8,128)(2,1)S(1)} %shard_map.34.refs_1_), custom_call_target="tpu_custom_call" | custom-call | tf_op jit(solution)/shard_map/pallas_call | solution.py:33
  15.3 2.5 %collective-permute-start.11 = (bf16[392,128]{1,0:T(8,128)(2,1)S(1)}, bf16[392,128]{1,0:T(8,128)(2,1)S(1)}, u32[]{:S(2)}, u32[]{:S(2)}) collective-permute-start(bf16[392,128]{1,0:T(8,128)(2,1)S(1)} %get-tuple-element.20), channel_id=1, source_target_pairs={{0,24},{8,16},{16,8},{24,0},{1,25},{9,17},{17,9},{25,1},{2,26},{10... | collective-permute-start | bytes 301064 | tf_op jit(solution)/shard_map/ppermute | solution.py:291
  17.8 0.5 %collective-permute-start.12 = (bf16[392,128]{1,0:T(8,128)(2,1)S(1)}, bf16[392,128]{1,0:T(8,128)(2,1)S(1)}, u32[]{:S(2)}, u32[]{:S(2)}) collective-permute-start(bf16[392,128]{1,0:T(8,128)(2,1)S(1)} %get-tuple-element.20), channel_id=1, source_target_pairs={{0,16},{8,24},{16,0},{24,8},{1,17},{9,25},{17,1},{25,9},{2,18},{10... | collective-permute-start | bytes 301064 | tf_op jit(solution)/shard_map/ppermute | solution.py:291
  18.3 0.0 collective-permute-done.7.refs_0_
  18.3 1.1 %collective-permute-start.13 = (bf16[392,128]{1,0:T(8,128)(2,1)S(1)}, bf16[392,128]{1,0:T(8,128)(2,1)S(1)}, u32[]{:S(2)}, u32[]{:S(2)}) collective-permute-start(bf16[392,128]{1,0:T(8,128)(2,1)S(1)} %get-tuple-element.20), channel_id=1, source_target_pairs={{0,8},{8,0},{16,24},{24,16},{1,9},{9,1},{17,25},{25,17},{2,10},{10... | collective-permute-start | bytes 301064 | tf_op jit(solution)/shard_map/ppermute | solution.py:291
  19.5 1.0 %collective-permute-done.8.refs_1_ = bf16[392,128]{1,0:T(8,128)(2,1)S(1)} collective-permute-done((bf16[392,128]{1,0:T(8,128)(2,1)S(1)}, bf16[392,128]{1,0:T(8,128)(2,1)S(1)}, u32[]{:S(2)}, u32[]{:S(2)}) %collective-permute-start.8) | collective-permute-done | bytes 100384 | tf_op jit(solution)/shard_map/ppermute | solution.py:291
  20.4 0.0 collective-permute-done.9.refs_2_
  20.5 0.1 collective-permute-start.10
  20.5 0.5 %collective-permute-start.5 = (bf16[1160,128]{1,0:T(8,128)(2,1)S(1)}, bf16[1160,128]{1,0:T(8,128)(2,1)S(1)}, u32[]{:S(2)}, u32[]{:S(2)}) collective-permute-start(bf16[1160,128]{1,0:T(8,128)(2,1)S(1)} %get-tuple-element.13.refs_0_), channel_id=1, source_target_pairs={{0,1},{1,0},{2,3},{3,2},{4,5},{5,4},{6,7},{7,6},{8,9},{9,8},{10,11... | collective-permute-start | bytes 890888 | tf_op jit(solution)/shard_map/ppermute | solution.py:288
  21.0 1.4 %collective-permute-done.11.refs_0_ = bf16[392,128]{1,0:T(8,128)(2,1)S(1)} collective-permute-done((bf16[392,128]{1,0:T(8,128)(2,1)S(1)}, bf16[392,128]{1,0:T(8,128)(2,1)S(1)}, u32[]{:S(2)}, u32[]{:S(2)}) %collective-permute-start.11) | collective-permute-done | bytes 100384 | tf_op jit(solution)/shard_map/ppermute | solution.py:291
  22.5 0.0 collective-permute-start.6
  22.5 0.9 %collective-permute-done.12.refs_1_ = bf16[392,128]{1,0:T(8,128)(2,1)S(1)} collective-permute-done((bf16[392,128]{1,0:T(8,128)(2,1)S(1)}, bf16[392,128]{1,0:T(8,128)(2,1)S(1)}, u32[]{:S(2)}, u32[]{:S(2)}) %collective-permute-start.12) | collective-permute-done | bytes 100384 | tf_op jit(solution)/shard_map/ppermute | solution.py:291
  23.4 0.0 collective-permute-done.13.refs_2_
  23.4 0.1 collective-permute-start.14
  23.5 0.0 collective-permute-done.5.refs_2_
  23.5 0.6 %collective-permute-done.6.refs_3_ = bf16[1160,128]{1,0:T(8,128)(2,1)S(1)} collective-permute-done((bf16[1160,128]{1,0:T(8,128)(2,1)S(1)}, bf16[1160,128]{1,0:T(8,128)(2,1)S(1)}, u32[]{:S(2)}, u32[]{:S(2)}) %collective-permute-start.6) | collective-permute-done | bytes 296992 | tf_op jit(solution)/shard_map/ppermute | solution.py:288
  24.1 0.0 collective-permute-done.10.refs_5_
  24.1 1.9 %shard_map.37 = (bf16[832,768]{1,0:T(8,128)(2,1)S(1)}, bf16[128,320]{1,0:T(8,128)(2,1)S(1)}, f32[512,128]{1,0:T(8,128)S(1)}, f32[16,128]{1,0:T(8,128)S(1)}) custom-call(bf16[1160,128]{1,0:T(8,128)(2,1)S(1)} %get-tuple-element.13.refs_0_, bf16[1160,128]{1,0:T(8,128)(2,1)S(1)} %get-tuple-element.14.refs_1_, ...), custom_call_target="tpu_custom_call" | custom-call | flops 477102080 | bytes 1277952 | tf_op jit(solution)/shard_map/pallas_call | solution.py:33
  25.9 0.0 collective-permute-done.14.refs_5_
  25.9 1.9 %shard_map.39 = f32[512,128]{1,0:T(8,128)} custom-call(bf16[832,768]{1,0:T(8,128)(2,1)S(1)} %get-tuple-element.16.refs_0_, bf16[128,320]{1,0:T(8,128)(2,1)S(1)} %get-tuple-element.17.refs_1_, f32[512,128]{1,0:T(8,128)S(1)} %get-tuple-element.18.refs_2_, f32[16,128]{1,0:T(8,128)S(1)} %get-tuple-element.19.refs_3_, bf16[1176,128]{1,0:T(8,128)(2,1)S(1)} %shard_map.38.refs_4_, ...), custom_call_target="tpu_custom_call" | custom-call | flops 352321536 | bytes 1572864 | tf_op jit(solution)/shard_map/pallas_call | solution.py:33
  (5 shorter events, 0.1 us)
Async XLA Ops:
  0.0 9.0 %collective-permute-start.2 = (bf16[64,768]{1,0:T(8,128)(2,1)}, bf16[64,768]{1,0:T(8,128)(2,1)S(1)}, u32[]{:S(2)}, u32[]{:S(2)}) collective-permute-start(bf16[64,768]{1,0:T(8,128)(2,1)} %refs_0_.1), channel_id=1, source_target_pairs={{0,4},{1,5},{2,6},{3,7},{4,0},{5,1},{6,2},{7,3},{8,12},{9,13},{10,... | collective-permute-start | bytes 294920 | tf_op jit(solution)/shard_map/ppermute | solution.py:288
  4.0 6.9 %collective-permute-start = (bf16[64,768]{1,0:T(8,128)(2,1)}, bf16[64,768]{1,0:T(8,128)(2,1)S(1)}, u32[]{:S(2)}, u32[]{:S(2)}) collective-permute-start(bf16[64,768]{1,0:T(8,128)(2,1)} %refs_0_.1), channel_id=1, source_target_pairs={{0,2},{1,3},{2,0},{3,1},{4,6},{5,7},{6,4},{7,5},{8,10},{9,11},{10,... | collective-permute-start | bytes 294920 | tf_op jit(solution)/shard_map/ppermute | solution.py:288
  5.6 4.6 %collective-permute-start.3 = (s32[1,64]{1,0:T(1,128)}, s32[1,64]{1,0:T(1,128)S(1)}, u32[]{:S(2)}, u32[]{:S(2)}) collective-permute-start(s32[1,64]{1,0:T(1,128)} %bitcast.1), channel_id=1, source_target_pairs={{0,4},{1,5},{2,6},{3,7},{4,0},{5,1},{6,2},{7,3},{8,12},{9,13},{10,... | collective-permute-start | bytes 776 | tf_op jit(solution)/shard_map/ppermute | solution.py:288
  6.0 5.0 %collective-permute-start.1 = (s32[1,64]{1,0:T(1,128)}, s32[1,64]{1,0:T(1,128)S(1)}, u32[]{:S(2)}, u32[]{:S(2)}) collective-permute-start(s32[1,64]{1,0:T(1,128)} %bitcast.2), channel_id=1, source_target_pairs={{0,2},{1,3},{2,0},{3,1},{4,6},{5,7},{6,4},{7,5},{8,10},{9,11},{10,... | collective-permute-start | bytes 776 | tf_op jit(solution)/shard_map/ppermute | solution.py:288
  6.1 0.9 %copy-start = (bf16[64,768]{1,0:T(8,128)(2,1)S(1)}, bf16[64,768]{1,0:T(8,128)(2,1)}, u32[]{:S(2)}) copy-start(bf16[64,768]{1,0:T(8,128)(2,1)} %refs_0_.1) | copy-start | bytes 294916
  7.0 0.7 %copy-start.1 = (s32[64]{0:T(128)S(1)}, s32[64]{0:T(128)}, u32[]{:S(2)}) copy-start(s32[64]{0:T(128)} %param.3) | copy-start | bytes 772
  10.3 4.7 %collective-permute-start.4 = (bf16[392,128]{1,0:T(8,128)(2,1)S(1)}, bf16[392,128]{1,0:T(8,128)(2,1)S(1)}, u32[]{:S(2)}, u32[]{:S(2)}) collective-permute-start(bf16[392,128]{1,0:T(8,128)(2,1)S(1)} %shard_map.32.refs_2_.refs_0_), channel_id=1, source_target_pairs={{0,2},{1,3},{2,0},{3,1},{4,6},{5,7},{6,4},{7,5},{8,10},{9,11},{10,... | collective-permute-start | bytes 301064 | tf_op jit(solution)/shard_map/ppermute | solution.py:288
  11.4 6.9 %collective-permute-start.7 = (bf16[392,128]{1,0:T(8,128)(2,1)S(1)}, bf16[392,128]{1,0:T(8,128)(2,1)S(1)}, u32[]{:S(2)}, u32[]{:S(2)}) collective-permute-start(bf16[392,128]{1,0:T(8,128)(2,1)S(1)} %get-tuple-element.15), channel_id=1, source_target_pairs={{0,24},{8,16},{16,8},{24,0},{1,25},{9,17},{17,9},{25,1},{2,26},{10... | collective-permute-start | bytes 301064 | tf_op jit(solution)/shard_map/ppermute | solution.py:291
  13.9 6.6 %collective-permute-start.8 = (bf16[392,128]{1,0:T(8,128)(2,1)S(1)}, bf16[392,128]{1,0:T(8,128)(2,1)S(1)}, u32[]{:S(2)}, u32[]{:S(2)}) collective-permute-start(bf16[392,128]{1,0:T(8,128)(2,1)S(1)} %get-tuple-element.15), channel_id=1, source_target_pairs={{0,16},{8,24},{16,0},{24,8},{1,17},{9,25},{17,1},{25,9},{2,18},{10... | collective-permute-start | bytes 301064 | tf_op jit(solution)/shard_map/ppermute | solution.py:291
  14.4 6.1 %collective-permute-start.9 = (bf16[392,128]{1,0:T(8,128)(2,1)S(1)}, bf16[392,128]{1,0:T(8,128)(2,1)S(1)}, u32[]{:S(2)}, u32[]{:S(2)}) collective-permute-start(bf16[392,128]{1,0:T(8,128)(2,1)S(1)} %get-tuple-element.15), channel_id=1, source_target_pairs={{0,8},{8,0},{16,24},{24,16},{1,9},{9,1},{17,25},{25,17},{2,10},{10... | collective-permute-start | bytes 301064 | tf_op jit(solution)/shard_map/ppermute | solution.py:291
  15.3 7.1 %collective-permute-start.11 = (bf16[392,128]{1,0:T(8,128)(2,1)S(1)}, bf16[392,128]{1,0:T(8,128)(2,1)S(1)}, u32[]{:S(2)}, u32[]{:S(2)}) collective-permute-start(bf16[392,128]{1,0:T(8,128)(2,1)S(1)} %get-tuple-element.20), channel_id=1, source_target_pairs={{0,24},{8,16},{16,8},{24,0},{1,25},{9,17},{17,9},{25,1},{2,26},{10... | collective-permute-start | bytes 301064 | tf_op jit(solution)/shard_map/ppermute | solution.py:291
  17.8 5.6 %collective-permute-start.12 = (bf16[392,128]{1,0:T(8,128)(2,1)S(1)}, bf16[392,128]{1,0:T(8,128)(2,1)S(1)}, u32[]{:S(2)}, u32[]{:S(2)}) collective-permute-start(bf16[392,128]{1,0:T(8,128)(2,1)S(1)} %get-tuple-element.20), channel_id=1, source_target_pairs={{0,16},{8,24},{16,0},{24,8},{1,17},{9,25},{17,1},{25,9},{2,18},{10... | collective-permute-start | bytes 301064 | tf_op jit(solution)/shard_map/ppermute | solution.py:291
  18.3 5.1 %collective-permute-start.13 = (bf16[392,128]{1,0:T(8,128)(2,1)S(1)}, bf16[392,128]{1,0:T(8,128)(2,1)S(1)}, u32[]{:S(2)}, u32[]{:S(2)}) collective-permute-start(bf16[392,128]{1,0:T(8,128)(2,1)S(1)} %get-tuple-element.20), channel_id=1, source_target_pairs={{0,8},{8,0},{16,24},{24,16},{1,9},{9,1},{17,25},{25,17},{2,10},{10... | collective-permute-start | bytes 301064 | tf_op jit(solution)/shard_map/ppermute | solution.py:291
  20.5 3.6 %collective-permute-start.10 = (bf16[1176,128]{1,0:T(8,128)(2,1)S(1)}, bf16[1176,128]{1,0:T(8,128)(2,1)S(1)}, u32[]{:S(2)}, u32[]{:S(2)}) collective-permute-start(bf16[1176,128]{1,0:T(8,128)(2,1)S(1)} %shard_map.36.refs_4_), channel_id=1, source_target_pairs={{0,1},{1,0},{2,3},{3,2},{4,5},{5,4},{6,7},{7,6},{8,9},{9,8},{10,11... | collective-permute-start | bytes 903176 | tf_op jit(solution)/shard_map/ppermute | solution.py:288
  20.5 3.0 %collective-permute-start.5 = (bf16[1160,128]{1,0:T(8,128)(2,1)S(1)}, bf16[1160,128]{1,0:T(8,128)(2,1)S(1)}, u32[]{:S(2)}, u32[]{:S(2)}) collective-permute-start(bf16[1160,128]{1,0:T(8,128)(2,1)S(1)} %get-tuple-element.13.refs_0_), channel_id=1, source_target_pairs={{0,1},{1,0},{2,3},{3,2},{4,5},{5,4},{6,7},{7,6},{8,9},{9,8},{10,11... | collective-permute-start | bytes 890888 | tf_op jit(solution)/shard_map/ppermute | solution.py:288
  22.5 1.6 %collective-permute-start.6 = (bf16[1160,128]{1,0:T(8,128)(2,1)S(1)}, bf16[1160,128]{1,0:T(8,128)(2,1)S(1)}, u32[]{:S(2)}, u32[]{:S(2)}) collective-permute-start(bf16[1160,128]{1,0:T(8,128)(2,1)S(1)} %get-tuple-element.14.refs_1_), channel_id=1, source_target_pairs={{0,1},{1,0},{2,3},{3,2},{4,5},{5,4},{6,7},{7,6},{8,9},{9,8},{10,11... | collective-permute-start | bytes 890888 | tf_op jit(solution)/shard_map/ppermute | solution.py:288
  23.4 2.5 %collective-permute-start.14 = (bf16[1176,128]{1,0:T(8,128)(2,1)S(1)}, bf16[1176,128]{1,0:T(8,128)(2,1)S(1)}, u32[]{:S(2)}, u32[]{:S(2)}) collective-permute-start(bf16[1176,128]{1,0:T(8,128)(2,1)S(1)} %shard_map.38.refs_4_), channel_id=1, source_target_pairs={{0,1},{1,0},{2,3},{3,2},{4,5},{5,4},{6,7},{7,6},{8,9},{9,8},{10,11... | collective-permute-start | bytes 903176 | tf_op jit(solution)/shard_map/ppermute | solution.py:288

commit v5 on v4

--- a/solution.py
+++ b/solution.py
@@ -245,9 +245,9 @@
     )
 
 
-def sum_slots(sets, width):
-    arrays = [one for one, *_ in sets]
-    counts = [base * LANES // width for _, base, *_ in sets if base]
+def sum_slots(local, sets, width):
+    arrays = [one for one, _ in local] + [one for one, base, *_ in sets if not base]
+    counts = [base * LANES // width for _, base in local]
     parts = parts_of(sets, arrays, width)
     rows, slots = sum(counts), sum(part[2] for part in parts)
     return call(
@@ -327,13 +327,13 @@
         return [(one, base, half, False), (over_col(one, 1), base, half, True)]
 
     pairs = [both_cores(*one) for one in near]
+    local = [pair[side][:2] for side in range(2) for pair in pairs]
     got, base, half = last[0]
-    first = both_cores(stack(*got), base, half)
-    old = [pair[0] for pair in pairs] + [pair[1] for pair in pairs] + first
+    old = [*pairs[0], *both_cores(stack(*got), base, half)]
     order = [q for side in range(2) for batch in places for q in (one ^ side for one in batch)]
-    sums = sum_slots(old, width)
+    sums = sum_slots(local, old, width)
     got, base, half = last[1]
-    return finish(order, sums, both_cores(stack(*got), base, half), width)
+    return finish(order, sums, [*pairs[1], *both_cores(stack(*got), base, half)], width)
 
 
 def solution(mesh):

time: 28 us -> 27.5 us (0.982)
  Pallas kernels: 4.81 us -> 4.39 us
    pallas_call x12, Pallas kernels: 4.81 us -> 4.39 us  [call(): pl.pallas_call(body, out_shape=out_shape, in_specs=[VMEM] * count + [pl.B...]
  transfers between devices with their start and end apart: 15 -> 15, of which waited for: 6 -> 6; matrix products, arithmetic and copies ran while one was open for 0% -> 0% of each run, Pallas kernels for 11% -> 9%
where the time goes in v5:
time: 27.5 us; the launch traced here: 27.4 us
  starting transfers between devices  15 us (55%)
  waiting for transfers between devices  6.37 us (23%)
  Pallas kernels  4.39 us (16%)
  local copies, waits for them, and re-layouts  1.55 us (6%)
    ppermute x6, starting transfers between devices, over_row(): lax.ppermute(values, 'row', [(i, i ^ bits) for i in range(row_count)])  7.67 us
    ppermute x9, starting transfers between devices, over_col(): lax.ppermute(values, 'col', [(i, i ^ bits) for i in range(group_count)])  7.33 us
    pallas_call x12, Pallas kernels, call(): pl.pallas_call(body, out_shape=out_shape, in_specs=[VMEM] * count + [pl.B...  4.39 us
    ppermute x6, waiting for transfers between devices, over_row(): lax.ppermute(values, 'row', [(i, i ^ bits) for i in range(row_count)])  3.33 us
    ppermute x9, waiting for transfers between devices, over_col(): lax.ppermute(values, 'col', [(i, i ^ bits) for i in range(group_count)])  3.04 us
    unnamed x4, local copies, waits for them, and re-layouts  1.55 us
  transfers between devices with their start and end apart: 15, of which 6 were waited for; matrix products, arithmetic and copies ran while one was open for 0% of the time, Pallas kernels for 9%

profile of v5, /device:TPU:0, one launch (start us, length us, event | category | flops | bytes accessed | tf_op | source)
XLA Modules:
  0.0 27.4 jit_solution(5510952685883052251)
XLA Ops:
  0.0 4.0 %collective-permute-start.2 = (bf16[64,768]{1,0:T(8,128)(2,1)}, bf16[64,768]{1,0:T(8,128)(2,1)S(1)}, u32[]{:S(2)}, u32[]{:S(2)}) collective-permute-start(bf16[64,768]{1,0:T(8,128)(2,1)} %refs_0_.1), channel_id=1, source_target_pairs={{0,4},{1,5},{2,6},{3,7},{4,0},{5,1},{6,2},{7,3},{8,12},{9,13},{10,... | collective-permute-start | bytes 294920 | tf_op jit(solution)/shard_map/ppermute | solution.py:288
  4.0 1.6 %collective-permute-start = (bf16[64,768]{1,0:T(8,128)(2,1)}, bf16[64,768]{1,0:T(8,128)(2,1)S(1)}, u32[]{:S(2)}, u32[]{:S(2)}) collective-permute-start(bf16[64,768]{1,0:T(8,128)(2,1)} %refs_0_.1), channel_id=1, source_target_pairs={{0,2},{1,3},{2,0},{3,1},{4,6},{5,7},{6,4},{7,5},{8,10},{9,11},{10,... | collective-permute-start | bytes 294920 | tf_op jit(solution)/shard_map/ppermute | solution.py:288
  5.6 0.3 %collective-permute-start.3 = (s32[1,64]{1,0:T(1,128)}, s32[1,64]{1,0:T(1,128)S(1)}, u32[]{:S(2)}, u32[]{:S(2)}) collective-permute-start(s32[1,64]{1,0:T(1,128)} %bitcast.1), channel_id=1, source_target_pairs={{0,4},{1,5},{2,6},{3,7},{4,0},{5,1},{6,2},{7,3},{8,12},{9,13},{10,... | collective-permute-start | bytes 776 | tf_op jit(solution)/shard_map/ppermute | solution.py:288
  6.0 0.1 collective-permute-start.1
  6.1 0.0 copy-start
  6.1 0.9 %copy-done = bf16[64,768]{1,0:T(8,128)(2,1)S(1)} copy-done((bf16[64,768]{1,0:T(8,128)(2,1)S(1)}, bf16[64,768]{1,0:T(8,128)(2,1)}, u32[]{:S(2)}) %copy-start) | copy-done | bytes 98328
  7.0 0.0 copy-start.1
  7.0 0.7 %copy-done.1 = s32[64]{0:T(128)S(1)} copy-done((s32[64]{0:T(128)S(1)}, s32[64]{0:T(128)}, u32[]{:S(2)}) %copy-start.1) | copy-done | bytes 280
  7.6 0.1 shard_map.28.refs_0_
  7.7 1.3 %collective-permute-done.2.refs_0_ = bf16[64,768]{1,0:T(8,128)(2,1)S(1)} collective-permute-done((bf16[64,768]{1,0:T(8,128)(2,1)}, bf16[64,768]{1,0:T(8,128)(2,1)S(1)}, u32[]{:S(2)}, u32[]{:S(2)}) %collective-permute-start.2) | collective-permute-done | bytes 98336 | tf_op jit(solution)/shard_map/ppermute | solution.py:288
  9.1 1.1 %collective-permute-done.3.refs_1_ = s32[1,64]{1,0:T(1,128)S(1)} collective-permute-done((s32[1,64]{1,0:T(1,128)}, s32[1,64]{1,0:T(1,128)S(1)}, u32[]{:S(2)}, u32[]{:S(2)}) %collective-permute-start.3) | collective-permute-done | bytes 288 | tf_op jit(solution)/shard_map/ppermute | solution.py:288
  10.2 0.1 shard_map.32.refs_2_.refs_0_
  10.3 0.6 %collective-permute-start.4 = (bf16[392,128]{1,0:T(8,128)(2,1)S(1)}, bf16[392,128]{1,0:T(8,128)(2,1)S(1)}, u32[]{:S(2)}, u32[]{:S(2)}) collective-permute-start(bf16[392,128]{1,0:T(8,128)(2,1)S(1)} %shard_map.32.refs_2_.refs_0_), channel_id=1, source_target_pairs={{0,2},{1,3},{2,0},{3,1},{4,6},{5,7},{6,4},{7,5},{8,10},{9,11},{10,... | collective-permute-start | bytes 301064 | tf_op jit(solution)/shard_map/ppermute | solution.py:288
  10.9 0.0 collective-permute-done.refs_0_
  10.9 0.0 collective-permute-done.1.refs_1_
  10.9 0.1 shard_map.30.refs_1_
  11.0 0.4 %shard_map.33 = (bf16[1160,128]{1,0:T(8,128)(2,1)S(1)}, bf16[392,128]{1,0:T(8,128)(2,1)S(1)}) custom-call(bf16[392,128]{1,0:T(8,128)(2,1)S(1)} %shard_map.28.refs_0_, bf16[392,128]{1,0:T(8,128)(2,1)S(1)} %shard_map.30.refs_1_, bf16[392,128]{1,0:T(8,128)(2,1)S(1)} %shard_map.32.refs_2_.refs_0_), custom_call_target="tpu_custom_call" | custom-call | tf_op jit(solution)/shard_map/pallas_call | solution.py:33
  11.4 2.5 %collective-permute-start.7 = (bf16[392,128]{1,0:T(8,128)(2,1)S(1)}, bf16[392,128]{1,0:T(8,128)(2,1)S(1)}, u32[]{:S(2)}, u32[]{:S(2)}) collective-permute-start(bf16[392,128]{1,0:T(8,128)(2,1)S(1)} %get-tuple-element.15), channel_id=1, source_target_pairs={{0,24},{8,16},{16,8},{24,0},{1,25},{9,17},{17,9},{25,1},{2,26},{10... | collective-permute-start | bytes 301064 | tf_op jit(solution)/shard_map/ppermute | solution.py:291
  13.9 0.5 %collective-permute-start.8 = (bf16[392,128]{1,0:T(8,128)(2,1)S(1)}, bf16[392,128]{1,0:T(8,128)(2,1)S(1)}, u32[]{:S(2)}, u32[]{:S(2)}) collective-permute-start(bf16[392,128]{1,0:T(8,128)(2,1)S(1)} %get-tuple-element.15), channel_id=1, source_target_pairs={{0,16},{8,24},{16,0},{24,8},{1,17},{9,25},{17,1},{25,9},{2,18},{10... | collective-permute-start | bytes 301064 | tf_op jit(solution)/shard_map/ppermute | solution.py:291
  14.4 0.6 %collective-permute-start.9 = (bf16[392,128]{1,0:T(8,128)(2,1)S(1)}, bf16[392,128]{1,0:T(8,128)(2,1)S(1)}, u32[]{:S(2)}, u32[]{:S(2)}) collective-permute-start(bf16[392,128]{1,0:T(8,128)(2,1)S(1)} %get-tuple-element.15), channel_id=1, source_target_pairs={{0,8},{8,0},{16,24},{24,16},{1,9},{9,1},{17,25},{25,17},{2,10},{10... | collective-permute-start | bytes 301064 | tf_op jit(solution)/shard_map/ppermute | solution.py:291
  14.9 0.0 collective-permute-done.4.refs_0_
  15.0 0.4 %shard_map.35 = (bf16[1160,128]{1,0:T(8,128)(2,1)S(1)}, bf16[392,128]{1,0:T(8,128)(2,1)S(1)}) custom-call(bf16[392,128]{1,0:T(8,128)(2,1)S(1)} %shard_map.32.refs_2_.refs_0_, bf16[392,128]{1,0:T(8,128)(2,1)S(1)} %shard_map.34.refs_1_), custom_call_target="tpu_custom_call" | custom-call | tf_op jit(solution)/shard_map/pallas_call | solution.py:33
  15.3 2.5 %collective-permute-start.11 = (bf16[392,128]{1,0:T(8,128)(2,1)S(1)}, bf16[392,128]{1,0:T(8,128)(2,1)S(1)}, u32[]{:S(2)}, u32[]{:S(2)}) collective-permute-start(bf16[392,128]{1,0:T(8,128)(2,1)S(1)} %get-tuple-element.20), channel_id=1, source_target_pairs={{0,24},{8,16},{16,8},{24,0},{1,25},{9,17},{17,9},{25,1},{2,26},{10... | collective-permute-start | bytes 301064 | tf_op jit(solution)/shard_map/ppermute | solution.py:291
  17.8 0.5 %collective-permute-start.12 = (bf16[392,128]{1,0:T(8,128)(2,1)S(1)}, bf16[392,128]{1,0:T(8,128)(2,1)S(1)}, u32[]{:S(2)}, u32[]{:S(2)}) collective-permute-start(bf16[392,128]{1,0:T(8,128)(2,1)S(1)} %get-tuple-element.20), channel_id=1, source_target_pairs={{0,16},{8,24},{16,0},{24,8},{1,17},{9,25},{17,1},{25,9},{2,18},{10... | collective-permute-start | bytes 301064 | tf_op jit(solution)/shard_map/ppermute | solution.py:291
  18.3 0.0 collective-permute-done.7.refs_0_
  18.3 1.1 %collective-permute-start.13 = (bf16[392,128]{1,0:T(8,128)(2,1)S(1)}, bf16[392,128]{1,0:T(8,128)(2,1)S(1)}, u32[]{:S(2)}, u32[]{:S(2)}) collective-permute-start(bf16[392,128]{1,0:T(8,128)(2,1)S(1)} %get-tuple-element.20), channel_id=1, source_target_pairs={{0,8},{8,0},{16,24},{24,16},{1,9},{9,1},{17,25},{25,17},{2,10},{10... | collective-permute-start | bytes 301064 | tf_op jit(solution)/shard_map/ppermute | solution.py:291
  19.5 1.0 %collective-permute-done.8.refs_1_ = bf16[392,128]{1,0:T(8,128)(2,1)S(1)} collective-permute-done((bf16[392,128]{1,0:T(8,128)(2,1)S(1)}, bf16[392,128]{1,0:T(8,128)(2,1)S(1)}, u32[]{:S(2)}, u32[]{:S(2)}) %collective-permute-start.8) | collective-permute-done | bytes 100384 | tf_op jit(solution)/shard_map/ppermute | solution.py:291
  20.4 0.0 collective-permute-done.9.refs_2_
  20.5 0.1 collective-permute-start.10
  20.5 0.5 %collective-permute-start.5 = (bf16[1160,128]{1,0:T(8,128)(2,1)S(1)}, bf16[1160,128]{1,0:T(8,128)(2,1)S(1)}, u32[]{:S(2)}, u32[]{:S(2)}) collective-permute-start(bf16[1160,128]{1,0:T(8,128)(2,1)S(1)} %get-tuple-element.13.refs_0_), channel_id=1, source_target_pairs={{0,1},{1,0},{2,3},{3,2},{4,5},{5,4},{6,7},{7,6},{8,9},{9,8},{10,11... | collective-permute-start | bytes 890888 | tf_op jit(solution)/shard_map/ppermute | solution.py:288
  21.0 1.4 %collective-permute-done.11.refs_0_ = bf16[392,128]{1,0:T(8,128)(2,1)S(1)} collective-permute-done((bf16[392,128]{1,0:T(8,128)(2,1)S(1)}, bf16[392,128]{1,0:T(8,128)(2,1)S(1)}, u32[]{:S(2)}, u32[]{:S(2)}) %collective-permute-start.11) | collective-permute-done | bytes 100384 | tf_op jit(solution)/shard_map/ppermute | solution.py:291
  22.5 0.0 collective-permute-start.6
  22.5 0.9 %collective-permute-done.12.refs_1_ = bf16[392,128]{1,0:T(8,128)(2,1)S(1)} collective-permute-done((bf16[392,128]{1,0:T(8,128)(2,1)S(1)}, bf16[392,128]{1,0:T(8,128)(2,1)S(1)}, u32[]{:S(2)}, u32[]{:S(2)}) %collective-permute-start.12) | collective-permute-done | bytes 100384 | tf_op jit(solution)/shard_map/ppermute | solution.py:291
  23.4 0.0 collective-permute-done.13.refs_2_
  23.4 0.1 collective-permute-start.14
  23.5 0.0 collective-permute-done.5.refs_2_
  23.5 0.6 %collective-permute-done.6.refs_3_.refs_5_ = bf16[1160,128]{1,0:T(8,128)(2,1)S(1)} collective-permute-done((bf16[1160,128]{1,0:T(8,128)(2,1)S(1)}, bf16[1160,128]{1,0:T(8,128)(2,1)S(1)}, u32[]{:S(2)}, u32[]{:S(2)}) %collective-permute-start.6) | collective-permute-done | bytes 296992 | tf_op jit(solution)/shard_map/ppermute | solution.py:288
  24.1 0.0 collective-permute-done.10.refs_5_
  24.1 1.4 %shard_map.37 = (bf16[768,768]{1,0:T(8,128)(2,1)S(1)}, bf16[128,256]{1,0:T(8,128)(2,1)S(1)}, f32[512,128]{1,0:T(8,128)S(1)}, f32[16,128]{1,0:T(8,128)S(1)}) custom-call(bf16[1160,128]{1,0:T(8,128)(2,1)S(1)} %get-tuple-element.13.refs_0_, bf16[1160,128]{1,0:T(8,128)(2,1)S(1)} %get-tuple-element.14.refs_1_.refs_4_, ...), custom_call_target="tpu_custom_call" | custom-call | flops 352321536 | bytes 1179648 | tf_op jit(solution)/shard_map/pallas_call | solution.py:33
  25.4 0.0 collective-permute-done.14.refs_7_
  25.4 2.0 %shard_map.39 = f32[512,128]{1,0:T(8,128)} custom-call(bf16[768,768]{1,0:T(8,128)(2,1)S(1)} %get-tuple-element.16.refs_0_, bf16[128,256]{1,0:T(8,128)(2,1)S(1)} %get-tuple-element.17.refs_1_, f32[512,128]{1,0:T(8,128)S(1)} %get-tuple-element.18.refs_2_, f32[16,128]{1,0:T(8,128)S(1)} %get-tuple-element.19.refs_3_, ...), custom_call_target="tpu_custom_call" | custom-call | flops 469762048 | bytes 1572864 | tf_op jit(solution)/shard_map/pallas_call | solution.py:33
  (5 shorter events, 0.1 us)
Async XLA Ops:
  0.0 9.0 %collective-permute-start.2 = (bf16[64,768]{1,0:T(8,128)(2,1)}, bf16[64,768]{1,0:T(8,128)(2,1)S(1)}, u32[]{:S(2)}, u32[]{:S(2)}) collective-permute-start(bf16[64,768]{1,0:T(8,128)(2,1)} %refs_0_.1), channel_id=1, source_target_pairs={{0,4},{1,5},{2,6},{3,7},{4,0},{5,1},{6,2},{7,3},{8,12},{9,13},{10,... | collective-permute-start | bytes 294920 | tf_op jit(solution)/shard_map/ppermute | solution.py:288
  4.0 6.9 %collective-permute-start = (bf16[64,768]{1,0:T(8,128)(2,1)}, bf16[64,768]{1,0:T(8,128)(2,1)S(1)}, u32[]{:S(2)}, u32[]{:S(2)}) collective-permute-start(bf16[64,768]{1,0:T(8,128)(2,1)} %refs_0_.1), channel_id=1, source_target_pairs={{0,2},{1,3},{2,0},{3,1},{4,6},{5,7},{6,4},{7,5},{8,10},{9,11},{10,... | collective-permute-start | bytes 294920 | tf_op jit(solution)/shard_map/ppermute | solution.py:288
  5.6 4.6 %collective-permute-start.3 = (s32[1,64]{1,0:T(1,128)}, s32[1,64]{1,0:T(1,128)S(1)}, u32[]{:S(2)}, u32[]{:S(2)}) collective-permute-start(s32[1,64]{1,0:T(1,128)} %bitcast.1), channel_id=1, source_target_pairs={{0,4},{1,5},{2,6},{3,7},{4,0},{5,1},{6,2},{7,3},{8,12},{9,13},{10,... | collective-permute-start | bytes 776 | tf_op jit(solution)/shard_map/ppermute | solution.py:288
  6.0 5.0 %collective-permute-start.1 = (s32[1,64]{1,0:T(1,128)}, s32[1,64]{1,0:T(1,128)S(1)}, u32[]{:S(2)}, u32[]{:S(2)}) collective-permute-start(s32[1,64]{1,0:T(1,128)} %bitcast.2), channel_id=1, source_target_pairs={{0,2},{1,3},{2,0},{3,1},{4,6},{5,7},{6,4},{7,5},{8,10},{9,11},{10,... | collective-permute-start | bytes 776 | tf_op jit(solution)/shard_map/ppermute | solution.py:288
  6.1 0.9 %copy-start = (bf16[64,768]{1,0:T(8,128)(2,1)S(1)}, bf16[64,768]{1,0:T(8,128)(2,1)}, u32[]{:S(2)}) copy-start(bf16[64,768]{1,0:T(8,128)(2,1)} %refs_0_.1) | copy-start | bytes 294916
  7.0 0.7 %copy-start.1 = (s32[64]{0:T(128)S(1)}, s32[64]{0:T(128)}, u32[]{:S(2)}) copy-start(s32[64]{0:T(128)} %param.3) | copy-start | bytes 772
  10.3 4.7 %collective-permute-start.4 = (bf16[392,128]{1,0:T(8,128)(2,1)S(1)}, bf16[392,128]{1,0:T(8,128)(2,1)S(1)}, u32[]{:S(2)}, u32[]{:S(2)}) collective-permute-start(bf16[392,128]{1,0:T(8,128)(2,1)S(1)} %shard_map.32.refs_2_.refs_0_), channel_id=1, source_target_pairs={{0,2},{1,3},{2,0},{3,1},{4,6},{5,7},{6,4},{7,5},{8,10},{9,11},{10,... | collective-permute-start | bytes 301064 | tf_op jit(solution)/shard_map/ppermute | solution.py:288
  11.4 6.9 %collective-permute-start.7 = (bf16[392,128]{1,0:T(8,128)(2,1)S(1)}, bf16[392,128]{1,0:T(8,128)(2,1)S(1)}, u32[]{:S(2)}, u32[]{:S(2)}) collective-permute-start(bf16[392,128]{1,0:T(8,128)(2,1)S(1)} %get-tuple-element.15), channel_id=1, source_target_pairs={{0,24},{8,16},{16,8},{24,0},{1,25},{9,17},{17,9},{25,1},{2,26},{10... | collective-permute-start | bytes 301064 | tf_op jit(solution)/shard_map/ppermute | solution.py:291
  13.9 6.6 %collective-permute-start.8 = (bf16[392,128]{1,0:T(8,128)(2,1)S(1)}, bf16[392,128]{1,0:T(8,128)(2,1)S(1)}, u32[]{:S(2)}, u32[]{:S(2)}) collective-permute-start(bf16[392,128]{1,0:T(8,128)(2,1)S(1)} %get-tuple-element.15), channel_id=1, source_target_pairs={{0,16},{8,24},{16,0},{24,8},{1,17},{9,25},{17,1},{25,9},{2,18},{10... | collective-permute-start | bytes 301064 | tf_op jit(solution)/shard_map/ppermute | solution.py:291
  14.4 6.1 %collective-permute-start.9 = (bf16[392,128]{1,0:T(8,128)(2,1)S(1)}, bf16[392,128]{1,0:T(8,128)(2,1)S(1)}, u32[]{:S(2)}, u32[]{:S(2)}) collective-permute-start(bf16[392,128]{1,0:T(8,128)(2,1)S(1)} %get-tuple-element.15), channel_id=1, source_target_pairs={{0,8},{8,0},{16,24},{24,16},{1,9},{9,1},{17,25},{25,17},{2,10},{10... | collective-permute-start | bytes 301064 | tf_op jit(solution)/shard_map/ppermute | solution.py:291
  15.3 7.1 %collective-permute-start.11 = (bf16[392,128]{1,0:T(8,128)(2,1)S(1)}, bf16[392,128]{1,0:T(8,128)(2,1)S(1)}, u32[]{:S(2)}, u32[]{:S(2)}) collective-permute-start(bf16[392,128]{1,0:T(8,128)(2,1)S(1)} %get-tuple-element.20), channel_id=1, source_target_pairs={{0,24},{8,16},{16,8},{24,0},{1,25},{9,17},{17,9},{25,1},{2,26},{10... | collective-permute-start | bytes 301064 | tf_op jit(solution)/shard_map/ppermute | solution.py:291
  17.8 5.6 %collective-permute-start.12 = (bf16[392,128]{1,0:T(8,128)(2,1)S(1)}, bf16[392,128]{1,0:T(8,128)(2,1)S(1)}, u32[]{:S(2)}, u32[]{:S(2)}) collective-permute-start(bf16[392,128]{1,0:T(8,128)(2,1)S(1)} %get-tuple-element.20), channel_id=1, source_target_pairs={{0,16},{8,24},{16,0},{24,8},{1,17},{9,25},{17,1},{25,9},{2,18},{10... | collective-permute-start | bytes 301064 | tf_op jit(solution)/shard_map/ppermute | solution.py:291
  18.3 5.1 %collective-permute-start.13 = (bf16[392,128]{1,0:T(8,128)(2,1)S(1)}, bf16[392,128]{1,0:T(8,128)(2,1)S(1)}, u32[]{:S(2)}, u32[]{:S(2)}) collective-permute-start(bf16[392,128]{1,0:T(8,128)(2,1)S(1)} %get-tuple-element.20), channel_id=1, source_target_pairs={{0,8},{8,0},{16,24},{24,16},{1,9},{9,1},{17,25},{25,17},{2,10},{10... | collective-permute-start | bytes 301064 | tf_op jit(solution)/shard_map/ppermute | solution.py:291
  20.5 3.6 %collective-permute-start.10 = (bf16[1176,128]{1,0:T(8,128)(2,1)S(1)}, bf16[1176,128]{1,0:T(8,128)(2,1)S(1)}, u32[]{:S(2)}, u32[]{:S(2)}) collective-permute-start(bf16[1176,128]{1,0:T(8,128)(2,1)S(1)} %shard_map.36.refs_4_), channel_id=1, source_target_pairs={{0,1},{1,0},{2,3},{3,2},{4,5},{5,4},{6,7},{7,6},{8,9},{9,8},{10,11... | collective-permute-start | bytes 903176 | tf_op jit(solution)/shard_map/ppermute | solution.py:288
  20.5 3.0 %collective-permute-start.5 = (bf16[1160,128]{1,0:T(8,128)(2,1)S(1)}, bf16[1160,128]{1,0:T(8,128)(2,1)S(1)}, u32[]{:S(2)}, u32[]{:S(2)}) collective-permute-start(bf16[1160,128]{1,0:T(8,128)(2,1)S(1)} %get-tuple-element.13.refs_0_), channel_id=1, source_target_pairs={{0,1},{1,0},{2,3},{3,2},{4,5},{5,4},{6,7},{7,6},{8,9},{9,8},{10,11... | collective-permute-start | bytes 890888 | tf_op jit(solution)/shard_map/ppermute | solution.py:288
  22.5 1.6 %collective-permute-start.6 = (bf16[1160,128]{1,0:T(8,128)(2,1)S(1)}, bf16[1160,128]{1,0:T(8,128)(2,1)S(1)}, u32[]{:S(2)}, u32[]{:S(2)}) collective-permute-start(bf16[1160,128]{1,0:T(8,128)(2,1)S(1)} %get-tuple-element.14.refs_1_.refs_4_), channel_id=1, source_target_pairs={{0,1},{1,0},{2,3},{3,2},{4,5},{5,4},{6,7},{7,6},{8,9},{9,8},{10,11... | collective-permute-start | bytes 890888 | tf_op jit(solution)/shard_map/ppermute | solution.py:288
  23.4 2.0 %collective-permute-start.14 = (bf16[1176,128]{1,0:T(8,128)(2,1)S(1)}, bf16[1176,128]{1,0:T(8,128)(2,1)S(1)}, u32[]{:S(2)}, u32[]{:S(2)}) collective-permute-start(bf16[1176,128]{1,0:T(8,128)(2,1)S(1)} %shard_map.38.refs_6_), channel_id=1, source_target_pairs={{0,1},{1,0},{2,3},{3,2},{4,5},{5,4},{6,7},{7,6},{8,9},{9,8},{10,11... | collective-permute-start | bytes 903176 | tf_op jit(solution)/shard_map/ppermute | solution.py:288

commit v6 on v5

--- a/solution.py
+++ b/solution.py
@@ -76,8 +76,7 @@
         < lax.broadcasted_iota(jnp.int32, (own_count, own_count), 1)
     ).astype(jnp.bfloat16)
     slot = lax.broadcasted_iota(jnp.int32, (2 * half, own_count), 0)
-    ids = jnp.zeros((ID_ROWS, 2 * half), jnp.float32)
-    dispatch = []
+    relatives, labels = [], []
     for n, block_ref in enumerate(block_refs):
         for t in range(width // LANES):
             points_ref[n * own_count : (n + 1) * own_count, t * LANES : (t + 1) * LANES] = block_ref[
@@ -85,18 +84,23 @@
             ]
         end = block_ref.shape[0] - ID_ROWS
         group_of = block_ref[end:, :own_count].astype(jnp.float32).astype(jnp.int32)
-        labels = block_ref[end:, own_count : 2 * own_count].astype(jnp.float32) + 1.0
-        relative = group_of ^ me
-        member = lax.broadcasted_iota(jnp.int32, (ID_ROWS, own_count), 0) == relative
-        rank = dot(member.astype(jnp.bfloat16), earlier, NN)
-        position = jnp.sum(jnp.where(member, rank, 0.0), axis=0, keepdims=True)
-        target = jnp.where(
-            relative < 2, relative * half + n * slots + position.astype(jnp.int32), -1
-        )
-        chosen = (slot == target[:1]).astype(jnp.bfloat16)
-        ids += dot(labels.astype(jnp.bfloat16), chosen, NT)
-        dispatch.append(chosen)
-    rows = dot(jnp.concatenate(dispatch, axis=1), points_ref[...], NN).astype(jnp.bfloat16)
+        relatives.append(group_of ^ me)
+        labels.append(block_ref[end:, own_count : 2 * own_count].astype(jnp.float32) + 1.0)
+    members = [
+        lax.broadcasted_iota(jnp.int32, (ID_ROWS, own_count), 0) == relative
+        for relative in relatives
+    ]
+    marks = [member.astype(jnp.float32) for member in members]
+    ranks = dot(jnp.concatenate(marks, axis=0).astype(jnp.bfloat16), earlier, NN)
+    dispatch = []
+    for n, (relative, mark) in enumerate(zip(relatives, marks)):
+        rank = ranks[n * ID_ROWS : (n + 1) * ID_ROWS] * mark
+        position = jnp.sum(rank, axis=0, keepdims=True).astype(jnp.int32)
+        target = jnp.where(relative < 2, relative * half + n * slots + position, -1)
+        dispatch.append((slot == target[:1]).astype(jnp.bfloat16))
+    dispatch = jnp.concatenate(dispatch, axis=1)
+    rows = dot(dispatch, points_ref[...], NN).astype(jnp.bfloat16)
+    ids = dot(jnp.concatenate(labels, axis=1).astype(jnp.bfloat16), dispatch, NT)
     put_tall(local_ref, 0, points_ref[...])
     for ref, start in ((local_ref, points * width // LANES), (set_ref, 0)):
         end = ref.shape[0] - ID_ROWS
@@ -208,9 +212,17 @@
         place = end
     slots, hot = slots_ref[...], hot_ref[...]
     norms = row_norms(slots_ref)
+    whole = kern(left_ref[...], slots, norms) if total * place <= MIB else None
+
+    def tiles(begin, end):
+        if whole is not None:
+            yield begin, end, whole[begin:end]
+            return
+        for start, stop in chunks(begin, end, 512):
+            yield start, stop, kern(left_ref[start:stop, :], slots, norms)
+
     shares = dot(hot, kern(slots, slots, norms), NN)
-    for start, end in chunks(rows, total, 512):
-        tile = kern(left_ref[start:end, :], slots, norms)
+    for start, end, tile in tiles(rows, total):
         shares += 2.0 * dot(old_hot_ref[:, start - rows : end - rows], tile, NN)
     column = jnp.sum(shares * hot.astype(jnp.float32), axis=1, keepdims=True)
     totals = totals_ref[:1, :] + row_of(column)
@@ -220,9 +232,8 @@
     factor = 2.0 / sizes
     me = lax.axis_index("col")
     own_count = rows // len(order)
-    for start, end in chunks(0, rows, 512):
-        part = sums_ref[start:end, :] + dot(kern(left_ref[start:end, :], slots, norms), hot, NT)
-        part = offset - part * factor
+    for start, end, tile in tiles(0, rows):
+        part = offset - (sums_ref[start:end, :] + dot(tile, hot, NT)) * factor
         for b in range((end - start) // own_count):
             row = pl.multiple_of((me ^ order[start // own_count + b]) * own_count, own_count)
             out_ref[pl.ds(row, own_count), :] = part[b * own_count : (b + 1) * own_count]

time: 27.5 us -> 27.4 us (level)
  no operation moved by 1% of the time
where the time goes in v6:
time: 27.4 us; the launch traced here: 27.3 us
  starting transfers between devices  15 us (55%)
  waiting for transfers between devices  6.36 us (23%)
  Pallas kernels  4.29 us (16%)
  local copies, waits for them, and re-layouts  1.55 us (6%)
    ppermute x6, starting transfers between devices, over_row(): lax.ppermute(values, 'row', [(i, i ^ bits) for i in range(row_count)])  7.69 us
    ppermute x9, starting transfers between devices, over_col(): lax.ppermute(values, 'col', [(i, i ^ bits) for i in range(group_count)])  7.33 us
    pallas_call x12, Pallas kernels, call(): pl.pallas_call(body, out_shape=out_shape, in_specs=[VMEM] * count + [pl.B...  4.29 us
    ppermute x6, waiting for transfers between devices, over_row(): lax.ppermute(values, 'row', [(i, i ^ bits) for i in range(row_count)])  3.32 us
    ppermute x9, waiting for transfers between devices, over_col(): lax.ppermute(values, 'col', [(i, i ^ bits) for i in range(group_count)])  3.04 us
    unnamed x4, local copies, waits for them, and re-layouts  1.55 us
  transfers between devices with their start and end apart: 15, of which 6 were waited for; matrix products, arithmetic and copies ran while one was open for 0% of the time, Pallas kernels for 9%

profile of v6, /device:TPU:0, one launch (start us, length us, event | category | flops | bytes accessed | tf_op | source)
XLA Modules:
  0.0 27.3 jit_solution(8397903400379815571)
XLA Ops:
  0.0 4.0 %collective-permute-start.2 = (bf16[64,768]{1,0:T(8,128)(2,1)}, bf16[64,768]{1,0:T(8,128)(2,1)S(1)}, u32[]{:S(2)}, u32[]{:S(2)}) collective-permute-start(bf16[64,768]{1,0:T(8,128)(2,1)} %refs_0_.1), channel_id=1, source_target_pairs={{0,4},{1,5},{2,6},{3,7},{4,0},{5,1},{6,2},{7,3},{8,12},{9,13},{10,... | collective-permute-start | bytes 294920 | tf_op jit(solution)/shard_map/ppermute | solution.py:299
  4.0 1.6 %collective-permute-start = (bf16[64,768]{1,0:T(8,128)(2,1)}, bf16[64,768]{1,0:T(8,128)(2,1)S(1)}, u32[]{:S(2)}, u32[]{:S(2)}) collective-permute-start(bf16[64,768]{1,0:T(8,128)(2,1)} %refs_0_.1), channel_id=1, source_target_pairs={{0,2},{1,3},{2,0},{3,1},{4,6},{5,7},{6,4},{7,5},{8,10},{9,11},{10,... | collective-permute-start | bytes 294920 | tf_op jit(solution)/shard_map/ppermute | solution.py:299
  5.6 0.3 %collective-permute-start.3 = (s32[1,64]{1,0:T(1,128)}, s32[1,64]{1,0:T(1,128)S(1)}, u32[]{:S(2)}, u32[]{:S(2)}) collective-permute-start(s32[1,64]{1,0:T(1,128)} %bitcast.1), channel_id=1, source_target_pairs={{0,4},{1,5},{2,6},{3,7},{4,0},{5,1},{6,2},{7,3},{8,12},{9,13},{10,... | collective-permute-start | bytes 776 | tf_op jit(solution)/shard_map/ppermute | solution.py:299
  6.0 0.1 collective-permute-start.1
  6.1 0.0 copy-start
  6.1 0.9 %copy-done = bf16[64,768]{1,0:T(8,128)(2,1)S(1)} copy-done((bf16[64,768]{1,0:T(8,128)(2,1)S(1)}, bf16[64,768]{1,0:T(8,128)(2,1)}, u32[]{:S(2)}) %copy-start) | copy-done | bytes 98328
  7.0 0.0 copy-start.1
  7.0 0.7 %copy-done.1 = s32[64]{0:T(128)S(1)} copy-done((s32[64]{0:T(128)S(1)}, s32[64]{0:T(128)}, u32[]{:S(2)}) %copy-start.1) | copy-done | bytes 280
  7.6 0.1 shard_map.28.refs_0_
  7.7 1.3 %collective-permute-done.2.refs_0_ = bf16[64,768]{1,0:T(8,128)(2,1)S(1)} collective-permute-done((bf16[64,768]{1,0:T(8,128)(2,1)}, bf16[64,768]{1,0:T(8,128)(2,1)S(1)}, u32[]{:S(2)}, u32[]{:S(2)}) %collective-permute-start.2) | collective-permute-done | bytes 98336 | tf_op jit(solution)/shard_map/ppermute | solution.py:299
  9.1 1.1 %collective-permute-done.3.refs_1_ = s32[1,64]{1,0:T(1,128)S(1)} collective-permute-done((s32[1,64]{1,0:T(1,128)}, s32[1,64]{1,0:T(1,128)S(1)}, u32[]{:S(2)}, u32[]{:S(2)}) %collective-permute-start.3) | collective-permute-done | bytes 288 | tf_op jit(solution)/shard_map/ppermute | solution.py:299
  10.2 0.1 shard_map.32.refs_2_.refs_0_
  10.3 0.6 %collective-permute-start.4 = (bf16[392,128]{1,0:T(8,128)(2,1)S(1)}, bf16[392,128]{1,0:T(8,128)(2,1)S(1)}, u32[]{:S(2)}, u32[]{:S(2)}) collective-permute-start(bf16[392,128]{1,0:T(8,128)(2,1)S(1)} %shard_map.32.refs_2_.refs_0_), channel_id=1, source_target_pairs={{0,2},{1,3},{2,0},{3,1},{4,6},{5,7},{6,4},{7,5},{8,10},{9,11},{10,... | collective-permute-start | bytes 301064 | tf_op jit(solution)/shard_map/ppermute | solution.py:299
  10.9 0.0 collective-permute-done.refs_0_
  10.9 0.0 collective-permute-done.1.refs_1_
  10.9 0.1 shard_map.30.refs_1_
  11.0 0.4 %shard_map.33 = (bf16[1160,128]{1,0:T(8,128)(2,1)S(1)}, bf16[392,128]{1,0:T(8,128)(2,1)S(1)}) custom-call(bf16[392,128]{1,0:T(8,128)(2,1)S(1)} %shard_map.28.refs_0_, bf16[392,128]{1,0:T(8,128)(2,1)S(1)} %shard_map.30.refs_1_, bf16[392,128]{1,0:T(8,128)(2,1)S(1)} %shard_map.32.refs_2_.refs_0_), custom_call_target="tpu_custom_call" | custom-call | tf_op jit(solution)/shard_map/pallas_call | solution.py:33
  11.4 2.5 %collective-permute-start.7 = (bf16[392,128]{1,0:T(8,128)(2,1)S(1)}, bf16[392,128]{1,0:T(8,128)(2,1)S(1)}, u32[]{:S(2)}, u32[]{:S(2)}) collective-permute-start(bf16[392,128]{1,0:T(8,128)(2,1)S(1)} %get-tuple-element.15), channel_id=1, source_target_pairs={{0,24},{8,16},{16,8},{24,0},{1,25},{9,17},{17,9},{25,1},{2,26},{10... | collective-permute-start | bytes 301064 | tf_op jit(solution)/shard_map/ppermute | solution.py:302
  13.9 0.5 %collective-permute-start.8 = (bf16[392,128]{1,0:T(8,128)(2,1)S(1)}, bf16[392,128]{1,0:T(8,128)(2,1)S(1)}, u32[]{:S(2)}, u32[]{:S(2)}) collective-permute-start(bf16[392,128]{1,0:T(8,128)(2,1)S(1)} %get-tuple-element.15), channel_id=1, source_target_pairs={{0,16},{8,24},{16,0},{24,8},{1,17},{9,25},{17,1},{25,9},{2,18},{10... | collective-permute-start | bytes 301064 | tf_op jit(solution)/shard_map/ppermute | solution.py:302
  14.4 0.6 %collective-permute-start.9 = (bf16[392,128]{1,0:T(8,128)(2,1)S(1)}, bf16[392,128]{1,0:T(8,128)(2,1)S(1)}, u32[]{:S(2)}, u32[]{:S(2)}) collective-permute-start(bf16[392,128]{1,0:T(8,128)(2,1)S(1)} %get-tuple-element.15), channel_id=1, source_target_pairs={{0,8},{8,0},{16,24},{24,16},{1,9},{9,1},{17,25},{25,17},{2,10},{10... | collective-permute-start | bytes 301064 | tf_op jit(solution)/shard_map/ppermute | solution.py:302
  14.9 0.0 collective-permute-done.4.refs_0_
  15.0 0.4 %shard_map.35 = (bf16[1160,128]{1,0:T(8,128)(2,1)S(1)}, bf16[392,128]{1,0:T(8,128)(2,1)S(1)}) custom-call(bf16[392,128]{1,0:T(8,128)(2,1)S(1)} %shard_map.32.refs_2_.refs_0_, bf16[392,128]{1,0:T(8,128)(2,1)S(1)} %shard_map.34.refs_1_), custom_call_target="tpu_custom_call" | custom-call | tf_op jit(solution)/shard_map/pallas_call | solution.py:33
  15.3 2.5 %collective-permute-start.11 = (bf16[392,128]{1,0:T(8,128)(2,1)S(1)}, bf16[392,128]{1,0:T(8,128)(2,1)S(1)}, u32[]{:S(2)}, u32[]{:S(2)}) collective-permute-start(bf16[392,128]{1,0:T(8,128)(2,1)S(1)} %get-tuple-element.20), channel_id=1, source_target_pairs={{0,24},{8,16},{16,8},{24,0},{1,25},{9,17},{17,9},{25,1},{2,26},{10... | collective-permute-start | bytes 301064 | tf_op jit(solution)/shard_map/ppermute | solution.py:302
  17.8 0.5 %collective-permute-start.12 = (bf16[392,128]{1,0:T(8,128)(2,1)S(1)}, bf16[392,128]{1,0:T(8,128)(2,1)S(1)}, u32[]{:S(2)}, u32[]{:S(2)}) collective-permute-start(bf16[392,128]{1,0:T(8,128)(2,1)S(1)} %get-tuple-element.20), channel_id=1, source_target_pairs={{0,16},{8,24},{16,0},{24,8},{1,17},{9,25},{17,1},{25,9},{2,18},{10... | collective-permute-start | bytes 301064 | tf_op jit(solution)/shard_map/ppermute | solution.py:302
  18.3 0.0 collective-permute-done.7.refs_0_
  18.3 1.1 %collective-permute-start.13 = (bf16[392,128]{1,0:T(8,128)(2,1)S(1)}, bf16[392,128]{1,0:T(8,128)(2,1)S(1)}, u32[]{:S(2)}, u32[]{:S(2)}) collective-permute-start(bf16[392,128]{1,0:T(8,128)(2,1)S(1)} %get-tuple-element.20), channel_id=1, source_target_pairs={{0,8},{8,0},{16,24},{24,16},{1,9},{9,1},{17,25},{25,17},{2,10},{10... | collective-permute-start | bytes 301064 | tf_op jit(solution)/shard_map/ppermute | solution.py:302
  19.5 1.0 %collective-permute-done.8.refs_1_ = bf16[392,128]{1,0:T(8,128)(2,1)S(1)} collective-permute-done((bf16[392,128]{1,0:T(8,128)(2,1)S(1)}, bf16[392,128]{1,0:T(8,128)(2,1)S(1)}, u32[]{:S(2)}, u32[]{:S(2)}) %collective-permute-start.8) | collective-permute-done | bytes 100384 | tf_op jit(solution)/shard_map/ppermute | solution.py:302
  20.4 0.0 collective-permute-done.9.refs_2_
  20.5 0.1 collective-permute-start.10
  20.5 0.5 %collective-permute-start.5 = (bf16[1160,128]{1,0:T(8,128)(2,1)S(1)}, bf16[1160,128]{1,0:T(8,128)(2,1)S(1)}, u32[]{:S(2)}, u32[]{:S(2)}) collective-permute-start(bf16[1160,128]{1,0:T(8,128)(2,1)S(1)} %get-tuple-element.13.refs_0_), channel_id=1, source_target_pairs={{0,1},{1,0},{2,3},{3,2},{4,5},{5,4},{6,7},{7,6},{8,9},{9,8},{10,11... | collective-permute-start | bytes 890888 | tf_op jit(solution)/shard_map/ppermute | solution.py:299
  21.0 1.4 %collective-permute-done.11.refs_0_ = bf16[392,128]{1,0:T(8,128)(2,1)S(1)} collective-permute-done((bf16[392,128]{1,0:T(8,128)(2,1)S(1)}, bf16[392,128]{1,0:T(8,128)(2,1)S(1)}, u32[]{:S(2)}, u32[]{:S(2)}) %collective-permute-start.11) | collective-permute-done | bytes 100384 | tf_op jit(solution)/shard_map/ppermute | solution.py:302
  22.5 0.0 collective-permute-start.6
  22.5 0.9 %collective-permute-done.12.refs_1_ = bf16[392,128]{1,0:T(8,128)(2,1)S(1)} collective-permute-done((bf16[392,128]{1,0:T(8,128)(2,1)S(1)}, bf16[392,128]{1,0:T(8,128)(2,1)S(1)}, u32[]{:S(2)}, u32[]{:S(2)}) %collective-permute-start.12) | collective-permute-done | bytes 100384 | tf_op jit(solution)/shard_map/ppermute | solution.py:302
  23.4 0.0 collective-permute-done.13.refs_2_
  23.4 0.1 collective-permute-start.14
  23.5 0.0 collective-permute-done.5.refs_2_
  23.5 0.6 %collective-permute-done.6.refs_3_.refs_5_ = bf16[1160,128]{1,0:T(8,128)(2,1)S(1)} collective-permute-done((bf16[1160,128]{1,0:T(8,128)(2,1)S(1)}, bf16[1160,128]{1,0:T(8,128)(2,1)S(1)}, u32[]{:S(2)}, u32[]{:S(2)}) %collective-permute-start.6) | collective-permute-done | bytes 296992 | tf_op jit(solution)/shard_map/ppermute | solution.py:299
  24.1 0.0 collective-permute-done.10.refs_5_
  24.1 1.4 %shard_map.37 = (bf16[768,768]{1,0:T(8,128)(2,1)S(1)}, bf16[128,256]{1,0:T(8,128)(2,1)S(1)}, f32[512,128]{1,0:T(8,128)S(1)}, f32[16,128]{1,0:T(8,128)S(1)}) custom-call(bf16[1160,128]{1,0:T(8,128)(2,1)S(1)} %get-tuple-element.13.refs_0_, bf16[1160,128]{1,0:T(8,128)(2,1)S(1)} %get-tuple-element.14.refs_1_.refs_4_, ...), custom_call_target="tpu_custom_call" | custom-call | flops 352321536 | bytes 1179648 | tf_op jit(solution)/shard_map/pallas_call | solution.py:33
  25.4 0.0 collective-permute-done.14.refs_7_
  25.4 1.9 %shard_map.39 = f32[512,128]{1,0:T(8,128)} custom-call(bf16[768,768]{1,0:T(8,128)(2,1)S(1)} %get-tuple-element.16.refs_0_, bf16[128,256]{1,0:T(8,128)(2,1)S(1)} %get-tuple-element.17.refs_1_, f32[512,128]{1,0:T(8,128)S(1)} %get-tuple-element.18.refs_2_, f32[16,128]{1,0:T(8,128)S(1)} %get-tuple-element.19.refs_3_, ...), custom_call_target="tpu_custom_call" | custom-call | flops 469762048 | bytes 1572864 | tf_op jit(solution)/shard_map/pallas_call | solution.py:33
  (5 shorter events, 0.1 us)
Async XLA Ops:
  0.0 9.0 %collective-permute-start.2 = (bf16[64,768]{1,0:T(8,128)(2,1)}, bf16[64,768]{1,0:T(8,128)(2,1)S(1)}, u32[]{:S(2)}, u32[]{:S(2)}) collective-permute-start(bf16[64,768]{1,0:T(8,128)(2,1)} %refs_0_.1), channel_id=1, source_target_pairs={{0,4},{1,5},{2,6},{3,7},{4,0},{5,1},{6,2},{7,3},{8,12},{9,13},{10,... | collective-permute-start | bytes 294920 | tf_op jit(solution)/shard_map/ppermute | solution.py:299
  4.0 6.9 %collective-permute-start = (bf16[64,768]{1,0:T(8,128)(2,1)}, bf16[64,768]{1,0:T(8,128)(2,1)S(1)}, u32[]{:S(2)}, u32[]{:S(2)}) collective-permute-start(bf16[64,768]{1,0:T(8,128)(2,1)} %refs_0_.1), channel_id=1, source_target_pairs={{0,2},{1,3},{2,0},{3,1},{4,6},{5,7},{6,4},{7,5},{8,10},{9,11},{10,... | collective-permute-start | bytes 294920 | tf_op jit(solution)/shard_map/ppermute | solution.py:299
  5.6 4.6 %collective-permute-start.3 = (s32[1,64]{1,0:T(1,128)}, s32[1,64]{1,0:T(1,128)S(1)}, u32[]{:S(2)}, u32[]{:S(2)}) collective-permute-start(s32[1,64]{1,0:T(1,128)} %bitcast.1), channel_id=1, source_target_pairs={{0,4},{1,5},{2,6},{3,7},{4,0},{5,1},{6,2},{7,3},{8,12},{9,13},{10,... | collective-permute-start | bytes 776 | tf_op jit(solution)/shard_map/ppermute | solution.py:299
  6.0 5.0 %collective-permute-start.1 = (s32[1,64]{1,0:T(1,128)}, s32[1,64]{1,0:T(1,128)S(1)}, u32[]{:S(2)}, u32[]{:S(2)}) collective-permute-start(s32[1,64]{1,0:T(1,128)} %bitcast.2), channel_id=1, source_target_pairs={{0,2},{1,3},{2,0},{3,1},{4,6},{5,7},{6,4},{7,5},{8,10},{9,11},{10,... | collective-permute-start | bytes 776 | tf_op jit(solution)/shard_map/ppermute | solution.py:299
  6.1 0.9 %copy-start = (bf16[64,768]{1,0:T(8,128)(2,1)S(1)}, bf16[64,768]{1,0:T(8,128)(2,1)}, u32[]{:S(2)}) copy-start(bf16[64,768]{1,0:T(8,128)(2,1)} %refs_0_.1) | copy-start | bytes 294916
  7.0 0.7 %copy-start.1 = (s32[64]{0:T(128)S(1)}, s32[64]{0:T(128)}, u32[]{:S(2)}) copy-start(s32[64]{0:T(128)} %param.3) | copy-start | bytes 772
  10.3 4.7 %collective-permute-start.4 = (bf16[392,128]{1,0:T(8,128)(2,1)S(1)}, bf16[392,128]{1,0:T(8,128)(2,1)S(1)}, u32[]{:S(2)}, u32[]{:S(2)}) collective-permute-start(bf16[392,128]{1,0:T(8,128)(2,1)S(1)} %shard_map.32.refs_2_.refs_0_), channel_id=1, source_target_pairs={{0,2},{1,3},{2,0},{3,1},{4,6},{5,7},{6,4},{7,5},{8,10},{9,11},{10,... | collective-permute-start | bytes 301064 | tf_op jit(solution)/shard_map/ppermute | solution.py:299
  11.4 6.9 %collective-permute-start.7 = (bf16[392,128]{1,0:T(8,128)(2,1)S(1)}, bf16[392,128]{1,0:T(8,128)(2,1)S(1)}, u32[]{:S(2)}, u32[]{:S(2)}) collective-permute-start(bf16[392,128]{1,0:T(8,128)(2,1)S(1)} %get-tuple-element.15), channel_id=1, source_target_pairs={{0,24},{8,16},{16,8},{24,0},{1,25},{9,17},{17,9},{25,1},{2,26},{10... | collective-permute-start | bytes 301064 | tf_op jit(solution)/shard_map/ppermute | solution.py:302
  13.9 6.6 %collective-permute-start.8 = (bf16[392,128]{1,0:T(8,128)(2,1)S(1)}, bf16[392,128]{1,0:T(8,128)(2,1)S(1)}, u32[]{:S(2)}, u32[]{:S(2)}) collective-permute-start(bf16[392,128]{1,0:T(8,128)(2,1)S(1)} %get-tuple-element.15), channel_id=1, source_target_pairs={{0,16},{8,24},{16,0},{24,8},{1,17},{9,25},{17,1},{25,9},{2,18},{10... | collective-permute-start | bytes 301064 | tf_op jit(solution)/shard_map/ppermute | solution.py:302
  14.4 6.1 %collective-permute-start.9 = (bf16[392,128]{1,0:T(8,128)(2,1)S(1)}, bf16[392,128]{1,0:T(8,128)(2,1)S(1)}, u32[]{:S(2)}, u32[]{:S(2)}) collective-permute-start(bf16[392,128]{1,0:T(8,128)(2,1)S(1)} %get-tuple-element.15), channel_id=1, source_target_pairs={{0,8},{8,0},{16,24},{24,16},{1,9},{9,1},{17,25},{25,17},{2,10},{10... | collective-permute-start | bytes 301064 | tf_op jit(solution)/shard_map/ppermute | solution.py:302
  15.3 7.1 %collective-permute-start.11 = (bf16[392,128]{1,0:T(8,128)(2,1)S(1)}, bf16[392,128]{1,0:T(8,128)(2,1)S(1)}, u32[]{:S(2)}, u32[]{:S(2)}) collective-permute-start(bf16[392,128]{1,0:T(8,128)(2,1)S(1)} %get-tuple-element.20), channel_id=1, source_target_pairs={{0,24},{8,16},{16,8},{24,0},{1,25},{9,17},{17,9},{25,1},{2,26},{10... | collective-permute-start | bytes 301064 | tf_op jit(solution)/shard_map/ppermute | solution.py:302
  17.8 5.6 %collective-permute-start.12 = (bf16[392,128]{1,0:T(8,128)(2,1)S(1)}, bf16[392,128]{1,0:T(8,128)(2,1)S(1)}, u32[]{:S(2)}, u32[]{:S(2)}) collective-permute-start(bf16[392,128]{1,0:T(8,128)(2,1)S(1)} %get-tuple-element.20), channel_id=1, source_target_pairs={{0,16},{8,24},{16,0},{24,8},{1,17},{9,25},{17,1},{25,9},{2,18},{10... | collective-permute-start | bytes 301064 | tf_op jit(solution)/shard_map/ppermute | solution.py:302
  18.3 5.1 %collective-permute-start.13 = (bf16[392,128]{1,0:T(8,128)(2,1)S(1)}, bf16[392,128]{1,0:T(8,128)(2,1)S(1)}, u32[]{:S(2)}, u32[]{:S(2)}) collective-permute-start(bf16[392,128]{1,0:T(8,128)(2,1)S(1)} %get-tuple-element.20), channel_id=1, source_target_pairs={{0,8},{8,0},{16,24},{24,16},{1,9},{9,1},{17,25},{25,17},{2,10},{10... | collective-permute-start | bytes 301064 | tf_op jit(solution)/shard_map/ppermute | solution.py:302
  20.5 3.6 %collective-permute-start.10 = (bf16[1176,128]{1,0:T(8,128)(2,1)S(1)}, bf16[1176,128]{1,0:T(8,128)(2,1)S(1)}, u32[]{:S(2)}, u32[]{:S(2)}) collective-permute-start(bf16[1176,128]{1,0:T(8,128)(2,1)S(1)} %shard_map.36.refs_4_), channel_id=1, source_target_pairs={{0,1},{1,0},{2,3},{3,2},{4,5},{5,4},{6,7},{7,6},{8,9},{9,8},{10,11... | collective-permute-start | bytes 903176 | tf_op jit(solution)/shard_map/ppermute | solution.py:299
  20.5 3.0 %collective-permute-start.5 = (bf16[1160,128]{1,0:T(8,128)(2,1)S(1)}, bf16[1160,128]{1,0:T(8,128)(2,1)S(1)}, u32[]{:S(2)}, u32[]{:S(2)}) collective-permute-start(bf16[1160,128]{1,0:T(8,128)(2,1)S(1)} %get-tuple-element.13.refs_0_), channel_id=1, source_target_pairs={{0,1},{1,0},{2,3},{3,2},{4,5},{5,4},{6,7},{7,6},{8,9},{9,8},{10,11... | collective-permute-start | bytes 890888 | tf_op jit(solution)/shard_map/ppermute | solution.py:299
  22.5 1.6 %collective-permute-start.6 = (bf16[1160,128]{1,0:T(8,128)(2,1)S(1)}, bf16[1160,128]{1,0:T(8,128)(2,1)S(1)}, u32[]{:S(2)}, u32[]{:S(2)}) collective-permute-start(bf16[1160,128]{1,0:T(8,128)(2,1)S(1)} %get-tuple-element.14.refs_1_.refs_4_), channel_id=1, source_target_pairs={{0,1},{1,0},{2,3},{3,2},{4,5},{5,4},{6,7},{7,6},{8,9},{9,8},{10,11... | collective-permute-start | bytes 890888 | tf_op jit(solution)/shard_map/ppermute | solution.py:299
  23.4 2.0 %collective-permute-start.14 = (bf16[1176,128]{1,0:T(8,128)(2,1)S(1)}, bf16[1176,128]{1,0:T(8,128)(2,1)S(1)}, u32[]{:S(2)}, u32[]{:S(2)}) collective-permute-start(bf16[1176,128]{1,0:T(8,128)(2,1)S(1)} %shard_map.38.refs_6_), channel_id=1, source_target_pairs={{0,1},{1,0},{2,3},{3,2},{4,5},{5,4},{6,7},{7,6},{8,9},{9,8},{10,11... | collective-permute-start | bytes 903176 | tf_op jit(solution)/shard_map/ppermute | solution.py:299

commit v7 on v6

--- a/solution.py
+++ b/solution.py
@@ -138,17 +138,22 @@
         return (clusters + 1 == ids).astype(jnp.bfloat16)
 
 
+def aligned(rows):
+    return -(-rows // 16) * 16
+
+
 def stack_kernel(*refs):
     *in_refs, out_ref = refs
     place = 0
     for in_ref in in_refs:
         out_ref[place : place + in_ref.shape[0], :] = in_ref[...]
-        place += in_ref.shape[0]
-
-
-def stack(*arrays, after=(), cost=None):
-    rows = sum(one.shape[0] for one in arrays)
-    return call(stack_kernel, [bf16(rows, arrays[0].shape[1])], arrays, after=after, cost=cost)[0]
+        place += aligned(in_ref.shape[0])
+
+
+def stack(*arrays, cost=None):
+    rows = sum(aligned(one.shape[0]) for one in arrays[:-1]) + arrays[-1].shape[0]
+    shape = jax.ShapeDtypeStruct((rows, arrays[0].shape[1]), arrays[0].dtype)
+    return call(stack_kernel, [shape], arrays, cost=cost)[0]
 
 
 def kern(rows, slots, slot_norms):
@@ -243,7 +248,7 @@
     parts = []
     for one, base, count, second in sets:
         n = [array is one for array in arrays].index(True)
-        for start in range(base, one.shape[0], 2 * count * width // LANES + ID_ROWS):
+        for start in range(base, one.shape[0], aligned(2 * count * width // LANES + ID_ROWS)):
             parts.append((n, start, count, second))
     return parts
 

time: 27.4 us -> 27.4 us (level)
  no operation moved by 1% of the time
where the time goes in v7:
time: 27.4 us; the launch traced here: 27.3 us
  starting transfers between devices  15 us (55%)
  waiting for transfers between devices  6.36 us (23%)
  Pallas kernels  4.29 us (16%)
  local copies, waits for them, and re-layouts  1.55 us (6%)
    ppermute x6, starting transfers between devices, over_row(): lax.ppermute(values, 'row', [(i, i ^ bits) for i in range(row_count)])  7.69 us
    ppermute x9, starting transfers between devices, over_col(): lax.ppermute(values, 'col', [(i, i ^ bits) for i in range(group_count)])  7.33 us
    pallas_call x12, Pallas kernels, call(): pl.pallas_call(body, out_shape=out_shape, in_specs=[VMEM] * count + [pl.B...  4.29 us
    ppermute x6, waiting for transfers between devices, over_row(): lax.ppermute(values, 'row', [(i, i ^ bits) for i in range(row_count)])  3.32 us
    ppermute x9, waiting for transfers between devices, over_col(): lax.ppermute(values, 'col', [(i, i ^ bits) for i in range(group_count)])  3.04 us
    unnamed x4, local copies, waits for them, and re-layouts  1.55 us
  transfers between devices with their start and end apart: 15, of which 6 were waited for; matrix products, arithmetic and copies ran while one was open for 0% of the time, Pallas kernels for 9%

profile of v7, /device:TPU:0, one launch (start us, length us, event | category | flops | bytes accessed | tf_op | source)
XLA Modules:
  0.0 27.3 jit_solution(15509927456166551613)
XLA Ops:
  0.0 4.0 %collective-permute-start.2 = (bf16[64,768]{1,0:T(8,128)(2,1)}, bf16[64,768]{1,0:T(8,128)(2,1)S(1)}, u32[]{:S(2)}, u32[]{:S(2)}) collective-permute-start(bf16[64,768]{1,0:T(8,128)(2,1)} %refs_0_.1), channel_id=1, source_target_pairs={{0,4},{1,5},{2,6},{3,7},{4,0},{5,1},{6,2},{7,3},{8,12},{9,13},{10,... | collective-permute-start | bytes 294920 | tf_op jit(solution)/shard_map/ppermute | solution.py:304
  4.0 1.6 %collective-permute-start = (bf16[64,768]{1,0:T(8,128)(2,1)}, bf16[64,768]{1,0:T(8,128)(2,1)S(1)}, u32[]{:S(2)}, u32[]{:S(2)}) collective-permute-start(bf16[64,768]{1,0:T(8,128)(2,1)} %refs_0_.1), channel_id=1, source_target_pairs={{0,2},{1,3},{2,0},{3,1},{4,6},{5,7},{6,4},{7,5},{8,10},{9,11},{10,... | collective-permute-start | bytes 294920 | tf_op jit(solution)/shard_map/ppermute | solution.py:304
  5.6 0.3 %collective-permute-start.3 = (s32[1,64]{1,0:T(1,128)}, s32[1,64]{1,0:T(1,128)S(1)}, u32[]{:S(2)}, u32[]{:S(2)}) collective-permute-start(s32[1,64]{1,0:T(1,128)} %bitcast.1), channel_id=1, source_target_pairs={{0,4},{1,5},{2,6},{3,7},{4,0},{5,1},{6,2},{7,3},{8,12},{9,13},{10,... | collective-permute-start | bytes 776 | tf_op jit(solution)/shard_map/ppermute | solution.py:304
  6.0 0.1 collective-permute-start.1
  6.1 0.0 copy-start
  6.1 0.9 %copy-done = bf16[64,768]{1,0:T(8,128)(2,1)S(1)} copy-done((bf16[64,768]{1,0:T(8,128)(2,1)S(1)}, bf16[64,768]{1,0:T(8,128)(2,1)}, u32[]{:S(2)}) %copy-start) | copy-done | bytes 98328
  7.0 0.0 copy-start.1
  7.0 0.7 %copy-done.1 = s32[64]{0:T(128)S(1)} copy-done((s32[64]{0:T(128)S(1)}, s32[64]{0:T(128)}, u32[]{:S(2)}) %copy-start.1) | copy-done | bytes 280
  7.6 0.1 shard_map.28.refs_0_
  7.7 1.3 %collective-permute-done.2.refs_0_ = bf16[64,768]{1,0:T(8,128)(2,1)S(1)} collective-permute-done((bf16[64,768]{1,0:T(8,128)(2,1)}, bf16[64,768]{1,0:T(8,128)(2,1)S(1)}, u32[]{:S(2)}, u32[]{:S(2)}) %collective-permute-start.2) | collective-permute-done | bytes 98336 | tf_op jit(solution)/shard_map/ppermute | solution.py:304
  9.1 1.1 %collective-permute-done.3.refs_1_ = s32[1,64]{1,0:T(1,128)S(1)} collective-permute-done((s32[1,64]{1,0:T(1,128)}, s32[1,64]{1,0:T(1,128)S(1)}, u32[]{:S(2)}, u32[]{:S(2)}) %collective-permute-start.3) | collective-permute-done | bytes 288 | tf_op jit(solution)/shard_map/ppermute | solution.py:304
  10.2 0.1 shard_map.32.refs_2_.refs_0_
  10.3 0.6 %collective-permute-start.4 = (bf16[392,128]{1,0:T(8,128)(2,1)S(1)}, bf16[392,128]{1,0:T(8,128)(2,1)S(1)}, u32[]{:S(2)}, u32[]{:S(2)}) collective-permute-start(bf16[392,128]{1,0:T(8,128)(2,1)S(1)} %shard_map.32.refs_2_.refs_0_), channel_id=1, source_target_pairs={{0,2},{1,3},{2,0},{3,1},{4,6},{5,7},{6,4},{7,5},{8,10},{9,11},{10,... | collective-permute-start | bytes 301064 | tf_op jit(solution)/shard_map/ppermute | solution.py:304
  10.9 0.0 collective-permute-done.refs_0_
  10.9 0.0 collective-permute-done.1.refs_1_
  10.9 0.1 shard_map.30.refs_1_
  11.0 0.4 %shard_map.33 = (bf16[1160,128]{1,0:T(8,128)(2,1)S(1)}, bf16[392,128]{1,0:T(8,128)(2,1)S(1)}) custom-call(bf16[392,128]{1,0:T(8,128)(2,1)S(1)} %shard_map.28.refs_0_, bf16[392,128]{1,0:T(8,128)(2,1)S(1)} %shard_map.30.refs_1_, bf16[392,128]{1,0:T(8,128)(2,1)S(1)} %shard_map.32.refs_2_.refs_0_), custom_call_target="tpu_custom_call" | custom-call | tf_op jit(solution)/shard_map/pallas_call | solution.py:33
  11.4 2.5 %collective-permute-start.7 = (bf16[392,128]{1,0:T(8,128)(2,1)S(1)}, bf16[392,128]{1,0:T(8,128)(2,1)S(1)}, u32[]{:S(2)}, u32[]{:S(2)}) collective-permute-start(bf16[392,128]{1,0:T(8,128)(2,1)S(1)} %get-tuple-element.15), channel_id=1, source_target_pairs={{0,24},{8,16},{16,8},{24,0},{1,25},{9,17},{17,9},{25,1},{2,26},{10... | collective-permute-start | bytes 301064 | tf_op jit(solution)/shard_map/ppermute | solution.py:307
  13.9 0.5 %collective-permute-start.8 = (bf16[392,128]{1,0:T(8,128)(2,1)S(1)}, bf16[392,128]{1,0:T(8,128)(2,1)S(1)}, u32[]{:S(2)}, u32[]{:S(2)}) collective-permute-start(bf16[392,128]{1,0:T(8,128)(2,1)S(1)} %get-tuple-element.15), channel_id=1, source_target_pairs={{0,16},{8,24},{16,0},{24,8},{1,17},{9,25},{17,1},{25,9},{2,18},{10... | collective-permute-start | bytes 301064 | tf_op jit(solution)/shard_map/ppermute | solution.py:307
  14.4 0.6 %collective-permute-start.9 = (bf16[392,128]{1,0:T(8,128)(2,1)S(1)}, bf16[392,128]{1,0:T(8,128)(2,1)S(1)}, u32[]{:S(2)}, u32[]{:S(2)}) collective-permute-start(bf16[392,128]{1,0:T(8,128)(2,1)S(1)} %get-tuple-element.15), channel_id=1, source_target_pairs={{0,8},{8,0},{16,24},{24,16},{1,9},{9,1},{17,25},{25,17},{2,10},{10... | collective-permute-start | bytes 301064 | tf_op jit(solution)/shard_map/ppermute | solution.py:307
  14.9 0.0 collective-permute-done.4.refs_0_
  15.0 0.4 %shard_map.35 = (bf16[1160,128]{1,0:T(8,128)(2,1)S(1)}, bf16[392,128]{1,0:T(8,128)(2,1)S(1)}) custom-call(bf16[392,128]{1,0:T(8,128)(2,1)S(1)} %shard_map.32.refs_2_.refs_0_, bf16[392,128]{1,0:T(8,128)(2,1)S(1)} %shard_map.34.refs_1_), custom_call_target="tpu_custom_call" | custom-call | tf_op jit(solution)/shard_map/pallas_call | solution.py:33
  15.3 2.5 %collective-permute-start.11 = (bf16[392,128]{1,0:T(8,128)(2,1)S(1)}, bf16[392,128]{1,0:T(8,128)(2,1)S(1)}, u32[]{:S(2)}, u32[]{:S(2)}) collective-permute-start(bf16[392,128]{1,0:T(8,128)(2,1)S(1)} %get-tuple-element.20), channel_id=1, source_target_pairs={{0,24},{8,16},{16,8},{24,0},{1,25},{9,17},{17,9},{25,1},{2,26},{10... | collective-permute-start | bytes 301064 | tf_op jit(solution)/shard_map/ppermute | solution.py:307
  17.8 0.5 %collective-permute-start.12 = (bf16[392,128]{1,0:T(8,128)(2,1)S(1)}, bf16[392,128]{1,0:T(8,128)(2,1)S(1)}, u32[]{:S(2)}, u32[]{:S(2)}) collective-permute-start(bf16[392,128]{1,0:T(8,128)(2,1)S(1)} %get-tuple-element.20), channel_id=1, source_target_pairs={{0,16},{8,24},{16,0},{24,8},{1,17},{9,25},{17,1},{25,9},{2,18},{10... | collective-permute-start | bytes 301064 | tf_op jit(solution)/shard_map/ppermute | solution.py:307
  18.3 0.0 collective-permute-done.7.refs_0_
  18.3 1.1 %collective-permute-start.13 = (bf16[392,128]{1,0:T(8,128)(2,1)S(1)}, bf16[392,128]{1,0:T(8,128)(2,1)S(1)}, u32[]{:S(2)}, u32[]{:S(2)}) collective-permute-start(bf16[392,128]{1,0:T(8,128)(2,1)S(1)} %get-tuple-element.20), channel_id=1, source_target_pairs={{0,8},{8,0},{16,24},{24,16},{1,9},{9,1},{17,25},{25,17},{2,10},{10... | collective-permute-start | bytes 301064 | tf_op jit(solution)/shard_map/ppermute | solution.py:307
  19.5 1.0 %collective-permute-done.8.refs_1_ = bf16[392,128]{1,0:T(8,128)(2,1)S(1)} collective-permute-done((bf16[392,128]{1,0:T(8,128)(2,1)S(1)}, bf16[392,128]{1,0:T(8,128)(2,1)S(1)}, u32[]{:S(2)}, u32[]{:S(2)}) %collective-permute-start.8) | collective-permute-done | bytes 100384 | tf_op jit(solution)/shard_map/ppermute | solution.py:307
  20.4 0.0 collective-permute-done.9.refs_2_
  20.5 0.1 collective-permute-start.10
  20.5 0.5 %collective-permute-start.5 = (bf16[1160,128]{1,0:T(8,128)(2,1)S(1)}, bf16[1160,128]{1,0:T(8,128)(2,1)S(1)}, u32[]{:S(2)}, u32[]{:S(2)}) collective-permute-start(bf16[1160,128]{1,0:T(8,128)(2,1)S(1)} %get-tuple-element.13.refs_0_), channel_id=1, source_target_pairs={{0,1},{1,0},{2,3},{3,2},{4,5},{5,4},{6,7},{7,6},{8,9},{9,8},{10,11... | collective-permute-start | bytes 890888 | tf_op jit(solution)/shard_map/ppermute | solution.py:304
  21.0 1.4 %collective-permute-done.11.refs_0_ = bf16[392,128]{1,0:T(8,128)(2,1)S(1)} collective-permute-done((bf16[392,128]{1,0:T(8,128)(2,1)S(1)}, bf16[392,128]{1,0:T(8,128)(2,1)S(1)}, u32[]{:S(2)}, u32[]{:S(2)}) %collective-permute-start.11) | collective-permute-done | bytes 100384 | tf_op jit(solution)/shard_map/ppermute | solution.py:307
  22.5 0.0 collective-permute-start.6
  22.5 0.9 %collective-permute-done.12.refs_1_ = bf16[392,128]{1,0:T(8,128)(2,1)S(1)} collective-permute-done((bf16[392,128]{1,0:T(8,128)(2,1)S(1)}, bf16[392,128]{1,0:T(8,128)(2,1)S(1)}, u32[]{:S(2)}, u32[]{:S(2)}) %collective-permute-start.12) | collective-permute-done | bytes 100384 | tf_op jit(solution)/shard_map/ppermute | solution.py:307
  23.4 0.0 collective-permute-done.13.refs_2_
  23.4 0.1 collective-permute-start.14
  23.5 0.0 collective-permute-done.5.refs_2_
  23.5 0.6 %collective-permute-done.6.refs_3_.refs_5_ = bf16[1160,128]{1,0:T(8,128)(2,1)S(1)} collective-permute-done((bf16[1160,128]{1,0:T(8,128)(2,1)S(1)}, bf16[1160,128]{1,0:T(8,128)(2,1)S(1)}, u32[]{:S(2)}, u32[]{:S(2)}) %collective-permute-start.6) | collective-permute-done | bytes 296992 | tf_op jit(solution)/shard_map/ppermute | solution.py:304
  24.1 0.0 collective-permute-done.10.refs_5_
  24.1 1.3 %shard_map.37 = (bf16[768,768]{1,0:T(8,128)(2,1)S(1)}, bf16[128,256]{1,0:T(8,128)(2,1)S(1)}, f32[512,128]{1,0:T(8,128)S(1)}, f32[16,128]{1,0:T(8,128)S(1)}) custom-call(bf16[1160,128]{1,0:T(8,128)(2,1)S(1)} %get-tuple-element.13.refs_0_, bf16[1160,128]{1,0:T(8,128)(2,1)S(1)} %get-tuple-element.14.refs_1_.refs_4_, ...), custom_call_target="tpu_custom_call" | custom-call | flops 352321536 | bytes 1179648 | tf_op jit(solution)/shard_map/pallas_call | solution.py:33
  25.4 0.0 collective-permute-done.14.refs_7_
  25.4 1.9 %shard_map.39 = f32[512,128]{1,0:T(8,128)} custom-call(bf16[768,768]{1,0:T(8,128)(2,1)S(1)} %get-tuple-element.16.refs_0_, bf16[128,256]{1,0:T(8,128)(2,1)S(1)} %get-tuple-element.17.refs_1_, f32[512,128]{1,0:T(8,128)S(1)} %get-tuple-element.18.refs_2_, f32[16,128]{1,0:T(8,128)S(1)} %get-tuple-element.19.refs_3_, ...), custom_call_target="tpu_custom_call" | custom-call | flops 469762048 | bytes 1572864 | tf_op jit(solution)/shard_map/pallas_call | solution.py:33
  (5 shorter events, 0.1 us)
Async XLA Ops:
  0.0 9.0 %collective-permute-start.2 = (bf16[64,768]{1,0:T(8,128)(2,1)}, bf16[64,768]{1,0:T(8,128)(2,1)S(1)}, u32[]{:S(2)}, u32[]{:S(2)}) collective-permute-start(bf16[64,768]{1,0:T(8,128)(2,1)} %refs_0_.1), channel_id=1, source_target_pairs={{0,4},{1,5},{2,6},{3,7},{4,0},{5,1},{6,2},{7,3},{8,12},{9,13},{10,... | collective-permute-start | bytes 294920 | tf_op jit(solution)/shard_map/ppermute | solution.py:304
  4.0 6.9 %collective-permute-start = (bf16[64,768]{1,0:T(8,128)(2,1)}, bf16[64,768]{1,0:T(8,128)(2,1)S(1)}, u32[]{:S(2)}, u32[]{:S(2)}) collective-permute-start(bf16[64,768]{1,0:T(8,128)(2,1)} %refs_0_.1), channel_id=1, source_target_pairs={{0,2},{1,3},{2,0},{3,1},{4,6},{5,7},{6,4},{7,5},{8,10},{9,11},{10,... | collective-permute-start | bytes 294920 | tf_op jit(solution)/shard_map/ppermute | solution.py:304
  5.6 4.6 %collective-permute-start.3 = (s32[1,64]{1,0:T(1,128)}, s32[1,64]{1,0:T(1,128)S(1)}, u32[]{:S(2)}, u32[]{:S(2)}) collective-permute-start(s32[1,64]{1,0:T(1,128)} %bitcast.1), channel_id=1, source_target_pairs={{0,4},{1,5},{2,6},{3,7},{4,0},{5,1},{6,2},{7,3},{8,12},{9,13},{10,... | collective-permute-start | bytes 776 | tf_op jit(solution)/shard_map/ppermute | solution.py:304
  6.0 5.0 %collective-permute-start.1 = (s32[1,64]{1,0:T(1,128)}, s32[1,64]{1,0:T(1,128)S(1)}, u32[]{:S(2)}, u32[]{:S(2)}) collective-permute-start(s32[1,64]{1,0:T(1,128)} %bitcast.2), channel_id=1, source_target_pairs={{0,2},{1,3},{2,0},{3,1},{4,6},{5,7},{6,4},{7,5},{8,10},{9,11},{10,... | collective-permute-start | bytes 776 | tf_op jit(solution)/shard_map/ppermute | solution.py:304
  6.1 0.9 %copy-start = (bf16[64,768]{1,0:T(8,128)(2,1)S(1)}, bf16[64,768]{1,0:T(8,128)(2,1)}, u32[]{:S(2)}) copy-start(bf16[64,768]{1,0:T(8,128)(2,1)} %refs_0_.1) | copy-start | bytes 294916
  7.0 0.7 %copy-start.1 = (s32[64]{0:T(128)S(1)}, s32[64]{0:T(128)}, u32[]{:S(2)}) copy-start(s32[64]{0:T(128)} %param.3) | copy-start | bytes 772
  10.3 4.7 %collective-permute-start.4 = (bf16[392,128]{1,0:T(8,128)(2,1)S(1)}, bf16[392,128]{1,0:T(8,128)(2,1)S(1)}, u32[]{:S(2)}, u32[]{:S(2)}) collective-permute-start(bf16[392,128]{1,0:T(8,128)(2,1)S(1)} %shard_map.32.refs_2_.refs_0_), channel_id=1, source_target_pairs={{0,2},{1,3},{2,0},{3,1},{4,6},{5,7},{6,4},{7,5},{8,10},{9,11},{10,... | collective-permute-start | bytes 301064 | tf_op jit(solution)/shard_map/ppermute | solution.py:304
  11.4 6.9 %collective-permute-start.7 = (bf16[392,128]{1,0:T(8,128)(2,1)S(1)}, bf16[392,128]{1,0:T(8,128)(2,1)S(1)}, u32[]{:S(2)}, u32[]{:S(2)}) collective-permute-start(bf16[392,128]{1,0:T(8,128)(2,1)S(1)} %get-tuple-element.15), channel_id=1, source_target_pairs={{0,24},{8,16},{16,8},{24,0},{1,25},{9,17},{17,9},{25,1},{2,26},{10... | collective-permute-start | bytes 301064 | tf_op jit(solution)/shard_map/ppermute | solution.py:307
  13.9 6.6 %collective-permute-start.8 = (bf16[392,128]{1,0:T(8,128)(2,1)S(1)}, bf16[392,128]{1,0:T(8,128)(2,1)S(1)}, u32[]{:S(2)}, u32[]{:S(2)}) collective-permute-start(bf16[392,128]{1,0:T(8,128)(2,1)S(1)} %get-tuple-element.15), channel_id=1, source_target_pairs={{0,16},{8,24},{16,0},{24,8},{1,17},{9,25},{17,1},{25,9},{2,18},{10... | collective-permute-start | bytes 301064 | tf_op jit(solution)/shard_map/ppermute | solution.py:307
  14.4 6.1 %collective-permute-start.9 = (bf16[392,128]{1,0:T(8,128)(2,1)S(1)}, bf16[392,128]{1,0:T(8,128)(2,1)S(1)}, u32[]{:S(2)}, u32[]{:S(2)}) collective-permute-start(bf16[392,128]{1,0:T(8,128)(2,1)S(1)} %get-tuple-element.15), channel_id=1, source_target_pairs={{0,8},{8,0},{16,24},{24,16},{1,9},{9,1},{17,25},{25,17},{2,10},{10... | collective-permute-start | bytes 301064 | tf_op jit(solution)/shard_map/ppermute | solution.py:307
  15.3 7.1 %collective-permute-start.11 = (bf16[392,128]{1,0:T(8,128)(2,1)S(1)}, bf16[392,128]{1,0:T(8,128)(2,1)S(1)}, u32[]{:S(2)}, u32[]{:S(2)}) collective-permute-start(bf16[392,128]{1,0:T(8,128)(2,1)S(1)} %get-tuple-element.20), channel_id=1, source_target_pairs={{0,24},{8,16},{16,8},{24,0},{1,25},{9,17},{17,9},{25,1},{2,26},{10... | collective-permute-start | bytes 301064 | tf_op jit(solution)/shard_map/ppermute | solution.py:307
  17.8 5.6 %collective-permute-start.12 = (bf16[392,128]{1,0:T(8,128)(2,1)S(1)}, bf16[392,128]{1,0:T(8,128)(2,1)S(1)}, u32[]{:S(2)}, u32[]{:S(2)}) collective-permute-start(bf16[392,128]{1,0:T(8,128)(2,1)S(1)} %get-tuple-element.20), channel_id=1, source_target_pairs={{0,16},{8,24},{16,0},{24,8},{1,17},{9,25},{17,1},{25,9},{2,18},{10... | collective-permute-start | bytes 301064 | tf_op jit(solution)/shard_map/ppermute | solution.py:307
  18.3 5.1 %collective-permute-start.13 = (bf16[392,128]{1,0:T(8,128)(2,1)S(1)}, bf16[392,128]{1,0:T(8,128)(2,1)S(1)}, u32[]{:S(2)}, u32[]{:S(2)}) collective-permute-start(bf16[392,128]{1,0:T(8,128)(2,1)S(1)} %get-tuple-element.20), channel_id=1, source_target_pairs={{0,8},{8,0},{16,24},{24,16},{1,9},{9,1},{17,25},{25,17},{2,10},{10... | collective-permute-start | bytes 301064 | tf_op jit(solution)/shard_map/ppermute | solution.py:307
  20.5 3.6 %collective-permute-start.10 = (bf16[1192,128]{1,0:T(8,128)(2,1)S(1)}, bf16[1192,128]{1,0:T(8,128)(2,1)S(1)}, u32[]{:S(2)}, u32[]{:S(2)}) collective-permute-start(bf16[1192,128]{1,0:T(8,128)(2,1)S(1)} %shard_map.36.refs_4_), channel_id=1, source_target_pairs={{0,1},{1,0},{2,3},{3,2},{4,5},{5,4},{6,7},{7,6},{8,9},{9,8},{10,11... | collective-permute-start | bytes 915464 | tf_op jit(solution)/shard_map/ppermute | solution.py:304
  20.5 3.0 %collective-permute-start.5 = (bf16[1160,128]{1,0:T(8,128)(2,1)S(1)}, bf16[1160,128]{1,0:T(8,128)(2,1)S(1)}, u32[]{:S(2)}, u32[]{:S(2)}) collective-permute-start(bf16[1160,128]{1,0:T(8,128)(2,1)S(1)} %get-tuple-element.13.refs_0_), channel_id=1, source_target_pairs={{0,1},{1,0},{2,3},{3,2},{4,5},{5,4},{6,7},{7,6},{8,9},{9,8},{10,11... | collective-permute-start | bytes 890888 | tf_op jit(solution)/shard_map/ppermute | solution.py:304
  22.5 1.6 %collective-permute-start.6 = (bf16[1160,128]{1,0:T(8,128)(2,1)S(1)}, bf16[1160,128]{1,0:T(8,128)(2,1)S(1)}, u32[]{:S(2)}, u32[]{:S(2)}) collective-permute-start(bf16[1160,128]{1,0:T(8,128)(2,1)S(1)} %get-tuple-element.14.refs_1_.refs_4_), channel_id=1, source_target_pairs={{0,1},{1,0},{2,3},{3,2},{4,5},{5,4},{6,7},{7,6},{8,9},{9,8},{10,11... | collective-permute-start | bytes 890888 | tf_op jit(solution)/shard_map/ppermute | solution.py:304
  23.4 2.0 %collective-permute-start.14 = (bf16[1192,128]{1,0:T(8,128)(2,1)S(1)}, bf16[1192,128]{1,0:T(8,128)(2,1)S(1)}, u32[]{:S(2)}, u32[]{:S(2)}) collective-permute-start(bf16[1192,128]{1,0:T(8,128)(2,1)S(1)} %shard_map.38.refs_6_), channel_id=1, source_target_pairs={{0,1},{1,0},{2,3},{3,2},{4,5},{5,4},{6,7},{7,6},{8,9},{9,8},{10,11... | collective-permute-start | bytes 915464 | tf_op jit(solution)/shard_map/ppermute | solution.py:304

commit v8 on v7

--- a/solution.py
+++ b/solution.py
@@ -334,7 +334,7 @@
             [pltpu.VMEM((len(batch) * own_count, width), jnp.bfloat16)],
             after=[] if last else [blocks[far]],
         )
-        got = [over_row(sets, bits) for bits in range(row_count - 1, 0, -1)]
+        got = [over_row(sets, bits) for bits in sorted(range(1, row_count), key=lambda bits: (-bits.bit_count(), bits if last else -bits))]
         places.append([2 * q for q in batch])
         near.append((here, base, half))
         last.append((got, 0, half))

time: 27.4 us -> 27.4 us (level)
  transfers between devices with their start and end apart: 15 -> 15, of which waited for: 6 -> 7; matrix products, arithmetic and copies ran while one was open for 0% -> 0% of each run, Pallas kernels for 9% -> 9%
where the time goes in v8:
time: 27.4 us; the launch traced here: 27.2 us
  starting transfers between devices  14.9 us (54%)
  waiting for transfers between devices  6.39 us (23%)
  Pallas kernels  4.29 us (16%)
  local copies, waits for them, and re-layouts  1.55 us (6%)
    ppermute x6, starting transfers between devices, over_row(): lax.ppermute(values, 'row', [(i, i ^ bits) for i in range(row_count)])  7.6 us
    ppermute x9, starting transfers between devices, over_col(): lax.ppermute(values, 'col', [(i, i ^ bits) for i in range(group_count)])  7.33 us
    pallas_call x12, Pallas kernels, call(): pl.pallas_call(body, out_shape=out_shape, in_specs=[VMEM] * count + [pl.B...  4.29 us
    ppermute x6, waiting for transfers between devices, over_row(): lax.ppermute(values, 'row', [(i, i ^ bits) for i in range(row_count)])  3.46 us
    ppermute x9, waiting for transfers between devices, over_col(): lax.ppermute(values, 'col', [(i, i ^ bits) for i in range(group_count)])  2.93 us
    unnamed x4, local copies, waits for them, and re-layouts  1.55 us
  transfers between devices with their start and end apart: 15, of which 7 were waited for; matrix products, arithmetic and copies ran while one was open for 0% of the time, Pallas kernels for 9%

profile of v8, /device:TPU:0, one launch (start us, length us, event | category | flops | bytes accessed | tf_op | source)
XLA Modules:
  0.0 27.2 jit_solution(18017270547986062135)
XLA Ops:
  0.0 4.0 %collective-permute-start.2 = (bf16[64,768]{1,0:T(8,128)(2,1)}, bf16[64,768]{1,0:T(8,128)(2,1)S(1)}, u32[]{:S(2)}, u32[]{:S(2)}) collective-permute-start(bf16[64,768]{1,0:T(8,128)(2,1)} %refs_0_.1), channel_id=1, source_target_pairs={{0,4},{1,5},{2,6},{3,7},{4,0},{5,1},{6,2},{7,3},{8,12},{9,13},{10,... | collective-permute-start | bytes 294920 | tf_op jit(solution)/shard_map/ppermute | solution.py:304
  4.0 1.6 %collective-permute-start = (bf16[64,768]{1,0:T(8,128)(2,1)}, bf16[64,768]{1,0:T(8,128)(2,1)S(1)}, u32[]{:S(2)}, u32[]{:S(2)}) collective-permute-start(bf16[64,768]{1,0:T(8,128)(2,1)} %refs_0_.1), channel_id=1, source_target_pairs={{0,2},{1,3},{2,0},{3,1},{4,6},{5,7},{6,4},{7,5},{8,10},{9,11},{10,... | collective-permute-start | bytes 294920 | tf_op jit(solution)/shard_map/ppermute | solution.py:304
  5.6 0.3 %collective-permute-start.3 = (s32[1,64]{1,0:T(1,128)}, s32[1,64]{1,0:T(1,128)S(1)}, u32[]{:S(2)}, u32[]{:S(2)}) collective-permute-start(s32[1,64]{1,0:T(1,128)} %bitcast.1), channel_id=1, source_target_pairs={{0,4},{1,5},{2,6},{3,7},{4,0},{5,1},{6,2},{7,3},{8,12},{9,13},{10,... | collective-permute-start | bytes 776 | tf_op jit(solution)/shard_map/ppermute | solution.py:304
  6.0 0.1 collective-permute-start.1
  6.1 0.0 copy-start
  6.1 0.9 %copy-done = bf16[64,768]{1,0:T(8,128)(2,1)S(1)} copy-done((bf16[64,768]{1,0:T(8,128)(2,1)S(1)}, bf16[64,768]{1,0:T(8,128)(2,1)}, u32[]{:S(2)}) %copy-start) | copy-done | bytes 98328
  7.0 0.0 copy-start.1
  7.0 0.7 %copy-done.1 = s32[64]{0:T(128)S(1)} copy-done((s32[64]{0:T(128)S(1)}, s32[64]{0:T(128)}, u32[]{:S(2)}) %copy-start.1) | copy-done | bytes 280
  7.6 0.1 shard_map.28.refs_0_
  7.7 1.3 %collective-permute-done.2.refs_0_ = bf16[64,768]{1,0:T(8,128)(2,1)S(1)} collective-permute-done((bf16[64,768]{1,0:T(8,128)(2,1)}, bf16[64,768]{1,0:T(8,128)(2,1)S(1)}, u32[]{:S(2)}, u32[]{:S(2)}) %collective-permute-start.2) | collective-permute-done | bytes 98336 | tf_op jit(solution)/shard_map/ppermute | solution.py:304
  9.1 1.1 %collective-permute-done.3.refs_1_ = s32[1,64]{1,0:T(1,128)S(1)} collective-permute-done((s32[1,64]{1,0:T(1,128)}, s32[1,64]{1,0:T(1,128)S(1)}, u32[]{:S(2)}, u32[]{:S(2)}) %collective-permute-start.3) | collective-permute-done | bytes 288 | tf_op jit(solution)/shard_map/ppermute | solution.py:304
  10.2 0.1 shard_map.32.refs_2_.refs_0_
  10.3 0.6 %collective-permute-start.4 = (bf16[392,128]{1,0:T(8,128)(2,1)S(1)}, bf16[392,128]{1,0:T(8,128)(2,1)S(1)}, u32[]{:S(2)}, u32[]{:S(2)}) collective-permute-start(bf16[392,128]{1,0:T(8,128)(2,1)S(1)} %shard_map.32.refs_2_.refs_0_), channel_id=1, source_target_pairs={{0,2},{1,3},{2,0},{3,1},{4,6},{5,7},{6,4},{7,5},{8,10},{9,11},{10,... | collective-permute-start | bytes 301064 | tf_op jit(solution)/shard_map/ppermute | solution.py:304
  10.9 0.0 collective-permute-done.refs_0_
  10.9 0.0 collective-permute-done.1.refs_1_
  10.9 0.1 shard_map.30.refs_1_
  11.0 0.4 %shard_map.33 = (bf16[1160,128]{1,0:T(8,128)(2,1)S(1)}, bf16[392,128]{1,0:T(8,128)(2,1)S(1)}) custom-call(bf16[392,128]{1,0:T(8,128)(2,1)S(1)} %shard_map.28.refs_0_, bf16[392,128]{1,0:T(8,128)(2,1)S(1)} %shard_map.30.refs_1_, bf16[392,128]{1,0:T(8,128)(2,1)S(1)} %shard_map.32.refs_2_.refs_0_), custom_call_target="tpu_custom_call" | custom-call | tf_op jit(solution)/shard_map/pallas_call | solution.py:33
  11.4 2.5 %collective-permute-start.7 = (bf16[392,128]{1,0:T(8,128)(2,1)S(1)}, bf16[392,128]{1,0:T(8,128)(2,1)S(1)}, u32[]{:S(2)}, u32[]{:S(2)}) collective-permute-start(bf16[392,128]{1,0:T(8,128)(2,1)S(1)} %get-tuple-element.15), channel_id=1, source_target_pairs={{0,24},{8,16},{16,8},{24,0},{1,25},{9,17},{17,9},{25,1},{2,26},{10... | collective-permute-start | bytes 301064 | tf_op jit(solution)/shard_map/ppermute | solution.py:307
  13.9 0.5 %collective-permute-start.8 = (bf16[392,128]{1,0:T(8,128)(2,1)S(1)}, bf16[392,128]{1,0:T(8,128)(2,1)S(1)}, u32[]{:S(2)}, u32[]{:S(2)}) collective-permute-start(bf16[392,128]{1,0:T(8,128)(2,1)S(1)} %get-tuple-element.15), channel_id=1, source_target_pairs={{0,16},{8,24},{16,0},{24,8},{1,17},{9,25},{17,1},{25,9},{2,18},{10... | collective-permute-start | bytes 301064 | tf_op jit(solution)/shard_map/ppermute | solution.py:307
  14.4 0.6 %collective-permute-start.9 = (bf16[392,128]{1,0:T(8,128)(2,1)S(1)}, bf16[392,128]{1,0:T(8,128)(2,1)S(1)}, u32[]{:S(2)}, u32[]{:S(2)}) collective-permute-start(bf16[392,128]{1,0:T(8,128)(2,1)S(1)} %get-tuple-element.15), channel_id=1, source_target_pairs={{0,8},{8,0},{16,24},{24,16},{1,9},{9,1},{17,25},{25,17},{2,10},{10... | collective-permute-start | bytes 301064 | tf_op jit(solution)/shard_map/ppermute | solution.py:307
  14.9 0.0 collective-permute-done.4.refs_0_
  15.0 0.4 %shard_map.35 = (bf16[1160,128]{1,0:T(8,128)(2,1)S(1)}, bf16[392,128]{1,0:T(8,128)(2,1)S(1)}) custom-call(bf16[392,128]{1,0:T(8,128)(2,1)S(1)} %shard_map.32.refs_2_.refs_0_, bf16[392,128]{1,0:T(8,128)(2,1)S(1)} %shard_map.34.refs_1_), custom_call_target="tpu_custom_call" | custom-call | tf_op jit(solution)/shard_map/pallas_call | solution.py:33
  15.3 2.5 %collective-permute-start.11 = (bf16[392,128]{1,0:T(8,128)(2,1)S(1)}, bf16[392,128]{1,0:T(8,128)(2,1)S(1)}, u32[]{:S(2)}, u32[]{:S(2)}) collective-permute-start(bf16[392,128]{1,0:T(8,128)(2,1)S(1)} %get-tuple-element.20), channel_id=1, source_target_pairs={{0,24},{8,16},{16,8},{24,0},{1,25},{9,17},{17,9},{25,1},{2,26},{10... | collective-permute-start | bytes 301064 | tf_op jit(solution)/shard_map/ppermute | solution.py:307
  17.8 0.5 %collective-permute-start.12 = (bf16[392,128]{1,0:T(8,128)(2,1)S(1)}, bf16[392,128]{1,0:T(8,128)(2,1)S(1)}, u32[]{:S(2)}, u32[]{:S(2)}) collective-permute-start(bf16[392,128]{1,0:T(8,128)(2,1)S(1)} %get-tuple-element.20), channel_id=1, source_target_pairs={{0,8},{8,0},{16,24},{24,16},{1,9},{9,1},{17,25},{25,17},{2,10},{10... | collective-permute-start | bytes 301064 | tf_op jit(solution)/shard_map/ppermute | solution.py:307
  18.3 0.0 collective-permute-done.7.refs_0_
  18.4 1.0 %collective-permute-start.13 = (bf16[392,128]{1,0:T(8,128)(2,1)S(1)}, bf16[392,128]{1,0:T(8,128)(2,1)S(1)}, u32[]{:S(2)}, u32[]{:S(2)}) collective-permute-start(bf16[392,128]{1,0:T(8,128)(2,1)S(1)} %get-tuple-element.20), channel_id=1, source_target_pairs={{0,16},{8,24},{16,0},{24,8},{1,17},{9,25},{17,1},{25,9},{2,18},{10... | collective-permute-start | bytes 301064 | tf_op jit(solution)/shard_map/ppermute | solution.py:307
  19.4 1.0 %collective-permute-done.8.refs_1_ = bf16[392,128]{1,0:T(8,128)(2,1)S(1)} collective-permute-done((bf16[392,128]{1,0:T(8,128)(2,1)S(1)}, bf16[392,128]{1,0:T(8,128)(2,1)S(1)}, u32[]{:S(2)}, u32[]{:S(2)}) %collective-permute-start.8) | collective-permute-done | bytes 100384 | tf_op jit(solution)/shard_map/ppermute | solution.py:307
  20.4 0.0 collective-permute-done.9.refs_2_
  20.4 0.1 collective-permute-start.10
  20.5 0.5 %collective-permute-start.5 = (bf16[1160,128]{1,0:T(8,128)(2,1)S(1)}, bf16[1160,128]{1,0:T(8,128)(2,1)S(1)}, u32[]{:S(2)}, u32[]{:S(2)}) collective-permute-start(bf16[1160,128]{1,0:T(8,128)(2,1)S(1)} %get-tuple-element.13.refs_0_), channel_id=1, source_target_pairs={{0,1},{1,0},{2,3},{3,2},{4,5},{5,4},{6,7},{7,6},{8,9},{9,8},{10,11... | collective-permute-start | bytes 890888 | tf_op jit(solution)/shard_map/ppermute | solution.py:304
  21.0 1.4 %collective-permute-done.11.refs_0_ = bf16[392,128]{1,0:T(8,128)(2,1)S(1)} collective-permute-done((bf16[392,128]{1,0:T(8,128)(2,1)S(1)}, bf16[392,128]{1,0:T(8,128)(2,1)S(1)}, u32[]{:S(2)}, u32[]{:S(2)}) %collective-permute-start.11) | collective-permute-done | bytes 100384 | tf_op jit(solution)/shard_map/ppermute | solution.py:307
  22.4 0.0 collective-permute-start.6
  22.4 0.3 %collective-permute-done.12.refs_1_ = bf16[392,128]{1,0:T(8,128)(2,1)S(1)} collective-permute-done((bf16[392,128]{1,0:T(8,128)(2,1)S(1)}, bf16[392,128]{1,0:T(8,128)(2,1)S(1)}, u32[]{:S(2)}, u32[]{:S(2)}) %collective-permute-start.12) | collective-permute-done | bytes 100384 | tf_op jit(solution)/shard_map/ppermute | solution.py:307
  22.8 0.7 %collective-permute-done.13.refs_2_ = bf16[392,128]{1,0:T(8,128)(2,1)S(1)} collective-permute-done((bf16[392,128]{1,0:T(8,128)(2,1)S(1)}, bf16[392,128]{1,0:T(8,128)(2,1)S(1)}, u32[]{:S(2)}, u32[]{:S(2)}) %collective-permute-start.13) | collective-permute-done | bytes 100384 | tf_op jit(solution)/shard_map/ppermute | solution.py:307
  23.5 0.1 collective-permute-start.14
  23.5 0.0 collective-permute-done.5.refs_2_
  23.6 0.4 %collective-permute-done.6.refs_3_.refs_5_ = bf16[1160,128]{1,0:T(8,128)(2,1)S(1)} collective-permute-done((bf16[1160,128]{1,0:T(8,128)(2,1)S(1)}, bf16[1160,128]{1,0:T(8,128)(2,1)S(1)}, u32[]{:S(2)}, u32[]{:S(2)}) %collective-permute-start.6) | collective-permute-done | bytes 296992 | tf_op jit(solution)/shard_map/ppermute | solution.py:304
  24.0 0.0 collective-permute-done.10.refs_5_
  24.0 1.3 %shard_map.37 = (bf16[768,768]{1,0:T(8,128)(2,1)S(1)}, bf16[128,256]{1,0:T(8,128)(2,1)S(1)}, f32[512,128]{1,0:T(8,128)S(1)}, f32[16,128]{1,0:T(8,128)S(1)}) custom-call(bf16[1160,128]{1,0:T(8,128)(2,1)S(1)} %get-tuple-element.13.refs_0_, bf16[1160,128]{1,0:T(8,128)(2,1)S(1)} %get-tuple-element.14.refs_1_.refs_4_, ...), custom_call_target="tpu_custom_call" | custom-call | flops 352321536 | bytes 1179648 | tf_op jit(solution)/shard_map/pallas_call | solution.py:33
  25.3 0.0 collective-permute-done.14.refs_7_
  25.4 1.9 %shard_map.39 = f32[512,128]{1,0:T(8,128)} custom-call(bf16[768,768]{1,0:T(8,128)(2,1)S(1)} %get-tuple-element.16.refs_0_, bf16[128,256]{1,0:T(8,128)(2,1)S(1)} %get-tuple-element.17.refs_1_, f32[512,128]{1,0:T(8,128)S(1)} %get-tuple-element.18.refs_2_, f32[16,128]{1,0:T(8,128)S(1)} %get-tuple-element.19.refs_3_, ...), custom_call_target="tpu_custom_call" | custom-call | flops 469762048 | bytes 1572864 | tf_op jit(solution)/shard_map/pallas_call | solution.py:33
  (5 shorter events, 0.1 us)
Async XLA Ops:
  0.0 9.0 %collective-permute-start.2 = (bf16[64,768]{1,0:T(8,128)(2,1)}, bf16[64,768]{1,0:T(8,128)(2,1)S(1)}, u32[]{:S(2)}, u32[]{:S(2)}) collective-permute-start(bf16[64,768]{1,0:T(8,128)(2,1)} %refs_0_.1), channel_id=1, source_target_pairs={{0,4},{1,5},{2,6},{3,7},{4,0},{5,1},{6,2},{7,3},{8,12},{9,13},{10,... | collective-permute-start | bytes 294920 | tf_op jit(solution)/shard_map/ppermute | solution.py:304
  4.0 6.9 %collective-permute-start = (bf16[64,768]{1,0:T(8,128)(2,1)}, bf16[64,768]{1,0:T(8,128)(2,1)S(1)}, u32[]{:S(2)}, u32[]{:S(2)}) collective-permute-start(bf16[64,768]{1,0:T(8,128)(2,1)} %refs_0_.1), channel_id=1, source_target_pairs={{0,2},{1,3},{2,0},{3,1},{4,6},{5,7},{6,4},{7,5},{8,10},{9,11},{10,... | collective-permute-start | bytes 294920 | tf_op jit(solution)/shard_map/ppermute | solution.py:304
  5.6 4.6 %collective-permute-start.3 = (s32[1,64]{1,0:T(1,128)}, s32[1,64]{1,0:T(1,128)S(1)}, u32[]{:S(2)}, u32[]{:S(2)}) collective-permute-start(s32[1,64]{1,0:T(1,128)} %bitcast.1), channel_id=1, source_target_pairs={{0,4},{1,5},{2,6},{3,7},{4,0},{5,1},{6,2},{7,3},{8,12},{9,13},{10,... | collective-permute-start | bytes 776 | tf_op jit(solution)/shard_map/ppermute | solution.py:304
  6.0 5.0 %collective-permute-start.1 = (s32[1,64]{1,0:T(1,128)}, s32[1,64]{1,0:T(1,128)S(1)}, u32[]{:S(2)}, u32[]{:S(2)}) collective-permute-start(s32[1,64]{1,0:T(1,128)} %bitcast.2), channel_id=1, source_target_pairs={{0,2},{1,3},{2,0},{3,1},{4,6},{5,7},{6,4},{7,5},{8,10},{9,11},{10,... | collective-permute-start | bytes 776 | tf_op jit(solution)/shard_map/ppermute | solution.py:304
  6.1 0.9 %copy-start = (bf16[64,768]{1,0:T(8,128)(2,1)S(1)}, bf16[64,768]{1,0:T(8,128)(2,1)}, u32[]{:S(2)}) copy-start(bf16[64,768]{1,0:T(8,128)(2,1)} %refs_0_.1) | copy-start | bytes 294916
  7.0 0.7 %copy-start.1 = (s32[64]{0:T(128)S(1)}, s32[64]{0:T(128)}, u32[]{:S(2)}) copy-start(s32[64]{0:T(128)} %param.3) | copy-start | bytes 772
  10.3 4.7 %collective-permute-start.4 = (bf16[392,128]{1,0:T(8,128)(2,1)S(1)}, bf16[392,128]{1,0:T(8,128)(2,1)S(1)}, u32[]{:S(2)}, u32[]{:S(2)}) collective-permute-start(bf16[392,128]{1,0:T(8,128)(2,1)S(1)} %shard_map.32.refs_2_.refs_0_), channel_id=1, source_target_pairs={{0,2},{1,3},{2,0},{3,1},{4,6},{5,7},{6,4},{7,5},{8,10},{9,11},{10,... | collective-permute-start | bytes 301064 | tf_op jit(solution)/shard_map/ppermute | solution.py:304
  11.4 7.0 %collective-permute-start.7 = (bf16[392,128]{1,0:T(8,128)(2,1)S(1)}, bf16[392,128]{1,0:T(8,128)(2,1)S(1)}, u32[]{:S(2)}, u32[]{:S(2)}) collective-permute-start(bf16[392,128]{1,0:T(8,128)(2,1)S(1)} %get-tuple-element.15), channel_id=1, source_target_pairs={{0,24},{8,16},{16,8},{24,0},{1,25},{9,17},{17,9},{25,1},{2,26},{10... | collective-permute-start | bytes 301064 | tf_op jit(solution)/shard_map/ppermute | solution.py:307
  13.9 6.5 %collective-permute-start.8 = (bf16[392,128]{1,0:T(8,128)(2,1)S(1)}, bf16[392,128]{1,0:T(8,128)(2,1)S(1)}, u32[]{:S(2)}, u32[]{:S(2)}) collective-permute-start(bf16[392,128]{1,0:T(8,128)(2,1)S(1)} %get-tuple-element.15), channel_id=1, source_target_pairs={{0,16},{8,24},{16,0},{24,8},{1,17},{9,25},{17,1},{25,9},{2,18},{10... | collective-permute-start | bytes 301064 | tf_op jit(solution)/shard_map/ppermute | solution.py:307
  14.4 6.0 %collective-permute-start.9 = (bf16[392,128]{1,0:T(8,128)(2,1)S(1)}, bf16[392,128]{1,0:T(8,128)(2,1)S(1)}, u32[]{:S(2)}, u32[]{:S(2)}) collective-permute-start(bf16[392,128]{1,0:T(8,128)(2,1)S(1)} %get-tuple-element.15), channel_id=1, source_target_pairs={{0,8},{8,0},{16,24},{24,16},{1,9},{9,1},{17,25},{25,17},{2,10},{10... | collective-permute-start | bytes 301064 | tf_op jit(solution)/shard_map/ppermute | solution.py:307
  15.3 7.1 %collective-permute-start.11 = (bf16[392,128]{1,0:T(8,128)(2,1)S(1)}, bf16[392,128]{1,0:T(8,128)(2,1)S(1)}, u32[]{:S(2)}, u32[]{:S(2)}) collective-permute-start(bf16[392,128]{1,0:T(8,128)(2,1)S(1)} %get-tuple-element.20), channel_id=1, source_target_pairs={{0,24},{8,16},{16,8},{24,0},{1,25},{9,17},{17,9},{25,1},{2,26},{10... | collective-permute-start | bytes 301064 | tf_op jit(solution)/shard_map/ppermute | solution.py:307
  17.8 4.9 %collective-permute-start.12 = (bf16[392,128]{1,0:T(8,128)(2,1)S(1)}, bf16[392,128]{1,0:T(8,128)(2,1)S(1)}, u32[]{:S(2)}, u32[]{:S(2)}) collective-permute-start(bf16[392,128]{1,0:T(8,128)(2,1)S(1)} %get-tuple-element.20), channel_id=1, source_target_pairs={{0,8},{8,0},{16,24},{24,16},{1,9},{9,1},{17,25},{25,17},{2,10},{10... | collective-permute-start | bytes 301064 | tf_op jit(solution)/shard_map/ppermute | solution.py:307
  18.4 5.1 %collective-permute-start.13 = (bf16[392,128]{1,0:T(8,128)(2,1)S(1)}, bf16[392,128]{1,0:T(8,128)(2,1)S(1)}, u32[]{:S(2)}, u32[]{:S(2)}) collective-permute-start(bf16[392,128]{1,0:T(8,128)(2,1)S(1)} %get-tuple-element.20), channel_id=1, source_target_pairs={{0,16},{8,24},{16,0},{24,8},{1,17},{9,25},{17,1},{25,9},{2,18},{10... | collective-permute-start | bytes 301064 | tf_op jit(solution)/shard_map/ppermute | solution.py:307
  20.4 3.6 %collective-permute-start.10 = (bf16[1192,128]{1,0:T(8,128)(2,1)S(1)}, bf16[1192,128]{1,0:T(8,128)(2,1)S(1)}, u32[]{:S(2)}, u32[]{:S(2)}) collective-permute-start(bf16[1192,128]{1,0:T(8,128)(2,1)S(1)} %shard_map.36.refs_4_), channel_id=1, source_target_pairs={{0,1},{1,0},{2,3},{3,2},{4,5},{5,4},{6,7},{7,6},{8,9},{9,8},{10,11... | collective-permute-start | bytes 915464 | tf_op jit(solution)/shard_map/ppermute | solution.py:304
  20.5 3.1 %collective-permute-start.5 = (bf16[1160,128]{1,0:T(8,128)(2,1)S(1)}, bf16[1160,128]{1,0:T(8,128)(2,1)S(1)}, u32[]{:S(2)}, u32[]{:S(2)}) collective-permute-start(bf16[1160,128]{1,0:T(8,128)(2,1)S(1)} %get-tuple-element.13.refs_0_), channel_id=1, source_target_pairs={{0,1},{1,0},{2,3},{3,2},{4,5},{5,4},{6,7},{7,6},{8,9},{9,8},{10,11... | collective-permute-start | bytes 890888 | tf_op jit(solution)/shard_map/ppermute | solution.py:304
  22.4 1.6 %collective-permute-start.6 = (bf16[1160,128]{1,0:T(8,128)(2,1)S(1)}, bf16[1160,128]{1,0:T(8,128)(2,1)S(1)}, u32[]{:S(2)}, u32[]{:S(2)}) collective-permute-start(bf16[1160,128]{1,0:T(8,128)(2,1)S(1)} %get-tuple-element.14.refs_1_.refs_4_), channel_id=1, source_target_pairs={{0,1},{1,0},{2,3},{3,2},{4,5},{5,4},{6,7},{7,6},{8,9},{9,8},{10,11... | collective-permute-start | bytes 890888 | tf_op jit(solution)/shard_map/ppermute | solution.py:304
  23.5 1.9 %collective-permute-start.14 = (bf16[1192,128]{1,0:T(8,128)(2,1)S(1)}, bf16[1192,128]{1,0:T(8,128)(2,1)S(1)}, u32[]{:S(2)}, u32[]{:S(2)}) collective-permute-start(bf16[1192,128]{1,0:T(8,128)(2,1)S(1)} %shard_map.38.refs_6_), channel_id=1, source_target_pairs={{0,1},{1,0},{2,3},{3,2},{4,5},{5,4},{6,7},{7,6},{8,9},{9,8},{10,11... | collective-permute-start | bytes 915464 | tf_op jit(solution)/shard_map/ppermute | solution.py:304

commit v9 on v7

--- a/solution.py
+++ b/solution.py
@@ -192,7 +192,7 @@
         place = end
     slots, hot = left_ref[rows:, :], hot_ref[...]
     norms = row_norms(left_ref.at[rows:])
-    for start, end in chunks(0, rows, 256):
+    for start, end in chunks(0, rows, 512):
         sums_ref[start:end, :] = dot(kern(left_ref[start:end, :], slots, norms), hot, NT)
     shares = jnp.zeros(hot.shape, jnp.float32)
     for start, end in chunks(rows, total, 256):

time: 27.4 us -> 27.4 us (level)
  no operation moved by 1% of the time
where the time goes in v9:
time: 27.4 us; the launch traced here: 27.3 us
  starting transfers between devices  15 us (55%)
  waiting for transfers between devices  6.36 us (23%)
  Pallas kernels  4.26 us (16%)
  local copies, waits for them, and re-layouts  1.55 us (6%)
    ppermute x6, starting transfers between devices, over_row(): lax.ppermute(values, 'row', [(i, i ^ bits) for i in range(row_count)])  7.69 us
    ppermute x9, starting transfers between devices, over_col(): lax.ppermute(values, 'col', [(i, i ^ bits) for i in range(group_count)])  7.33 us
    pallas_call x12, Pallas kernels, call(): pl.pallas_call(body, out_shape=out_shape, in_specs=[VMEM] * count + [pl.B...  4.26 us
    ppermute x6, waiting for transfers between devices, over_row(): lax.ppermute(values, 'row', [(i, i ^ bits) for i in range(row_count)])  3.32 us
    ppermute x9, waiting for transfers between devices, over_col(): lax.ppermute(values, 'col', [(i, i ^ bits) for i in range(group_count)])  3.04 us
    unnamed x4, local copies, waits for them, and re-layouts  1.55 us
  transfers between devices with their start and end apart: 15, of which 6 were waited for; matrix products, arithmetic and copies ran while one was open for 0% of the time, Pallas kernels for 9%

profile of v9, /device:TPU:0, one launch (start us, length us, event | category | flops | bytes accessed | tf_op | source)
XLA Modules:
  0.0 27.3 jit_solution(9960025196673036508)
XLA Ops:
  0.0 4.0 %collective-permute-start.2 = (bf16[64,768]{1,0:T(8,128)(2,1)}, bf16[64,768]{1,0:T(8,128)(2,1)S(1)}, u32[]{:S(2)}, u32[]{:S(2)}) collective-permute-start(bf16[64,768]{1,0:T(8,128)(2,1)} %refs_0_.1), channel_id=1, source_target_pairs={{0,4},{1,5},{2,6},{3,7},{4,0},{5,1},{6,2},{7,3},{8,12},{9,13},{10,... | collective-permute-start | bytes 294920 | tf_op jit(solution)/shard_map/ppermute | solution.py:304
  4.0 1.6 %collective-permute-start = (bf16[64,768]{1,0:T(8,128)(2,1)}, bf16[64,768]{1,0:T(8,128)(2,1)S(1)}, u32[]{:S(2)}, u32[]{:S(2)}) collective-permute-start(bf16[64,768]{1,0:T(8,128)(2,1)} %refs_0_.1), channel_id=1, source_target_pairs={{0,2},{1,3},{2,0},{3,1},{4,6},{5,7},{6,4},{7,5},{8,10},{9,11},{10,... | collective-permute-start | bytes 294920 | tf_op jit(solution)/shard_map/ppermute | solution.py:304
  5.6 0.3 %collective-permute-start.3 = (s32[1,64]{1,0:T(1,128)}, s32[1,64]{1,0:T(1,128)S(1)}, u32[]{:S(2)}, u32[]{:S(2)}) collective-permute-start(s32[1,64]{1,0:T(1,128)} %bitcast.1), channel_id=1, source_target_pairs={{0,4},{1,5},{2,6},{3,7},{4,0},{5,1},{6,2},{7,3},{8,12},{9,13},{10,... | collective-permute-start | bytes 776 | tf_op jit(solution)/shard_map/ppermute | solution.py:304
  6.0 0.1 collective-permute-start.1
  6.1 0.0 copy-start
  6.1 0.9 %copy-done = bf16[64,768]{1,0:T(8,128)(2,1)S(1)} copy-done((bf16[64,768]{1,0:T(8,128)(2,1)S(1)}, bf16[64,768]{1,0:T(8,128)(2,1)}, u32[]{:S(2)}) %copy-start) | copy-done | bytes 98328
  7.0 0.0 copy-start.1
  7.0 0.7 %copy-done.1 = s32[64]{0:T(128)S(1)} copy-done((s32[64]{0:T(128)S(1)}, s32[64]{0:T(128)}, u32[]{:S(2)}) %copy-start.1) | copy-done | bytes 280
  7.6 0.1 shard_map.28.refs_0_
  7.7 1.3 %collective-permute-done.2.refs_0_ = bf16[64,768]{1,0:T(8,128)(2,1)S(1)} collective-permute-done((bf16[64,768]{1,0:T(8,128)(2,1)}, bf16[64,768]{1,0:T(8,128)(2,1)S(1)}, u32[]{:S(2)}, u32[]{:S(2)}) %collective-permute-start.2) | collective-permute-done | bytes 98336 | tf_op jit(solution)/shard_map/ppermute | solution.py:304
  9.1 1.1 %collective-permute-done.3.refs_1_ = s32[1,64]{1,0:T(1,128)S(1)} collective-permute-done((s32[1,64]{1,0:T(1,128)}, s32[1,64]{1,0:T(1,128)S(1)}, u32[]{:S(2)}, u32[]{:S(2)}) %collective-permute-start.3) | collective-permute-done | bytes 288 | tf_op jit(solution)/shard_map/ppermute | solution.py:304
  10.2 0.1 shard_map.32.refs_2_.refs_0_
  10.3 0.6 %collective-permute-start.4 = (bf16[392,128]{1,0:T(8,128)(2,1)S(1)}, bf16[392,128]{1,0:T(8,128)(2,1)S(1)}, u32[]{:S(2)}, u32[]{:S(2)}) collective-permute-start(bf16[392,128]{1,0:T(8,128)(2,1)S(1)} %shard_map.32.refs_2_.refs_0_), channel_id=1, source_target_pairs={{0,2},{1,3},{2,0},{3,1},{4,6},{5,7},{6,4},{7,5},{8,10},{9,11},{10,... | collective-permute-start | bytes 301064 | tf_op jit(solution)/shard_map/ppermute | solution.py:304
  10.9 0.0 collective-permute-done.refs_0_
  10.9 0.0 collective-permute-done.1.refs_1_
  10.9 0.1 shard_map.30.refs_1_
  11.0 0.4 %shard_map.33 = (bf16[1160,128]{1,0:T(8,128)(2,1)S(1)}, bf16[392,128]{1,0:T(8,128)(2,1)S(1)}) custom-call(bf16[392,128]{1,0:T(8,128)(2,1)S(1)} %shard_map.28.refs_0_, bf16[392,128]{1,0:T(8,128)(2,1)S(1)} %shard_map.30.refs_1_, bf16[392,128]{1,0:T(8,128)(2,1)S(1)} %shard_map.32.refs_2_.refs_0_), custom_call_target="tpu_custom_call" | custom-call | tf_op jit(solution)/shard_map/pallas_call | solution.py:33
  11.4 2.5 %collective-permute-start.7 = (bf16[392,128]{1,0:T(8,128)(2,1)S(1)}, bf16[392,128]{1,0:T(8,128)(2,1)S(1)}, u32[]{:S(2)}, u32[]{:S(2)}) collective-permute-start(bf16[392,128]{1,0:T(8,128)(2,1)S(1)} %get-tuple-element.15), channel_id=1, source_target_pairs={{0,24},{8,16},{16,8},{24,0},{1,25},{9,17},{17,9},{25,1},{2,26},{10... | collective-permute-start | bytes 301064 | tf_op jit(solution)/shard_map/ppermute | solution.py:307
  13.9 0.5 %collective-permute-start.8 = (bf16[392,128]{1,0:T(8,128)(2,1)S(1)}, bf16[392,128]{1,0:T(8,128)(2,1)S(1)}, u32[]{:S(2)}, u32[]{:S(2)}) collective-permute-start(bf16[392,128]{1,0:T(8,128)(2,1)S(1)} %get-tuple-element.15), channel_id=1, source_target_pairs={{0,16},{8,24},{16,0},{24,8},{1,17},{9,25},{17,1},{25,9},{2,18},{10... | collective-permute-start | bytes 301064 | tf_op jit(solution)/shard_map/ppermute | solution.py:307
  14.4 0.6 %collective-permute-start.9 = (bf16[392,128]{1,0:T(8,128)(2,1)S(1)}, bf16[392,128]{1,0:T(8,128)(2,1)S(1)}, u32[]{:S(2)}, u32[]{:S(2)}) collective-permute-start(bf16[392,128]{1,0:T(8,128)(2,1)S(1)} %get-tuple-element.15), channel_id=1, source_target_pairs={{0,8},{8,0},{16,24},{24,16},{1,9},{9,1},{17,25},{25,17},{2,10},{10... | collective-permute-start | bytes 301064 | tf_op jit(solution)/shard_map/ppermute | solution.py:307
  14.9 0.0 collective-permute-done.4.refs_0_
  15.0 0.4 %shard_map.35 = (bf16[1160,128]{1,0:T(8,128)(2,1)S(1)}, bf16[392,128]{1,0:T(8,128)(2,1)S(1)}) custom-call(bf16[392,128]{1,0:T(8,128)(2,1)S(1)} %shard_map.32.refs_2_.refs_0_, bf16[392,128]{1,0:T(8,128)(2,1)S(1)} %shard_map.34.refs_1_), custom_call_target="tpu_custom_call" | custom-call | tf_op jit(solution)/shard_map/pallas_call | solution.py:33
  15.3 2.5 %collective-permute-start.11 = (bf16[392,128]{1,0:T(8,128)(2,1)S(1)}, bf16[392,128]{1,0:T(8,128)(2,1)S(1)}, u32[]{:S(2)}, u32[]{:S(2)}) collective-permute-start(bf16[392,128]{1,0:T(8,128)(2,1)S(1)} %get-tuple-element.20), channel_id=1, source_target_pairs={{0,24},{8,16},{16,8},{24,0},{1,25},{9,17},{17,9},{25,1},{2,26},{10... | collective-permute-start | bytes 301064 | tf_op jit(solution)/shard_map/ppermute | solution.py:307
  17.8 0.5 %collective-permute-start.12 = (bf16[392,128]{1,0:T(8,128)(2,1)S(1)}, bf16[392,128]{1,0:T(8,128)(2,1)S(1)}, u32[]{:S(2)}, u32[]{:S(2)}) collective-permute-start(bf16[392,128]{1,0:T(8,128)(2,1)S(1)} %get-tuple-element.20), channel_id=1, source_target_pairs={{0,16},{8,24},{16,0},{24,8},{1,17},{9,25},{17,1},{25,9},{2,18},{10... | collective-permute-start | bytes 301064 | tf_op jit(solution)/shard_map/ppermute | solution.py:307
  18.3 0.0 collective-permute-done.7.refs_0_
  18.3 1.1 %collective-permute-start.13 = (bf16[392,128]{1,0:T(8,128)(2,1)S(1)}, bf16[392,128]{1,0:T(8,128)(2,1)S(1)}, u32[]{:S(2)}, u32[]{:S(2)}) collective-permute-start(bf16[392,128]{1,0:T(8,128)(2,1)S(1)} %get-tuple-element.20), channel_id=1, source_target_pairs={{0,8},{8,0},{16,24},{24,16},{1,9},{9,1},{17,25},{25,17},{2,10},{10... | collective-permute-start | bytes 301064 | tf_op jit(solution)/shard_map/ppermute | solution.py:307
  19.5 1.0 %collective-permute-done.8.refs_1_ = bf16[392,128]{1,0:T(8,128)(2,1)S(1)} collective-permute-done((bf16[392,128]{1,0:T(8,128)(2,1)S(1)}, bf16[392,128]{1,0:T(8,128)(2,1)S(1)}, u32[]{:S(2)}, u32[]{:S(2)}) %collective-permute-start.8) | collective-permute-done | bytes 100384 | tf_op jit(solution)/shard_map/ppermute | solution.py:307
  20.4 0.0 collective-permute-done.9.refs_2_
  20.5 0.1 collective-permute-start.10
  20.5 0.5 %collective-permute-start.5 = (bf16[1160,128]{1,0:T(8,128)(2,1)S(1)}, bf16[1160,128]{1,0:T(8,128)(2,1)S(1)}, u32[]{:S(2)}, u32[]{:S(2)}) collective-permute-start(bf16[1160,128]{1,0:T(8,128)(2,1)S(1)} %get-tuple-element.13.refs_0_), channel_id=1, source_target_pairs={{0,1},{1,0},{2,3},{3,2},{4,5},{5,4},{6,7},{7,6},{8,9},{9,8},{10,11... | collective-permute-start | bytes 890888 | tf_op jit(solution)/shard_map/ppermute | solution.py:304
  21.0 1.4 %collective-permute-done.11.refs_0_ = bf16[392,128]{1,0:T(8,128)(2,1)S(1)} collective-permute-done((bf16[392,128]{1,0:T(8,128)(2,1)S(1)}, bf16[392,128]{1,0:T(8,128)(2,1)S(1)}, u32[]{:S(2)}, u32[]{:S(2)}) %collective-permute-start.11) | collective-permute-done | bytes 100384 | tf_op jit(solution)/shard_map/ppermute | solution.py:307
  22.5 0.0 collective-permute-start.6
  22.5 0.9 %collective-permute-done.12.refs_1_ = bf16[392,128]{1,0:T(8,128)(2,1)S(1)} collective-permute-done((bf16[392,128]{1,0:T(8,128)(2,1)S(1)}, bf16[392,128]{1,0:T(8,128)(2,1)S(1)}, u32[]{:S(2)}, u32[]{:S(2)}) %collective-permute-start.12) | collective-permute-done | bytes 100384 | tf_op jit(solution)/shard_map/ppermute | solution.py:307
  23.4 0.0 collective-permute-done.13.refs_2_
  23.4 0.1 collective-permute-start.14
  23.5 0.0 collective-permute-done.5.refs_2_
  23.5 0.6 %collective-permute-done.6.refs_3_.refs_5_ = bf16[1160,128]{1,0:T(8,128)(2,1)S(1)} collective-permute-done((bf16[1160,128]{1,0:T(8,128)(2,1)S(1)}, bf16[1160,128]{1,0:T(8,128)(2,1)S(1)}, u32[]{:S(2)}, u32[]{:S(2)}) %collective-permute-start.6) | collective-permute-done | bytes 296992 | tf_op jit(solution)/shard_map/ppermute | solution.py:304
  24.1 0.0 collective-permute-done.10.refs_5_
  24.1 1.3 %shard_map.37 = (bf16[768,768]{1,0:T(8,128)(2,1)S(1)}, bf16[128,256]{1,0:T(8,128)(2,1)S(1)}, f32[512,128]{1,0:T(8,128)S(1)}, f32[16,128]{1,0:T(8,128)S(1)}) custom-call(bf16[1160,128]{1,0:T(8,128)(2,1)S(1)} %get-tuple-element.13.refs_0_, bf16[1160,128]{1,0:T(8,128)(2,1)S(1)} %get-tuple-element.14.refs_1_.refs_4_, ...), custom_call_target="tpu_custom_call" | custom-call | flops 352321536 | bytes 1179648 | tf_op jit(solution)/shard_map/pallas_call | solution.py:33
  25.4 0.0 collective-permute-done.14.refs_7_
  25.4 1.9 %shard_map.39 = f32[512,128]{1,0:T(8,128)} custom-call(bf16[768,768]{1,0:T(8,128)(2,1)S(1)} %get-tuple-element.16.refs_0_, bf16[128,256]{1,0:T(8,128)(2,1)S(1)} %get-tuple-element.17.refs_1_, f32[512,128]{1,0:T(8,128)S(1)} %get-tuple-element.18.refs_2_, f32[16,128]{1,0:T(8,128)S(1)} %get-tuple-element.19.refs_3_, ...), custom_call_target="tpu_custom_call" | custom-call | flops 469762048 | bytes 1572864 | tf_op jit(solution)/shard_map/pallas_call | solution.py:33
  (5 shorter events, 0.1 us)
Async XLA Ops:
  0.0 9.0 %collective-permute-start.2 = (bf16[64,768]{1,0:T(8,128)(2,1)}, bf16[64,768]{1,0:T(8,128)(2,1)S(1)}, u32[]{:S(2)}, u32[]{:S(2)}) collective-permute-start(bf16[64,768]{1,0:T(8,128)(2,1)} %refs_0_.1), channel_id=1, source_target_pairs={{0,4},{1,5},{2,6},{3,7},{4,0},{5,1},{6,2},{7,3},{8,12},{9,13},{10,... | collective-permute-start | bytes 294920 | tf_op jit(solution)/shard_map/ppermute | solution.py:304
  4.0 6.9 %collective-permute-start = (bf16[64,768]{1,0:T(8,128)(2,1)}, bf16[64,768]{1,0:T(8,128)(2,1)S(1)}, u32[]{:S(2)}, u32[]{:S(2)}) collective-permute-start(bf16[64,768]{1,0:T(8,128)(2,1)} %refs_0_.1), channel_id=1, source_target_pairs={{0,2},{1,3},{2,0},{3,1},{4,6},{5,7},{6,4},{7,5},{8,10},{9,11},{10,... | collective-permute-start | bytes 294920 | tf_op jit(solution)/shard_map/ppermute | solution.py:304
  5.6 4.6 %collective-permute-start.3 = (s32[1,64]{1,0:T(1,128)}, s32[1,64]{1,0:T(1,128)S(1)}, u32[]{:S(2)}, u32[]{:S(2)}) collective-permute-start(s32[1,64]{1,0:T(1,128)} %bitcast.1), channel_id=1, source_target_pairs={{0,4},{1,5},{2,6},{3,7},{4,0},{5,1},{6,2},{7,3},{8,12},{9,13},{10,... | collective-permute-start | bytes 776 | tf_op jit(solution)/shard_map/ppermute | solution.py:304
  6.0 5.0 %collective-permute-start.1 = (s32[1,64]{1,0:T(1,128)}, s32[1,64]{1,0:T(1,128)S(1)}, u32[]{:S(2)}, u32[]{:S(2)}) collective-permute-start(s32[1,64]{1,0:T(1,128)} %bitcast.2), channel_id=1, source_target_pairs={{0,2},{1,3},{2,0},{3,1},{4,6},{5,7},{6,4},{7,5},{8,10},{9,11},{10,... | collective-permute-start | bytes 776 | tf_op jit(solution)/shard_map/ppermute | solution.py:304
  6.1 0.9 %copy-start = (bf16[64,768]{1,0:T(8,128)(2,1)S(1)}, bf16[64,768]{1,0:T(8,128)(2,1)}, u32[]{:S(2)}) copy-start(bf16[64,768]{1,0:T(8,128)(2,1)} %refs_0_.1) | copy-start | bytes 294916
  7.0 0.7 %copy-start.1 = (s32[64]{0:T(128)S(1)}, s32[64]{0:T(128)}, u32[]{:S(2)}) copy-start(s32[64]{0:T(128)} %param.3) | copy-start | bytes 772
  10.3 4.7 %collective-permute-start.4 = (bf16[392,128]{1,0:T(8,128)(2,1)S(1)}, bf16[392,128]{1,0:T(8,128)(2,1)S(1)}, u32[]{:S(2)}, u32[]{:S(2)}) collective-permute-start(bf16[392,128]{1,0:T(8,128)(2,1)S(1)} %shard_map.32.refs_2_.refs_0_), channel_id=1, source_target_pairs={{0,2},{1,3},{2,0},{3,1},{4,6},{5,7},{6,4},{7,5},{8,10},{9,11},{10,... | collective-permute-start | bytes 301064 | tf_op jit(solution)/shard_map/ppermute | solution.py:304
  11.4 6.9 %collective-permute-start.7 = (bf16[392,128]{1,0:T(8,128)(2,1)S(1)}, bf16[392,128]{1,0:T(8,128)(2,1)S(1)}, u32[]{:S(2)}, u32[]{:S(2)}) collective-permute-start(bf16[392,128]{1,0:T(8,128)(2,1)S(1)} %get-tuple-element.15), channel_id=1, source_target_pairs={{0,24},{8,16},{16,8},{24,0},{1,25},{9,17},{17,9},{25,1},{2,26},{10... | collective-permute-start | bytes 301064 | tf_op jit(solution)/shard_map/ppermute | solution.py:307
  13.9 6.6 %collective-permute-start.8 = (bf16[392,128]{1,0:T(8,128)(2,1)S(1)}, bf16[392,128]{1,0:T(8,128)(2,1)S(1)}, u32[]{:S(2)}, u32[]{:S(2)}) collective-permute-start(bf16[392,128]{1,0:T(8,128)(2,1)S(1)} %get-tuple-element.15), channel_id=1, source_target_pairs={{0,16},{8,24},{16,0},{24,8},{1,17},{9,25},{17,1},{25,9},{2,18},{10... | collective-permute-start | bytes 301064 | tf_op jit(solution)/shard_map/ppermute | solution.py:307
  14.4 6.1 %collective-permute-start.9 = (bf16[392,128]{1,0:T(8,128)(2,1)S(1)}, bf16[392,128]{1,0:T(8,128)(2,1)S(1)}, u32[]{:S(2)}, u32[]{:S(2)}) collective-permute-start(bf16[392,128]{1,0:T(8,128)(2,1)S(1)} %get-tuple-element.15), channel_id=1, source_target_pairs={{0,8},{8,0},{16,24},{24,16},{1,9},{9,1},{17,25},{25,17},{2,10},{10... | collective-permute-start | bytes 301064 | tf_op jit(solution)/shard_map/ppermute | solution.py:307
  15.3 7.1 %collective-permute-start.11 = (bf16[392,128]{1,0:T(8,128)(2,1)S(1)}, bf16[392,128]{1,0:T(8,128)(2,1)S(1)}, u32[]{:S(2)}, u32[]{:S(2)}) collective-permute-start(bf16[392,128]{1,0:T(8,128)(2,1)S(1)} %get-tuple-element.20), channel_id=1, source_target_pairs={{0,24},{8,16},{16,8},{24,0},{1,25},{9,17},{17,9},{25,1},{2,26},{10... | collective-permute-start | bytes 301064 | tf_op jit(solution)/shard_map/ppermute | solution.py:307
  17.8 5.6 %collective-permute-start.12 = (bf16[392,128]{1,0:T(8,128)(2,1)S(1)}, bf16[392,128]{1,0:T(8,128)(2,1)S(1)}, u32[]{:S(2)}, u32[]{:S(2)}) collective-permute-start(bf16[392,128]{1,0:T(8,128)(2,1)S(1)} %get-tuple-element.20), channel_id=1, source_target_pairs={{0,16},{8,24},{16,0},{24,8},{1,17},{9,25},{17,1},{25,9},{2,18},{10... | collective-permute-start | bytes 301064 | tf_op jit(solution)/shard_map/ppermute | solution.py:307
  18.3 5.1 %collective-permute-start.13 = (bf16[392,128]{1,0:T(8,128)(2,1)S(1)}, bf16[392,128]{1,0:T(8,128)(2,1)S(1)}, u32[]{:S(2)}, u32[]{:S(2)}) collective-permute-start(bf16[392,128]{1,0:T(8,128)(2,1)S(1)} %get-tuple-element.20), channel_id=1, source_target_pairs={{0,8},{8,0},{16,24},{24,16},{1,9},{9,1},{17,25},{25,17},{2,10},{10... | collective-permute-start | bytes 301064 | tf_op jit(solution)/shard_map/ppermute | solution.py:307
  20.5 3.6 %collective-permute-start.10 = (bf16[1192,128]{1,0:T(8,128)(2,1)S(1)}, bf16[1192,128]{1,0:T(8,128)(2,1)S(1)}, u32[]{:S(2)}, u32[]{:S(2)}) collective-permute-start(bf16[1192,128]{1,0:T(8,128)(2,1)S(1)} %shard_map.36.refs_4_), channel_id=1, source_target_pairs={{0,1},{1,0},{2,3},{3,2},{4,5},{5,4},{6,7},{7,6},{8,9},{9,8},{10,11... | collective-permute-start | bytes 915464 | tf_op jit(solution)/shard_map/ppermute | solution.py:304
  20.5 3.0 %collective-permute-start.5 = (bf16[1160,128]{1,0:T(8,128)(2,1)S(1)}, bf16[1160,128]{1,0:T(8,128)(2,1)S(1)}, u32[]{:S(2)}, u32[]{:S(2)}) collective-permute-start(bf16[1160,128]{1,0:T(8,128)(2,1)S(1)} %get-tuple-element.13.refs_0_), channel_id=1, source_target_pairs={{0,1},{1,0},{2,3},{3,2},{4,5},{5,4},{6,7},{7,6},{8,9},{9,8},{10,11... | collective-permute-start | bytes 890888 | tf_op jit(solution)/shard_map/ppermute | solution.py:304
  22.5 1.6 %collective-permute-start.6 = (bf16[1160,128]{1,0:T(8,128)(2,1)S(1)}, bf16[1160,128]{1,0:T(8,128)(2,1)S(1)}, u32[]{:S(2)}, u32[]{:S(2)}) collective-permute-start(bf16[1160,128]{1,0:T(8,128)(2,1)S(1)} %get-tuple-element.14.refs_1_.refs_4_), channel_id=1, source_target_pairs={{0,1},{1,0},{2,3},{3,2},{4,5},{5,4},{6,7},{7,6},{8,9},{9,8},{10,11... | collective-permute-start | bytes 890888 | tf_op jit(solution)/shard_map/ppermute | solution.py:304
  23.4 2.0 %collective-permute-start.14 = (bf16[1192,128]{1,0:T(8,128)(2,1)S(1)}, bf16[1192,128]{1,0:T(8,128)(2,1)S(1)}, u32[]{:S(2)}, u32[]{:S(2)}) collective-permute-start(bf16[1192,128]{1,0:T(8,128)(2,1)S(1)} %shard_map.38.refs_6_), channel_id=1, source_target_pairs={{0,1},{1,0},{2,3},{3,2},{4,5},{5,4},{6,7},{7,6},{8,9},{9,8},{10,11... | collective-permute-start | bytes 915464 | tf_op jit(solution)/shard_map/ppermute | solution.py:304
